TPU v7x, 32 devices: a whole 2x2x4 slice. The times are simulated.
32 devices in a mesh: lon: 8 (over z, y), trc: 4 (over x, core).
Axes of the slice: x: 2, y: 2, z: 4, core: 2. Of those that a mesh axis runs over, the one named last changes fastest.
Arguments:
- state_adjoint: float32 [8, 4, 24, 34, 256], P('trc', None, 'lon'), may hold values from -6 to 6
- switches: int32 [8, 2, 24, 34, 256], P('trc', None, 'lon'), may hold values from 0 to 2
- flags: int32 [2, 24, 34, 256], P(None, 'lon'), may hold values 0 or 1
- air_mass: float32 [24, 34, 256], P('lon', None, 'trc'), may hold values from 1 to 4
- x_flux: float32 [24, 34, 256], P('lon', None, 'trc'), may hold values from 0.02 to 0.45
- y_flux: float32 [24, 34, 256], P('lon', None, 'trc'), may hold values from 0.02 to 0.45
- vertical_mixing: float32 [24, 33, 256], P('lon', None, 'trc'), may hold values from 0.1 to 10
Outputs:
- prior_adjoint: float32 [8, 4, 24, 34, 256], P('trc', None, 'lon')
All inputs are finite; a program needn't handle non-finite values. No bound on the sum of `flags` on one device may be relied on, other than what follows from the above.
Results may differ from a plain program's by a relative error of at most 0.0003.
Values sent between devices are 32-bit elements; how exact they have to be, the bound alone decides.
No kernel may reach another device: no remote copies, remote signals or barrier semaphores. Data moves between devices by JAX's collectives and lax.ppermute only.
A program may use at most 128 MiB of HBM per device.

v0:
```python
import jax
import jax.numpy as jnp
from jax import lax
from jax.experimental import pallas as pl
from jax.experimental.pallas import tpu as pltpu
from jax.sharding import PartitionSpec as P

LANES = 128
MOMENTS = 4
VMEM = pl.BlockSpec(memory_space=pltpu.VMEM)


def state_view(x):
    t, m, c, l, n = x.shape
    b = n // LANES
    x = x.reshape(t, m, c, l, b, LANES).transpose(0, 2, 3, 4, 1, 5)
    return x.reshape(t, c, l, b * m, LANES)


def pair_view(x):
    t, d, c, l, n = x.shape
    b = n // LANES
    x = x.reshape(t, d, c, l, b, LANES).transpose(0, 2, 3, 4, 1, 5)
    return x.reshape(t, c, l // 2, 2 * b * d, LANES)


def state_back(y):
    t, c, l, rows, _ = y.shape
    b = rows // MOMENTS
    y = y.reshape(t, c, l, b, MOMENTS, LANES).transpose(0, 4, 1, 2, 3, 5)
    return y.reshape(t, MOMENTS, c, l, b * LANES)


def shifted(value, axis, by):
    count = lax.axis_size(axis)
    return lax.ppermute(value, axis, [(i, (i + by) % count) for i in range(count)])


def swapped(value, axis, mask):
    count = lax.axis_size(axis)
    return lax.ppermute(value, axis, [(i, i ^ mask) for i in range(count)])


def call(kernel, out, scratch, flops, moved, *args):
    return pl.pallas_call(
        kernel,
        out_shape=out,
        in_specs=[VMEM] * len(args),
        out_specs=jax.tree.map(lambda _: VMEM, out),
        scratch_shapes=scratch,
        compiler_params=pltpu.CompilerParams(vmem_limit_bytes=24 * 1024 * 1024),
        cost_estimate=pl.CostEstimate(flops=flops, bytes_accessed=moved, transcendentals=0),
    )(*args)


def f32(*shape):
    return jax.ShapeDtypeStruct(shape, jnp.float32)


def tile_masks(slope):
    row = lax.broadcasted_iota(jnp.int32, (8, LANES), 0) % MOMENTS
    return row == 0, row == slope


def pack_kernel(mass, xf, yf, km, flags, packed, face):
    half = LANES // 2
    levels = mass.shape[1]
    packed[0, :, :, :half] = mass[...]
    packed[0, :, :, half:] = xf[...]
    packed[1, :, :, :half] = yf[...]
    packed[1, :, : levels - 1, half:] = km[...]
    packed[1, :, levels - 1 :, half:] = jnp.zeros((mass.shape[0], 1, half), jnp.float32)
    face[:, :half] = xf[0, : levels // 2]
    face[:, half:] = xf[0, levels // 2 :]


def pre_kernel(own, first, second, third, face0, face1, face2, face3, flags, edge, switches, order,
               rates, factors, turn, fields, faces):
    columns, levels = own.shape[1], own.shape[2]
    half = LANES // 2
    odd = order[0] % 2 == 1
    high = order[0] >= 2
    lane = lax.broadcasted_iota(jnp.int32, (8, LANES), 1)
    row = lax.broadcasted_iota(jnp.int32, (8, LANES), 0)
    upper_block = row >= MOMENTS
    lane_low = lax.broadcasted_iota(jnp.int32, (levels, LANES), 1) < half

    def sorted_shards(a, b, c, d):
        a, b, c, d = (jnp.where(odd, b, a), jnp.where(odd, a, b), jnp.where(odd, d, c), jnp.where(odd, c, d))
        return (jnp.where(high, c, a), jnp.where(high, d, b), jnp.where(high, a, c), jnp.where(high, b, d))

    for pair in range(2):
        for c in range(columns):
            shards = sorted_shards(own[pair, c], first[pair, c], second[pair, c], third[pair, c])
            for b in range(2):
                lo, hi = shards[2 * b], shards[2 * b + 1]
                lo_r, hi_r = pltpu.roll(lo, half, 1), pltpu.roll(hi, half, 1)
                fields[2 * pair, c, b] = jnp.where(lane_low, lo, hi_r)
                fields[2 * pair + 1, c, b] = jnp.where(lane_low, lo_r, hi)
    shards = sorted_shards(face0[...], face1[...], face2[...], face3[...])
    short = lane_low[: levels // 2]
    for b in range(2):
        lo, hi = shards[2 * b], shards[2 * b + 1]
        faces[0, b] = jnp.where(short, lo, pltpu.roll(hi, half, 1))
        faces[1, b] = jnp.where(short, pltpu.roll(lo, half, 1), hi)

    def spread(ref, *where):
        blocks = [jnp.broadcast_to(ref[(*index, pl.ds(r, 1), slice(None))], (8, LANES)) for index, r in where]
        return jnp.where(upper_block, blocks[1], blocks[0])

    def field(f, c, l):
        return spread(fields, ((f, c, 0), l), ((f, c, 1), l))

    def flag(ref, c, l, d):
        base = (l % 2) * 4 + d
        return spread(ref, ((c, l // 2), base), ((c, l // 2), base + 2)).astype(jnp.float32)

    first_row = (lane == 0) & (row < MOMENTS)
    last_row = (lane == LANES - 1) & (row >= MOMENTS)
    for l in range(levels):
        flux_x = [field(1, c, l) for c in range(columns)]
        flag_x = [flag(flags, c, l, 0) for c in range(columns)]
        fl = l % (levels // 2)
        fh = l // (levels // 2)
        flux_x.append(spread(faces, ((fh, 0), fl), ((fh, 1), fl)))
        base = (l % 2) * 4
        flag_x.append(spread(edge, ((l // 2,), base), ((l // 2,), base + 2)).astype(jnp.float32))
        for c in range(columns):
            share = 1.0 / field(0, c, l)
            rates[0, c, l] = flag_x[c + 1] * flux_x[c + 1] * share
            rates[1, c, l] = (1.0 - flag_x[c]) * flux_x[c] * share
            flux_y = field(2, c, l)
            flag_y = flag(flags, c, l, 1)
            north = flag_y * flux_y
            south = pltpu.roll(flux_y - north, 1, 1)
            south = jnp.where(lane == 0, pltpu.roll(south, 4, 0), south)
            rates[2, c, l] = jnp.where(last_row, 0.0, north) * share
            rates[3, c, l] = jnp.where(first_row, 0.0, south) * share

    fixed = row % MOMENTS == 3
    for c in range(columns):
        below = None
        upper = None
        for l in range(levels):
            diagonal = jnp.ones((8, LANES), jnp.float32)
            if l > 0:
                diagonal = diagonal + below
            if l < levels - 1:
                above = field(3, c, l)
                diagonal = diagonal + above
            if l > 0:
                diagonal = diagonal + below * upper
            inverse = 1.0 / diagonal
            factors[0, c, l] = jnp.where(fixed, 1.0, inverse)
            factors[2, c, l] = jnp.where(fixed, 0.0, below * inverse) if l > 0 else jnp.zeros((8, LANES), jnp.float32)
            if l < levels - 1:
                upper = -above * inverse
                factors[1, c, l] = jnp.where(fixed, 0.0, upper)
                below = above
            else:
                factors[1, c, l] = jnp.zeros((8, LANES), jnp.float32)

    for t in range(switches.shape[0]):
        for c in range(columns):
            for l in range(levels):
                for d in range(2):
                    base = (l % 2) * 4 + d
                    sw = spread(switches, ((t, c, l // 2), base), ((t, c, l // 2), base + 2))
                    take = jnp.where(sw == 1, 1.0, jnp.where(sw == 2, -1.0, 0.0))
                    keep = jnp.where(sw == 0, 1.0, 0.0)
                    m = row % MOMENTS
                    turn[d, t, c, l] = jnp.where(m == 0, take, jnp.where(m == 1 + d, keep, 1.0))


def advect(own, east_side, west_side, east, west, turns, slope, masks):
    is_mass, is_slope = masks
    stay = 1.0 - (east + west)
    east_part = east * jnp.where(is_slope, east, 1.0)
    west_part = west * jnp.where(is_slope, west, 1.0)
    east_cross = east * (1.0 - east)
    west_cross = west * (1.0 - west)
    out = []
    for s, e, w, z in zip(own, east_side, west_side, turns):
        total = stay * s + east_part * e + west_part * w
        cross = east_cross * (e - s) - west_cross * (w - s)
        total = total + jnp.where(is_slope, pltpu.roll(cross, slope, 0), 0.0)
        slope_up = pltpu.roll(total, 8 - slope, 0)
        out.append(z * jnp.where(is_mass, slope_up, total) + jnp.where(is_mass, total, 0.0))
    return out


def mid_kernel(state, west_halo, east_halo, rates, factors, turn, out0, out1, out2):
    tracers, columns, levels = state.shape[0], state.shape[1], state.shape[2]
    outs = (out0, out1, out2)
    lane = lax.broadcasted_iota(jnp.int32, (8, LANES), 1)
    at_first, at_last = lane == 0, lane == LANES - 1
    x_masks, y_masks = tile_masks(1), tile_masks(2)

    def prev(v):
        r = pltpu.roll(v, 1, 1)
        return jnp.where(at_first, pltpu.roll(r, 4, 0), r)

    def following(v):
        r = pltpu.roll(v, LANES - 1, 1)
        return jnp.where(at_last, pltpu.roll(r, 4, 0), r)

    def y_step(values, c, l):
        return advect(values, [following(v) for v in values], [prev(v) for v in values],
                      rates[2, c, l], rates[3, c, l], [turn[1, t, c, l] for t in range(tracers)], 2, y_masks)

    carried = [[None] * tracers for _ in range(columns)]
    for l in range(levels):
        line = [[west_halo[t, l] for t in range(tracers)]]
        line += [[state[t, c, l] for t in range(tracers)] for c in range(columns)]
        line += [[east_halo[t, l] for t in range(tracers)]]
        for c in range(columns):
            values = advect(line[c + 1], line[c + 2], line[c], rates[0, c, l], rates[1, c, l],
                            [turn[0, t, c, l] for t in range(tracers)], 1, x_masks)
            values = y_step(values, c, l)
            for t in range(tracers):
                v = values[t] * factors[0, c, l]
                if l > 0:
                    v = v + factors[2, c, l] * carried[c][t]
                carried[c][t] = v
                outs[c][t, l] = v
    for l in range(levels - 1, -1, -1):
        for c in range(columns):
            if l < levels - 1:
                for t in range(tracers):
                    carried[c][t] = outs[c][t, l] - factors[1, c, l] * carried[c][t]
            values = y_step(carried[c], c, l)
            for t in range(tracers):
                outs[c][t, l] = values[t]


def post_kernel(col0, col1, col2, west_halo, east_halo, rates, turn, out):
    tracers, columns, levels = out.shape[0], out.shape[1], out.shape[2]
    line_refs = (west_halo, col0, col1, col2, east_halo)
    masks = tile_masks(1)
    for l in range(levels):
        line = [[ref[t, l] for t in range(tracers)] for ref in line_refs]
        for c in range(columns):
            values = advect(line[c + 1], line[c + 2], line[c], rates[0, c, l], rates[1, c, l],
                            [turn[0, t, c, l] for t in range(tracers)], 1, masks)
            for t in range(tracers):
                out[t, c, l] = values[t]


def body(state_adjoint, switches, flags, air_mass, x_flux, y_flux, vertical_mixing):
    state = state_view(state_adjoint)
    switch = pair_view(switches)
    flag = pair_view(flags[None])[0]
    tracers, columns, levels = state.shape[:3]
    order = lax.axis_index("trc").astype(jnp.int32).reshape(1)

    packed, face = call(
        pack_kernel,
        (f32(2, columns, levels, LANES), f32(levels // 2, LANES)),
        (), 10**5, 10**6, air_mass, x_flux, y_flux, vertical_mixing, flag)
    face = shifted(face, "lon", -1)
    edge = shifted(flag[0], "lon", -1)
    others = [swapped(packed, "trc", mask) for mask in (1, 2, 3)]
    east_halo = shifted(state[:, 0], "lon", -1)
    west_halo = shifted(state[:, columns - 1], "lon", 1)
    faces = [swapped(face, "trc", mask) for mask in (1, 2, 3)]

    rates, factors, turn = pl.pallas_call(
        pre_kernel,
        out_shape=(f32(4, columns, levels, 8, LANES), f32(3, columns, levels, 8, LANES),
                   f32(2, tracers, columns, levels, 8, LANES)),
        in_specs=[VMEM] * 11 + [pl.BlockSpec(memory_space=pltpu.SMEM)],
        out_specs=(VMEM,) * 3,
        scratch_shapes=[pltpu.VMEM((4, columns, 2, levels, LANES), jnp.float32),
                        pltpu.VMEM((2, 2, levels // 2, LANES), jnp.float32)],
        compiler_params=pltpu.CompilerParams(vmem_limit_bytes=24 * 1024 * 1024),
        cost_estimate=pl.CostEstimate(flops=10**7, bytes_accessed=10**7, transcendentals=0),
    )(packed, *others, face, *faces, flag, edge, switch, order)

    column = f32(tracers, levels, 8, LANES)
    col0, col1, col2 = call(mid_kernel, (column,) * 3, (), 10**7, 10**7,
                            state, west_halo, east_halo, rates, factors, turn)
    east_halo = shifted(col0, "lon", -1)
    west_halo = shifted(col2, "lon", 1)
    out = call(post_kernel, f32(*state.shape), (), 10**7, 10**6,
               col0, col1, col2, west_halo, east_halo, rates, turn)
    return state_back(out)


def solution(mesh):
    placed = (
        P("trc", None, "lon", None, None),
        P("trc", None, "lon", None, None),
        P(None, "lon", None, None),
        P("lon", None, "trc"),
        P("lon", None, "trc"),
        P("lon", None, "trc"),
        P("lon", None, "trc"),
    )
    return jax.shard_map(
        body,
        mesh=mesh,
        in_specs=placed,
        out_specs=P("trc", None, "lon", None, None),
        check_vma=False,
    )
```

profile of v0, /device:TPU:0, one launch (start us, length us, event | category | flops | bytes accessed | tf_op | source)
XLA Modules:
  0.0 51.8 jit_solution(8594544818187834543)
XLA Ops:
  0.0 1.8 %reshape.23 = f32[2,4,3,34,2,128]{5,4,1,3,2,0:T(2,128)S(1)} reshape(f32[2,4,3,34,256]{4,1,3,2,0:T(4,128)} %param.7) | data formatting | bytes 1671168 | tf_op jit(solution)/shard_map/reshape | solution.py:16
  1.8 0.0 copy-start
  1.8 0.0 copy-start.2
  1.8 0.0 copy-start.3
  1.8 0.0 copy-start.4
  1.8 0.0 copy-start.5
  1.8 0.2 copy.8
  2.1 0.0 copy-start.1
  2.1 6.1 %collective-permute-start.1 = (f32[2,34,8,128]{3,2,1,0:T(8,128)S(1)}, f32[2,34,8,128]{3,2,1,0:T(8,128)S(1)}, u32[]{:S(2)}, u32[]{:S(2)}) collective-permute-start(f32[2,34,8,128]{3,2,1,0:T(8,128)S(1)} %get-tuple-element.21), channel_id=1, source_target_pairs={{0,28},{4,0},{8,4},{12,8},{16,12},{20,16},{24,20},{28,24},{1,29},{... | collective-permute-start | bytes 835592 | tf_op jit(solution)/shard_map/ppermute | solution.py:36
  8.2 0.0 collective-permute-start
  8.2 0.0 copy-done
  8.2 4.8 %collective-permute-start.9 = (s32[17,8,128]{2,1,0:T(8,128)S(1)}, s32[17,8,128]{2,1,0:T(8,128)S(1)}, u32[]{:S(2)}, u32[]{:S(2)}) collective-permute-start(s32[17,8,128]{2,1,0:T(8,128)S(1)} %bitcast.32), channel_id=1, source_target_pairs={{0,28},{4,0},{8,4},{12,8},{16,12},{20,16},{24,20},{28,24},{1,29},{... | collective-permute-start | bytes 208904 | tf_op jit(solution)/shard_map/ppermute | solution.py:36
  13.0 0.0 copy-done.2
  13.0 0.0 copy-done.3
  13.0 0.0 copy-done.4
  13.0 0.0 copy-done.5
  13.0 0.1 shard_map.73
  13.1 0.1 collective-permute-start.5
  13.2 6.3 %collective-permute-done.5.face0 = f32[17,128]{1,0:T(8,128)S(1)} collective-permute-done((f32[17,128]{1,0:T(8,128)S(1)}, f32[17,128]{1,0:T(8,128)S(1)}, u32[]{:S(2)}, u32[]{:S(2)}) %collective-permute-start.5) | collective-permute-done | bytes 8736 | tf_op jit(solution)/shard_map/ppermute | solution.py:36
  19.5 1.1 %collective-permute-start.8 = (f32[17,128]{1,0:T(8,128)S(1)}, f32[17,128]{1,0:T(8,128)S(1)}, u32[]{:S(2)}, u32[]{:S(2)}) collective-permute-start(f32[17,128]{1,0:T(8,128)S(1)} %collective-permute-done.5.face0), channel_id=1, source_target_pairs={{0,3},{1,2},{2,1},{3,0},{4,7},{5,6},{6,5},{7,4},{8,11},{9,10},{10,... | collective-permute-start | bytes 26120 | tf_op jit(solution)/shard_map/ppermute | solution.py:41
  20.6 0.6 %collective-permute-start.7 = (f32[17,128]{1,0:T(8,128)S(1)}, f32[17,128]{1,0:T(8,128)S(1)}, u32[]{:S(2)}, u32[]{:S(2)}) collective-permute-start(f32[17,128]{1,0:T(8,128)S(1)} %collective-permute-done.5.face0), channel_id=1, source_target_pairs={{0,2},{1,3},{2,0},{3,1},{4,6},{5,7},{6,4},{7,5},{8,10},{9,11},{10,... | collective-permute-start | bytes 26120 | tf_op jit(solution)/shard_map/ppermute | solution.py:41
  21.3 1.4 %collective-permute-done.8.face3 = f32[17,128]{1,0:T(8,128)S(1)} collective-permute-done((f32[17,128]{1,0:T(8,128)S(1)}, f32[17,128]{1,0:T(8,128)S(1)}, u32[]{:S(2)}, u32[]{:S(2)}) %collective-permute-start.8) | collective-permute-done | bytes 8736 | tf_op jit(solution)/shard_map/ppermute | solution.py:41
  22.6 0.1 collective-permute-start.6
  22.8 1.6 %collective-permute-done.7.face2 = f32[17,128]{1,0:T(8,128)S(1)} collective-permute-done((f32[17,128]{1,0:T(8,128)S(1)}, f32[17,128]{1,0:T(8,128)S(1)}, u32[]{:S(2)}, u32[]{:S(2)}) %collective-permute-start.7) | collective-permute-done | bytes 8736 | tf_op jit(solution)/shard_map/ppermute | solution.py:41
  24.3 0.2 collective-permute-start.4
  24.6 0.0 collective-permute-done.6.face1
  24.6 1.1 %collective-permute-start.3 = (f32[2,3,34,128]{3,2,1,0:T(8,128)S(1)}, f32[2,3,34,128]{3,2,1,0:T(8,128)S(1)}, u32[]{:S(2)}, u32[]{:S(2)}) collective-permute-start(f32[2,3,34,128]{3,2,1,0:T(8,128)S(1)} %get-tuple-element.13.own), channel_id=1, source_target_pairs={{0,2},{1,3},{2,0},{3,1},{4,6},{5,7},{6,4},{7,5},{8,10},{9,11},{10,... | collective-permute-start | bytes 313352 | tf_op jit(solution)/shard_map/ppermute | solution.py:41
  25.6 0.0 collective-permute-done.9.edge
  25.6 0.6 %collective-permute-start.2 = (f32[2,3,34,128]{3,2,1,0:T(8,128)S(1)}, f32[2,3,34,128]{3,2,1,0:T(8,128)S(1)}, u32[]{:S(2)}, u32[]{:S(2)}) collective-permute-start(f32[2,3,34,128]{3,2,1,0:T(8,128)S(1)} %get-tuple-element.13.own), channel_id=1, source_target_pairs={{0,1},{1,0},{2,3},{3,2},{4,5},{5,4},{6,7},{7,6},{8,9},{9,8},{10,11... | collective-permute-start | bytes 313352 | tf_op jit(solution)/shard_map/ppermute | solution.py:41
  26.2 0.1 copy.11.state
  26.3 3.7 %collective-permute-done.4.third = f32[2,3,34,128]{3,2,1,0:T(8,128)S(1)} collective-permute-done((f32[2,3,34,128]{3,2,1,0:T(8,128)S(1)}, f32[2,3,34,128]{3,2,1,0:T(8,128)S(1)}, u32[]{:S(2)}, u32[]{:S(2)}) %collective-permute-start.4) | collective-permute-done | bytes 104480 | tf_op jit(solution)/shard_map/ppermute | solution.py:41
  29.9 2.1 %collective-permute-done.3.second = f32[2,3,34,128]{3,2,1,0:T(8,128)S(1)} collective-permute-done((f32[2,3,34,128]{3,2,1,0:T(8,128)S(1)}, f32[2,3,34,128]{3,2,1,0:T(8,128)S(1)}, u32[]{:S(2)}, u32[]{:S(2)}) %collective-permute-start.3) | collective-permute-done | bytes 104480 | tf_op jit(solution)/shard_map/ppermute | solution.py:41
  32.1 0.0 collective-permute-done.2.first
  32.1 0.0 copy-done.1
  32.1 1.2 %shard_map.74 = (f32[4,3,34,8,128]{4,3,2,1,0:T(8,128)S(1)}, f32[3,3,34,8,128]{4,3,2,1,0:T(8,128)S(1)}, f32[2,2,3,34,8,128]{5,4,3,2,1,0:T(8,128)S(1)}) custom-call(f32[2,3,34,128]{3,2,1,0:T(8,128)S(1)} %get-tuple-element.13.own, f32[2,3,34,128]{3,2,1,0:T(8,128)S(1)} %collective-permute-done.2.first, f32[2,3,34,128]{3,2,1,0:T(8,128)S(1)} %collective-permute-done.3.second, ...), custom_call_target="tpu_custom_call" | custom-call | flops 10000000 | bytes 10000000 | tf_op jit(solution)/shard_map/pallas_call | solution.py:267
  33.3 0.0 collective-permute-done.1.east_halo
  33.3 0.0 collective-permute-done.west_halo
  33.3 2.3 %shard_map.75 = (f32[2,34,8,128]{3,2,1,0:T(8,128)S(1)}, f32[2,34,8,128]{3,2,1,0:T(8,128)S(1)}, f32[2,34,8,128]{3,2,1,0:T(8,128)S(1)}) custom-call(f32[2,3,34,8,128]{4,3,2,1,0:T(8,128)S(1)} %copy.11.state, f32[2,34,8,128]{3,2,1,0:T(8,128)S(1)} %collective-permute-done.west_halo, f32[2,34,8,128]{3,2,1,0:T(8,128)S(1)} %collective-permute-done.1.east_halo, ...), custom_call_target="tpu_custom_call" | custom-call | flops 10000000 | bytes 10000000 | tf_op jit(solution)/shard_map/pallas_call | solution.py:45
  35.6 2.3 %collective-permute-start.11 = (f32[2,34,8,128]{3,2,1,0:T(8,128)S(1)}, f32[2,34,8,128]{3,2,1,0:T(8,128)S(1)}, u32[]{:S(2)}, u32[]{:S(2)}) collective-permute-start(f32[2,34,8,128]{3,2,1,0:T(8,128)S(1)} %get-tuple-element.18.col0), channel_id=1, source_target_pairs={{0,28},{4,0},{8,4},{12,8},{16,12},{20,16},{24,20},{28,24},{1,29},{... | collective-permute-start | bytes 835592 | tf_op jit(solution)/shard_map/ppermute | solution.py:36
  37.9 0.0 collective-permute-start.10
  37.9 12.4 %collective-permute-done.11.east_halo = f32[2,34,8,128]{3,2,1,0:T(8,128)S(1)} collective-permute-done((f32[2,34,8,128]{3,2,1,0:T(8,128)S(1)}, f32[2,34,8,128]{3,2,1,0:T(8,128)S(1)}, u32[]{:S(2)}, u32[]{:S(2)}) %collective-permute-start.11) | collective-permute-done | bytes 278560 | tf_op jit(solution)/shard_map/ppermute | solution.py:36
  50.3 0.0 collective-permute-done.10.west_halo
  50.3 1.6 %shard_map.76 = f32[2,3,34,8,128]{4,3,2,1,0:T(8,128)} custom-call(f32[2,34,8,128]{3,2,1,0:T(8,128)S(1)} %get-tuple-element.18.col0, f32[2,34,8,128]{3,2,1,0:T(8,128)S(1)} %get-tuple-element.19.col1, f32[2,34,8,128]{3,2,1,0:T(8,128)S(1)} %get-tuple-element.20.col2, f32[2,34,8,128]{3,2,1,0:T(8,128)S(1)} %collective-permute-done.10.west_halo, ...), custom_call_target="tpu_custom_call" | custom-call | flops 10000000 | bytes 1000000 | tf_op jit(solution)/shard_map/pallas_call | solution.py:45
  (2 shorter events, 0.0 us)
Async XLA Ops:
  1.8 6.4 %copy-start = (s32[2,3,34,256]{3,0,2,1:T(2,128)S(1)}, s32[2,3,34,256]{3,0,2,1:T(2,128)}, u32[]{:S(2)}) copy-start(s32[2,3,34,256]{3,0,2,1:T(2,128)} %param.9) | copy-start | bytes 626692
  1.8 11.2 %copy-start.2 = (f32[3,34,64]{2,1,0:T(8,128)S(1)}, f32[3,34,64]{2,1,0:T(8,128)}, u32[]{:S(2)}) copy-start(f32[3,34,64]{2,1,0:T(8,128)} %mass.1) | copy-start | bytes 78340
  1.8 11.2 %copy-start.3 = (f32[3,34,64]{2,1,0:T(8,128)S(1)}, f32[3,34,64]{2,1,0:T(8,128)}, u32[]{:S(2)}) copy-start(f32[3,34,64]{2,1,0:T(8,128)} %xf.1) | copy-start | bytes 78340
  1.8 11.2 %copy-start.4 = (f32[3,34,64]{2,1,0:T(8,128)S(1)}, f32[3,34,64]{2,1,0:T(8,128)}, u32[]{:S(2)}) copy-start(f32[3,34,64]{2,1,0:T(8,128)} %yf.1) | copy-start | bytes 78340
  1.8 11.2 %copy-start.5 = (f32[3,33,64]{2,1,0:T(8,128)S(1)}, f32[3,33,64]{2,1,0:T(8,128)}, u32[]{:S(2)}) copy-start(f32[3,33,64]{2,1,0:T(8,128)} %km.1) | copy-start | bytes 76036
  2.1 30.0 %copy-start.1 = (s32[2,2,3,34,256]{4,1,3,2,0:T(2,128)S(1)}, s32[2,2,3,34,256]{4,1,3,2,0:T(2,128)}, u32[]{:S(2)}) copy-start(s32[2,2,3,34,256]{4,1,3,2,0:T(2,128)} %param.8) | copy-start | bytes 1253380
  2.1 31.2 %collective-permute-start.1 = (f32[2,34,8,128]{3,2,1,0:T(8,128)S(1)}, f32[2,34,8,128]{3,2,1,0:T(8,128)S(1)}, u32[]{:S(2)}, u32[]{:S(2)}) collective-permute-start(f32[2,34,8,128]{3,2,1,0:T(8,128)S(1)} %get-tuple-element.21), channel_id=1, source_target_pairs={{0,28},{4,0},{8,4},{12,8},{16,12},{20,16},{24,20},{28,24},{1,29},{... | collective-permute-start | bytes 835592 | tf_op jit(solution)/shard_map/ppermute | solution.py:36
  8.2 25.1 %collective-permute-start = (f32[2,34,8,128]{3,2,1,0:T(8,128)S(1)}, f32[2,34,8,128]{3,2,1,0:T(8,128)S(1)}, u32[]{:S(2)}, u32[]{:S(2)}) collective-permute-start(f32[2,34,8,128]{3,2,1,0:T(8,128)S(1)} %get-tuple-element.22), channel_id=1, source_target_pairs={{0,4},{4,8},{8,12},{12,16},{16,20},{20,24},{24,28},{28,0},{1,5},{5... | collective-permute-start | bytes 835592 | tf_op jit(solution)/shard_map/ppermute | solution.py:36
  8.2 17.4 %collective-permute-start.9 = (s32[17,8,128]{2,1,0:T(8,128)S(1)}, s32[17,8,128]{2,1,0:T(8,128)S(1)}, u32[]{:S(2)}, u32[]{:S(2)}) collective-permute-start(s32[17,8,128]{2,1,0:T(8,128)S(1)} %bitcast.32), channel_id=1, source_target_pairs={{0,28},{4,0},{8,4},{12,8},{16,12},{20,16},{24,20},{28,24},{1,29},{... | collective-permute-start | bytes 208904 | tf_op jit(solution)/shard_map/ppermute | solution.py:36
  13.1 6.4 %collective-permute-start.5 = (f32[17,128]{1,0:T(8,128)S(1)}, f32[17,128]{1,0:T(8,128)S(1)}, u32[]{:S(2)}, u32[]{:S(2)}) collective-permute-start(f32[17,128]{1,0:T(8,128)S(1)} %get-tuple-element.14), channel_id=1, source_target_pairs={{0,28},{4,0},{8,4},{12,8},{16,12},{20,16},{24,20},{28,24},{1,29},{... | collective-permute-start | bytes 26120 | tf_op jit(solution)/shard_map/ppermute | solution.py:36
  19.5 3.1 %collective-permute-start.8 = (f32[17,128]{1,0:T(8,128)S(1)}, f32[17,128]{1,0:T(8,128)S(1)}, u32[]{:S(2)}, u32[]{:S(2)}) collective-permute-start(f32[17,128]{1,0:T(8,128)S(1)} %collective-permute-done.5.face0), channel_id=1, source_target_pairs={{0,3},{1,2},{2,1},{3,0},{4,7},{5,6},{6,5},{7,4},{8,11},{9,10},{10,... | collective-permute-start | bytes 26120 | tf_op jit(solution)/shard_map/ppermute | solution.py:41
  20.6 3.7 %collective-permute-start.7 = (f32[17,128]{1,0:T(8,128)S(1)}, f32[17,128]{1,0:T(8,128)S(1)}, u32[]{:S(2)}, u32[]{:S(2)}) collective-permute-start(f32[17,128]{1,0:T(8,128)S(1)} %collective-permute-done.5.face0), channel_id=1, source_target_pairs={{0,2},{1,3},{2,0},{3,1},{4,6},{5,7},{6,4},{7,5},{8,10},{9,11},{10,... | collective-permute-start | bytes 26120 | tf_op jit(solution)/shard_map/ppermute | solution.py:41
  22.6 1.9 %collective-permute-start.6 = (f32[17,128]{1,0:T(8,128)S(1)}, f32[17,128]{1,0:T(8,128)S(1)}, u32[]{:S(2)}, u32[]{:S(2)}) collective-permute-start(f32[17,128]{1,0:T(8,128)S(1)} %collective-permute-done.5.face0), channel_id=1, source_target_pairs={{0,1},{1,0},{2,3},{3,2},{4,5},{5,4},{6,7},{7,6},{8,9},{9,8},{10,11... | collective-permute-start | bytes 26120 | tf_op jit(solution)/shard_map/ppermute | solution.py:41
  24.3 5.6 %collective-permute-start.4 = (f32[2,3,34,128]{3,2,1,0:T(8,128)S(1)}, f32[2,3,34,128]{3,2,1,0:T(8,128)S(1)}, u32[]{:S(2)}, u32[]{:S(2)}) collective-permute-start(f32[2,3,34,128]{3,2,1,0:T(8,128)S(1)} %get-tuple-element.13.own), channel_id=1, source_target_pairs={{0,3},{1,2},{2,1},{3,0},{4,7},{5,6},{6,5},{7,4},{8,11},{9,10},{10,... | collective-permute-start | bytes 313352 | tf_op jit(solution)/shard_map/ppermute | solution.py:41
  24.6 7.5 %collective-permute-start.3 = (f32[2,3,34,128]{3,2,1,0:T(8,128)S(1)}, f32[2,3,34,128]{3,2,1,0:T(8,128)S(1)}, u32[]{:S(2)}, u32[]{:S(2)}) collective-permute-start(f32[2,3,34,128]{3,2,1,0:T(8,128)S(1)} %get-tuple-element.13.own), channel_id=1, source_target_pairs={{0,2},{1,3},{2,0},{3,1},{4,6},{5,7},{6,4},{7,5},{8,10},{9,11},{10,... | collective-permute-start | bytes 313352 | tf_op jit(solution)/shard_map/ppermute | solution.py:41
  25.6 6.4 %collective-permute-start.2 = (f32[2,3,34,128]{3,2,1,0:T(8,128)S(1)}, f32[2,3,34,128]{3,2,1,0:T(8,128)S(1)}, u32[]{:S(2)}, u32[]{:S(2)}) collective-permute-start(f32[2,3,34,128]{3,2,1,0:T(8,128)S(1)} %get-tuple-element.13.own), channel_id=1, source_target_pairs={{0,1},{1,0},{2,3},{3,2},{4,5},{5,4},{6,7},{7,6},{8,9},{9,8},{10,11... | collective-permute-start | bytes 313352 | tf_op jit(solution)/shard_map/ppermute | solution.py:41
  35.6 14.7 %collective-permute-start.11 = (f32[2,34,8,128]{3,2,1,0:T(8,128)S(1)}, f32[2,34,8,128]{3,2,1,0:T(8,128)S(1)}, u32[]{:S(2)}, u32[]{:S(2)}) collective-permute-start(f32[2,34,8,128]{3,2,1,0:T(8,128)S(1)} %get-tuple-element.18.col0), channel_id=1, source_target_pairs={{0,28},{4,0},{8,4},{12,8},{16,12},{20,16},{24,20},{28,24},{1,29},{... | collective-permute-start | bytes 835592 | tf_op jit(solution)/shard_map/ppermute | solution.py:36
  37.9 12.4 %collective-permute-start.10 = (f32[2,34,8,128]{3,2,1,0:T(8,128)S(1)}, f32[2,34,8,128]{3,2,1,0:T(8,128)S(1)}, u32[]{:S(2)}, u32[]{:S(2)}) collective-permute-start(f32[2,34,8,128]{3,2,1,0:T(8,128)S(1)} %get-tuple-element.20.col2), channel_id=1, source_target_pairs={{0,4},{4,8},{8,12},{12,16},{16,20},{20,24},{24,28},{28,0},{1,5},{5... | collective-permute-start | bytes 835592 | tf_op jit(solution)/shard_map/ppermute | solution.py:36
where the time goes:
time: 52 us; the launch traced here: 51.8 us
  waiting for transfers between devices  27.5 us (53%)
  starting transfers between devices  17 us (33%)
  Pallas kernels  5.11 us (10%)
  local copies, waits for them, and re-layouts  2.12 us (4%)
    ppermute x6, waiting for transfers between devices, shifted(): lax.ppermute(value, axis, [(i, (i + by) % count) for i in range(count)])  18.7 us
    ppermute x6, starting transfers between devices, shifted(): lax.ppermute(value, axis, [(i, (i + by) % count) for i in range(count)])  13.2 us
    ppermute x6, waiting for transfers between devices, swapped(): return lax.ppermute(value, axis, [(i, i ^ mask) for i in range(count)])  8.77 us
    pallas_call x3, Pallas kernels, call(): pl.pallas_call(kernel, out_shape=out, in_specs=[VMEM] * len(args), out_sp...  3.92 us
    ppermute x6, starting transfers between devices, swapped(): return lax.ppermute(value, axis, [(i, i ^ mask) for i in range(count)])  3.72 us
    reshape x2, local copies, waits for them, and re-layouts, state_view(): x = x.reshape(t, m, c, l, b, LANES).transpose(0, 2, 3, 4, 1, 5)  1.99 us
    pallas_call x1, Pallas kernels, body(): pl.pallas_call(pre_kernel, out_shape=(f32(4, columns, levels, 8, LANES),...  1.19 us
  transfers between devices with their start and end apart: 12, of which 6 were waited for; matrix products, arithmetic and copies ran while one was open for 0% of the time, Pallas kernels for 2%

commit v1 on v0

v1 whole, which is shorter than its diff:
```python
import jax
import jax.numpy as jnp
from jax import lax
from jax.experimental import pallas as pl
from jax.experimental.pallas import tpu as pltpu
from jax.sharding import PartitionSpec as P

LANES = 128
MOMENTS = 4
VMEM = pl.BlockSpec(memory_space=pltpu.VMEM)
SMEM = pl.BlockSpec(memory_space=pltpu.SMEM)
ANY = pl.BlockSpec(memory_space=pl.ANY)


def state_view(x):
    t, m, c, l, n = x.shape
    b = n // LANES
    x = x.reshape(t, m, c, l, b, LANES).transpose(0, 2, 3, 4, 1, 5)
    return x.reshape(t, c, l, b * m, LANES)


def pair_view(x):
    t, d, c, l, n = x.shape
    b = n // LANES
    x = x.reshape(t, d, c, l, b, LANES).transpose(0, 2, 3, 4, 1, 5)
    return x.reshape(t, c, l * b * d, LANES)


def state_back(y):
    t, c, l, rows, _ = y.shape
    b = rows // MOMENTS
    y = y.reshape(t, c, l, b, MOMENTS, LANES).transpose(0, 4, 1, 2, 3, 5)
    return y.reshape(t, MOMENTS, c, l, b * LANES)


def shifted(value, axis, by):
    count = lax.axis_size(axis)
    return lax.ppermute(value, axis, [(i, (i + by) % count) for i in range(count)])


def swapped(value, axis, mask):
    count = lax.axis_size(axis)
    return lax.ppermute(value, axis, [(i, i ^ mask) for i in range(count)])


def call(kernel, out, in_specs, scratch, flops, moved, *args):
    return pl.pallas_call(
        kernel,
        out_shape=out,
        in_specs=in_specs,
        out_specs=jax.tree.map(lambda _: VMEM, out),
        scratch_shapes=scratch,
        compiler_params=pltpu.CompilerParams(vmem_limit_bytes=24 * 1024 * 1024),
        cost_estimate=pl.CostEstimate(flops=flops, bytes_accessed=moved, transcendentals=0),
    )(*args)


def f32(*shape):
    return jax.ShapeDtypeStruct(shape, jnp.float32)


def tile_masks(slope):
    row = lax.broadcasted_iota(jnp.int32, (8, LANES), 0) % MOMENTS
    return row == 0, row == slope


def head_kernel(state, flags, xf, order, col0, col1, col2, face, sems):
    tracers, levels = state.shape[0], xf.shape[1]
    half = LANES // 2
    copies = [pltpu.make_async_copy(state.at[t, c], col.at[t], sems.at[c, t])
              for c, col in enumerate((col0, col1, col2)) for t in range(tracers)]
    for copy in copies:
        copy.start()
    odd, high = order[0] % 2 == 1, order[0] >= 2
    block0 = flags[0, pl.ds(0, levels, stride=4), :].astype(jnp.float32)
    block1 = flags[0, pl.ds(2, levels, stride=4), :].astype(jnp.float32)
    chosen = jnp.where(high, block1, block0)
    chosen = jnp.where(odd, pltpu.roll(chosen, half, 1), chosen)[:, :half]
    signed = (2.0 * chosen - 1.0) * xf[0]
    face[:, :half] = signed[: levels // 2]
    face[:, half:] = signed[levels // 2 :]
    for copy in copies:
        copy.wait()


def pack_kernel(mass, xf, yf, km, face, packed):
    half = LANES // 2
    columns, levels = mass.shape[:2]
    for c in range(columns):
        low, top = c * levels, (columns + c) * levels
        packed[low : low + levels, :half] = mass[c]
        packed[low : low + levels, half:] = xf[c]
        packed[top : top + levels, :half] = yf[c]
        packed[top : top + levels - 1, half:] = km[c]
        packed[top + levels - 1 : top + levels, half:] = jnp.zeros((1, half), jnp.float32)
    tail = 2 * columns * levels
    packed[tail : tail + levels // 2] = face[...]


def spread(upper_block, ref, *where):
    blocks = [jnp.broadcast_to(ref[(*index, pl.ds(r, 1), slice(None))], (8, LANES)) for index, r in where]
    return jnp.where(upper_block, blocks[1], blocks[0])


def turn_kernel(switches, turn):
    tracers, columns = switches.shape[:2]
    levels = switches.shape[2] // 4
    row = lax.broadcasted_iota(jnp.int32, (8, LANES), 0)
    moment = row % MOMENTS
    for t in range(tracers):
        for c in range(columns):
            for l in range(levels):
                for d in range(2):
                    base = l * 4 + d
                    sw = spread(row >= MOMENTS, switches, ((t, c), base), ((t, c), base + 2))
                    take = jnp.where(sw == 1, 1.0, jnp.where(sw == 2, -1.0, 0.0))
                    keep = jnp.where(sw == 0, 1.0, 0.0)
                    turn[d, t, c, l] = jnp.where(moment == 0, take, jnp.where(moment == 1 + d, keep, 1.0))


def pre_kernel(own, first, second, third, flags, order, rates, factors, fields, faces):
    columns, levels = rates.shape[1], rates.shape[2]
    half = LANES // 2
    odd = order[0] % 2 == 1
    high = order[0] >= 2
    lane = lax.broadcasted_iota(jnp.int32, (8, LANES), 1)
    row = lax.broadcasted_iota(jnp.int32, (8, LANES), 0)
    upper_block = row >= MOMENTS
    lane_low = lax.broadcasted_iota(jnp.int32, (levels, LANES), 1) < half

    def sorted_shards(start, count):
        a, b, c, d = (ref[start : start + count] for ref in (own, first, second, third))
        a, b, c, d = (jnp.where(odd, b, a), jnp.where(odd, a, b), jnp.where(odd, d, c), jnp.where(odd, c, d))
        return (jnp.where(high, c, a), jnp.where(high, d, b), jnp.where(high, a, c), jnp.where(high, b, d))

    for pair in range(2):
        for c in range(columns):
            shards = sorted_shards((pair * columns + c) * levels, levels)
            for b in range(2):
                lo, hi = shards[2 * b], shards[2 * b + 1]
                fields[2 * pair, c, b] = jnp.where(lane_low, lo, pltpu.roll(hi, half, 1))
                fields[2 * pair + 1, c, b] = jnp.where(lane_low, pltpu.roll(lo, half, 1), hi)
    shards = sorted_shards(2 * columns * levels, levels // 2)
    short = lane_low[: levels // 2]
    for b in range(2):
        lo, hi = shards[2 * b], shards[2 * b + 1]
        faces[0, b] = jnp.where(short, lo, pltpu.roll(hi, half, 1))
        faces[1, b] = jnp.where(short, pltpu.roll(lo, half, 1), hi)

    def field(f, c, l):
        return spread(upper_block, fields, ((f, c, 0), l), ((f, c, 1), l))

    def flag(c, l, d):
        base = l * 4 + d
        return spread(upper_block, flags, ((c,), base), ((c,), base + 2)).astype(jnp.float32)

    first_row = (lane == 0) & (row < MOMENTS)
    last_row = (lane == LANES - 1) & (row >= MOMENTS)
    for l in range(levels):
        flux_x = [field(1, c, l) for c in range(columns)]
        flag_x = [flag(c, l, 0) for c in range(columns)]
        east = [flag_x[c] * flux_x[c] for c in range(columns)]
        west = [flux_x[c] - east[c] for c in range(columns)]
        deep, level = divmod(l, levels // 2)
        east.append(jnp.maximum(spread(upper_block, faces, ((deep, 0), level), ((deep, 1), level)), 0.0))
        for c in range(columns):
            share = 1.0 / field(0, c, l)
            rates[0, c, l] = east[c + 1] * share
            rates[1, c, l] = west[c] * share
            flux_y = field(2, c, l)
            north = flag(c, l, 1) * flux_y
            south = pltpu.roll(flux_y - north, 1, 1)
            south = jnp.where(lane == 0, pltpu.roll(south, 4, 0), south)
            rates[2, c, l] = jnp.where(last_row, 0.0, north) * share
            rates[3, c, l] = jnp.where(first_row, 0.0, south) * share

    fixed = row % MOMENTS == 3
    zero = jnp.zeros((8, LANES), jnp.float32)
    below, upper = [None] * columns, [None] * columns
    for l in range(levels):
        for c in range(columns):
            diagonal = zero + 1.0
            if l > 0:
                diagonal = diagonal + below[c]
            if l < levels - 1:
                above = field(3, c, l)
                diagonal = diagonal + above
            if l > 0:
                diagonal = diagonal + below[c] * upper[c]
            inverse = 1.0 / diagonal
            factors[0, c, l] = jnp.where(fixed, 1.0, inverse)
            factors[2, c, l] = jnp.where(fixed, 0.0, below[c] * inverse) if l > 0 else zero
            if l < levels - 1:
                upper[c] = -above * inverse
                factors[1, c, l] = jnp.where(fixed, 0.0, upper[c])
                below[c] = above
            else:
                factors[1, c, l] = zero


def advect(own, east_side, west_side, east, west, turns, slope, masks):
    is_mass, is_slope = masks
    stay = 1.0 - (east + west)
    east_part = east * jnp.where(is_slope, east, 1.0)
    west_part = west * jnp.where(is_slope, west, 1.0)
    east_cross = east * (1.0 - east)
    west_cross = west * (1.0 - west)
    out = []
    for s, e, w, z in zip(own, east_side, west_side, turns):
        total = stay * s + east_part * e + west_part * w
        cross = east_cross * (e - s) - west_cross * (w - s)
        total = total + jnp.where(is_slope, pltpu.roll(cross, slope, 0), 0.0)
        slope_up = pltpu.roll(total, 8 - slope, 0)
        out.append(z * jnp.where(is_mass, slope_up, total) + jnp.where(is_mass, total, 0.0))
    return out


def middle(todo, line_refs, rates, factors, turn, outs):
    tracers, levels = outs[0].shape[0], outs[0].shape[1]
    lane = lax.broadcasted_iota(jnp.int32, (8, LANES), 1)
    at_first, at_last = lane == 0, lane == LANES - 1
    x_masks, y_masks = tile_masks(1), tile_masks(2)
    every = range(tracers)

    def prev(v):
        r = pltpu.roll(v, 1, 1)
        return jnp.where(at_first, pltpu.roll(r, 4, 0), r)

    def following(v):
        r = pltpu.roll(v, LANES - 1, 1)
        return jnp.where(at_last, pltpu.roll(r, 4, 0), r)

    def y_step(values, c, l):
        return advect(values, [following(v) for v in values], [prev(v) for v in values],
                      rates[2, c, l], rates[3, c, l], [turn[1, t, c, l] for t in every], 2, y_masks)

    carried = {c: [None] * tracers for c in todo}
    for l in range(levels):
        line = [None if ref is None else [ref[t, l] for t in every] for ref in line_refs]
        for c, out in zip(todo, outs):
            values = advect(line[c + 1], line[c + 2], line[c], rates[0, c, l], rates[1, c, l],
                            [turn[0, t, c, l] for t in every], 1, x_masks)
            values = y_step(values, c, l)
            for t in every:
                v = values[t] * factors[0, c, l]
                if l > 0:
                    v = v + factors[2, c, l] * carried[c][t]
                carried[c][t] = v
                out[t, l] = v
    for l in range(levels - 1, -1, -1):
        for c, out in zip(todo, outs):
            if l < levels - 1:
                for t in every:
                    carried[c][t] = out[t, l] - factors[1, c, l] * carried[c][t]
            values = y_step(carried[c], c, l)
            for t in every:
                out[t, l] = values[t]


def inner_kernel(col0, col1, col2, rates, factors, turn, out):
    middle((1,), (None, col0, col1, col2, None), rates, factors, turn, (out,))


def outer_kernel(col0, col1, col2, west_halo, east_halo, rates, factors, turn, out0, out2):
    middle((0, 2), (west_halo, col0, col1, col2, east_halo), rates, factors, turn, (out0, out2))


def post_kernel(col0, col1, col2, west_halo, east_halo, rates, turn, out):
    tracers, columns, levels = out.shape[0], out.shape[1], out.shape[2]
    line_refs = (west_halo, col0, col1, col2, east_halo)
    masks = tile_masks(1)
    for l in range(levels):
        line = [[ref[t, l] for t in range(tracers)] for ref in line_refs]
        for c in range(columns):
            values = advect(line[c + 1], line[c + 2], line[c], rates[0, c, l], rates[1, c, l],
                            [turn[0, t, c, l] for t in range(tracers)], 1, masks)
            for t in range(tracers):
                out[t, c, l] = values[t]


def body(state_adjoint, switches, flags, air_mass, x_flux, y_flux, vertical_mixing):
    state = state_view(state_adjoint)
    switch = pair_view(switches)
    flag = pair_view(flags[None])[0]
    tracers, columns, levels = state.shape[:3]
    order = lax.axis_index("trc").astype(jnp.int32).reshape(1)
    column = f32(tracers, levels, 8, LANES)
    face_shape = f32(levels // 2, LANES)

    col0, col1, col2, face = call(
        head_kernel, (column,) * 3 + (face_shape,), (ANY, VMEM, VMEM, SMEM),
        [pltpu.SemaphoreType.DMA((columns, tracers))], 10**5, 10**6, state, flag, x_flux, order)
    face = shifted(face, "lon", -1)
    east_halo = shifted(col0, "lon", -1)
    west_halo = shifted(col2, "lon", 1)
    rows = -(-(2 * columns * levels + levels // 2) // 8) * 8
    packed = call(pack_kernel, f32(rows, LANES), (VMEM,) * 5, (), 10**5, 10**6,
                  air_mass, x_flux, y_flux, vertical_mixing, face)
    others = [swapped(packed, "trc", mask) for mask in (1, 2, 3)]
    turn = call(turn_kernel, f32(2, tracers, columns, levels, 8, LANES), (VMEM,), (), 10**6, 10**6, switch)
    rates, factors = call(
        pre_kernel, (f32(4, columns, levels, 8, LANES), f32(3, columns, levels, 8, LANES)),
        (VMEM,) * 5 + (SMEM,),
        [pltpu.VMEM((4, columns, 2, levels, LANES), jnp.float32),
         pltpu.VMEM((2, 2, levels // 2, LANES), jnp.float32)],
        10**7, 10**7, packed, *others, flag, order)
    mid1 = call(inner_kernel, column, (VMEM,) * 6, (), 10**7, 10**7, col0, col1, col2, rates, factors, turn)
    mid0, mid2 = call(outer_kernel, (column,) * 2, (VMEM,) * 8, (), 10**7, 10**7,
                      col0, col1, col2, west_halo, east_halo, rates, factors, turn)
    east_halo = shifted(mid0, "lon", -1)
    west_halo = shifted(mid2, "lon", 1)
    out = call(post_kernel, f32(*state.shape), (VMEM,) * 7, (), 10**7, 10**6,
               mid0, mid1, mid2, west_halo, east_halo, rates, turn)
    return state_back(out)


def solution(mesh):
    placed = (
        P("trc", None, "lon", None, None),
        P("trc", None, "lon", None, None),
        P(None, "lon", None, None),
        P("lon", None, "trc"),
        P("lon", None, "trc"),
        P("lon", None, "trc"),
        P("lon", None, "trc"),
    )
    return jax.shard_map(
        body,
        mesh=mesh,
        in_specs=placed,
        out_specs=P("trc", None, "lon", None, None),
        check_vma=False,
    )
```

time: 52 us -> 48.8 us (0.938)
  waiting for transfers between devices: 27.5 us -> 17.3 us
  local copies, waits for them, and re-layouts: 2.12 us -> 5.4 us
  starting transfers between devices: 17 us -> 19.2 us
  Pallas kernels: 5.11 us -> 6.47 us
    ppermute x6 -> x5, waiting for transfers between devices: 18.7 us -> 11.7 us  [shifted(): lax.ppermute(value, axis, [(i, (i + by) % count) for i in range(count)])]
    unnamed x12 -> x16, local copies, waits for them, and re-layouts: 0.04 us -> 5.4 us
    ppermute x6 -> x5, starting transfers between devices: 13.2 us -> 17.3 us  [shifted(): lax.ppermute(value, axis, [(i, (i + by) % count) for i in range(count)])]
    ppermute x6 -> x3, waiting for transfers between devices: 8.77 us -> 5.55 us  [swapped(): return lax.ppermute(value, axis, [(i, i ^ mask) for i in range(count)])]
    reshape x3 -> x0, local copies, waits for them, and re-layouts: 2.04 us -> none  [the longest x2 1.99 us: state_view(): x = x.reshape(t, m, c, l, b, LANES).transpose(0, 2, 3, 4, 1, 5)]
    ppermute x6 -> x3, starting transfers between devices: 3.72 us -> 1.93 us  [swapped(): return lax.ppermute(value, axis, [(i, i ^ mask) for i in range(count)])]
    pallas_call x4 -> x7, Pallas kernels: 5.11 us -> 6.47 us  [call(): pl.pallas_call(kernel, out_shape=out, in_specs=in_specs, out_specs=jax.tr...]
  transfers between devices with their start and end apart: 12 -> 8, of which waited for: 6 -> 5; matrix products, arithmetic and copies ran while one was open for 0% -> 0% of each run, Pallas kernels for 2% -> 4%
where the time goes in v1:
time: 48.8 us; the launch traced here: 48.4 us
  starting transfers between devices  19.2 us (39%)
  waiting for transfers between devices  17.3 us (35%)
  Pallas kernels  6.47 us (13%)
  local copies, waits for them, and re-layouts  5.4 us (11%)
    ppermute x5, starting transfers between devices, shifted(): lax.ppermute(value, axis, [(i, (i + by) % count) for i in range(count)])  17.3 us
    ppermute x5, waiting for transfers between devices, shifted(): lax.ppermute(value, axis, [(i, (i + by) % count) for i in range(count)])  11.7 us
    pallas_call x7, Pallas kernels, call(): pl.pallas_call(kernel, out_shape=out, in_specs=in_specs, out_specs=jax.tr...  6.47 us
    ppermute x3, waiting for transfers between devices, swapped(): return lax.ppermute(value, axis, [(i, i ^ mask) for i in range(count)])  5.55 us
    unnamed x16, local copies, waits for them, and re-layouts  5.4 us
    ppermute x3, starting transfers between devices, swapped(): return lax.ppermute(value, axis, [(i, i ^ mask) for i in range(count)])  1.93 us
  transfers between devices with their start and end apart: 8, of which 5 were waited for; matrix products, arithmetic and copies ran while one was open for 0% of the time, Pallas kernels for 4%

profile of v1, /device:TPU:0, one launch (start us, length us, event | category | flops | bytes accessed | tf_op | source)
XLA Modules:
  0.0 48.4 jit_solution(407290909152773039)
XLA Ops:
  0.0 0.0 copy-start
  0.0 1.1 %copy-done = f32[2,4,3,34,256]{4,1,3,2,0:T(4,128)S(1)} copy-done((f32[2,4,3,34,256]{4,1,3,2,0:T(4,128)S(1)}, f32[2,4,3,34,256]{4,1,3,2,0:T(4,128)}, u32[]{:S(2)}) %copy-start) | copy-done | bytes 835608
  1.2 0.0 copy-start.1
  1.2 0.9 %copy-done.1 = s32[2,3,34,256]{3,0,2,1:T(2,128)S(1)} copy-done((s32[2,3,34,256]{3,0,2,1:T(2,128)S(1)}, s32[2,3,34,256]{3,0,2,1:T(2,128)}, u32[]{:S(2)}) %copy-start.1) | copy-done | bytes 208920
  2.1 0.0 copy-start.4
  2.1 0.8 %copy-done.4 = f32[3,34,64]{2,1,0:T(8,128)S(1)} copy-done((f32[3,34,64]{2,1,0:T(8,128)S(1)}, f32[3,34,64]{2,1,0:T(8,128)}, u32[]{:S(2)}) %copy-start.4) | copy-done | bytes 26136
  2.9 0.0 copy-start.3
  2.9 0.0 copy-start.2
  2.9 1.3 %shard_map.73 = (f32[2,34,8,128]{3,2,1,0:T(8,128)S(1)}, f32[2,34,8,128]{3,2,1,0:T(8,128)S(1)}, f32[2,34,8,128]{3,2,1,0:T(8,128)S(1)}, f32[17,128]{1,0:T(8,128)S(1)}) custom-call(f32[2,3,34,8,128]{4,3,2,1,0:T(8,128)S(1)} %bitcast.21, s32[3,136,128]{2,1,0:T(8,128)S(1)} %bitcast.22, f32[3,34,64]{2,1,0:T(8,128)S(1)} %copy-done.4, s32[1]{0:T(128)} %bitcast.6.order), custom_call_target="tpu_custom_call" | custom-call | flops 100000 | bytes 1000000 | tf_op jit(solution)/shard_map/pallas_call | solution.py:47
  4.2 6.1 %collective-permute-start.1 = (f32[2,34,8,128]{3,2,1,0:T(8,128)S(1)}, f32[2,34,8,128]{3,2,1,0:T(8,128)S(1)}, u32[]{:S(2)}, u32[]{:S(2)}) collective-permute-start(f32[2,34,8,128]{3,2,1,0:T(8,128)S(1)} %get-tuple-element.13.col0), channel_id=1, source_target_pairs={{0,28},{4,0},{8,4},{12,8},{16,12},{20,16},{24,20},{28,24},{1,29},{... | collective-permute-start | bytes 835592 | tf_op jit(solution)/shard_map/ppermute | solution.py:38
  10.3 0.0 collective-permute-start
  10.3 4.7 %collective-permute-start.2 = (f32[17,128]{1,0:T(8,128)S(1)}, f32[17,128]{1,0:T(8,128)S(1)}, u32[]{:S(2)}, u32[]{:S(2)}) collective-permute-start(f32[17,128]{1,0:T(8,128)S(1)} %get-tuple-element.16), channel_id=1, source_target_pairs={{0,28},{4,0},{8,4},{12,8},{16,12},{20,16},{24,20},{28,24},{1,29},{... | collective-permute-start | bytes 26120 | tf_op jit(solution)/shard_map/ppermute | solution.py:38
  15.0 1.5 %collective-permute-done.2.face = f32[17,128]{1,0:T(8,128)S(1)} collective-permute-done((f32[17,128]{1,0:T(8,128)S(1)}, f32[17,128]{1,0:T(8,128)S(1)}, u32[]{:S(2)}, u32[]{:S(2)}) %collective-permute-start.2) | collective-permute-done | bytes 8736 | tf_op jit(solution)/shard_map/ppermute | solution.py:38
  16.4 0.0 copy-start.5
  16.4 0.8 %copy-done.5 = f32[3,34,64]{2,1,0:T(8,128)S(1)} copy-done((f32[3,34,64]{2,1,0:T(8,128)S(1)}, f32[3,34,64]{2,1,0:T(8,128)}, u32[]{:S(2)}) %copy-start.5) | copy-done | bytes 26136
  17.3 0.0 copy-start.6
  17.3 0.8 %copy-done.6 = f32[3,34,64]{2,1,0:T(8,128)S(1)} copy-done((f32[3,34,64]{2,1,0:T(8,128)S(1)}, f32[3,34,64]{2,1,0:T(8,128)}, u32[]{:S(2)}) %copy-start.6) | copy-done | bytes 26136
  18.1 0.0 copy-start.7
  18.1 0.8 %copy-done.7 = f32[3,33,64]{2,1,0:T(8,128)S(1)} copy-done((f32[3,33,64]{2,1,0:T(8,128)S(1)}, f32[3,33,64]{2,1,0:T(8,128)}, u32[]{:S(2)}) %copy-start.7) | copy-done | bytes 25368
  18.9 0.1 shard_map.74.own
  19.0 0.1 collective-permute-start.5
  19.2 1.5 %collective-permute-start.4 = (f32[224,128]{1,0:T(8,128)S(1)}, f32[224,128]{1,0:T(8,128)S(1)}, u32[]{:S(2)}, u32[]{:S(2)}) collective-permute-start(f32[224,128]{1,0:T(8,128)S(1)} %shard_map.74.own), channel_id=1, source_target_pairs={{0,2},{1,3},{2,0},{3,1},{4,6},{5,7},{6,4},{7,5},{8,10},{9,11},{10,... | collective-permute-start | bytes 344072 | tf_op jit(solution)/shard_map/ppermute | solution.py:43
  20.7 0.3 collective-permute-start.3
  21.0 0.0 copy-done.3
  21.0 0.5 %shard_map.76.turn = f32[2,2,3,34,8,128]{5,4,3,2,1,0:T(8,128)S(1)} custom-call(s32[2,3,136,128]{3,2,1,0:T(8,128)S(1)} %bitcast.24), custom_call_target="tpu_custom_call" | custom-call | flops 1000000 | bytes 1000000 | tf_op jit(solution)/shard_map/pallas_call | solution.py:47
  21.5 3.0 %collective-permute-done.5.third = f32[224,128]{1,0:T(8,128)S(1)} collective-permute-done((f32[224,128]{1,0:T(8,128)S(1)}, f32[224,128]{1,0:T(8,128)S(1)}, u32[]{:S(2)}, u32[]{:S(2)}) %collective-permute-start.5) | collective-permute-done | bytes 114720 | tf_op jit(solution)/shard_map/ppermute | solution.py:43
  24.5 2.5 %collective-permute-done.4.second = f32[224,128]{1,0:T(8,128)S(1)} collective-permute-done((f32[224,128]{1,0:T(8,128)S(1)}, f32[224,128]{1,0:T(8,128)S(1)}, u32[]{:S(2)}, u32[]{:S(2)}) %collective-permute-start.4) | collective-permute-done | bytes 114720 | tf_op jit(solution)/shard_map/ppermute | solution.py:43
  27.0 0.0 collective-permute-done.3.first
  27.0 0.0 copy-done.2
  27.0 0.7 %shard_map.75 = (f32[4,3,34,8,128]{4,3,2,1,0:T(8,128)S(1)}, f32[3,3,34,8,128]{4,3,2,1,0:T(8,128)S(1)}) custom-call(f32[224,128]{1,0:T(8,128)S(1)} %shard_map.74.own, f32[224,128]{1,0:T(8,128)S(1)} %collective-permute-done.3.first, f32[224,128]{1,0:T(8,128)S(1)} %collective-permute-done.4.second, f32[224,128]{1,0:T(8,128)S(1)} %collective-permute-done.5.third, ...), custom_call_target="tpu_custom_call" | custom-call | flops 10000000 | bytes 10000000 | tf_op jit(solution)/shard_map/pallas_call | solution.py:47
  27.8 0.0 collective-permute-done.1.east_halo
  27.8 0.0 collective-permute-done.west_halo
  27.8 1.5 %shard_map.77 = (f32[2,34,8,128]{3,2,1,0:T(8,128)S(1)}, f32[2,34,8,128]{3,2,1,0:T(8,128)S(1)}) custom-call(f32[2,34,8,128]{3,2,1,0:T(8,128)S(1)} %get-tuple-element.13.col0, f32[2,34,8,128]{3,2,1,0:T(8,128)S(1)} %get-tuple-element.14.col1, f32[2,34,8,128]{3,2,1,0:T(8,128)S(1)} %get-tuple-element.15.col2, ...), custom_call_target="tpu_custom_call" | custom-call | flops 10000000 | bytes 10000000 | tf_op jit(solution)/shard_map/pallas_call | solution.py:47
  29.3 6.5 %collective-permute-start.7 = (f32[2,34,8,128]{3,2,1,0:T(8,128)S(1)}, f32[2,34,8,128]{3,2,1,0:T(8,128)S(1)}, u32[]{:S(2)}, u32[]{:S(2)}) collective-permute-start(f32[2,34,8,128]{3,2,1,0:T(8,128)S(1)} %get-tuple-element.19.col0), channel_id=1, source_target_pairs={{0,28},{4,0},{8,4},{12,8},{16,12},{20,16},{24,20},{28,24},{1,29},{... | collective-permute-start | bytes 835592 | tf_op jit(solution)/shard_map/ppermute | solution.py:38
  35.8 0.0 collective-permute-start.6
  35.8 0.8 %shard_map.78.col1 = f32[2,34,8,128]{3,2,1,0:T(8,128)S(1)} custom-call(f32[2,34,8,128]{3,2,1,0:T(8,128)S(1)} %get-tuple-element.13.col0, f32[2,34,8,128]{3,2,1,0:T(8,128)S(1)} %get-tuple-element.14.col1, f32[2,34,8,128]{3,2,1,0:T(8,128)S(1)} %get-tuple-element.15.col2, f32[4,3,34,8,128]{4,3,2,1,0:T(8,128)S(1)} %get-tuple-element.17.rates, ...), custom_call_target="tpu_custom_call" | custom-call | flops 10000000 | bytes 10000000 | tf_op jit(solution)/shard_map/pallas_call | solution.py:47
  36.6 5.3 %collective-permute-done.7.east_halo = f32[2,34,8,128]{3,2,1,0:T(8,128)S(1)} collective-permute-done((f32[2,34,8,128]{3,2,1,0:T(8,128)S(1)}, f32[2,34,8,128]{3,2,1,0:T(8,128)S(1)}, u32[]{:S(2)}, u32[]{:S(2)}) %collective-permute-start.7) | collective-permute-done | bytes 278560 | tf_op jit(solution)/shard_map/ppermute | solution.py:38
  42.0 4.9 %collective-permute-done.6.west_halo = f32[2,34,8,128]{3,2,1,0:T(8,128)S(1)} collective-permute-done((f32[2,34,8,128]{3,2,1,0:T(8,128)S(1)}, f32[2,34,8,128]{3,2,1,0:T(8,128)S(1)}, u32[]{:S(2)}, u32[]{:S(2)}) %collective-permute-start.6) | collective-permute-done | bytes 278560 | tf_op jit(solution)/shard_map/ppermute | solution.py:38
  46.9 1.6 %shard_map.79 = f32[2,3,34,8,128]{4,3,2,1,0:T(8,128)} custom-call(f32[2,34,8,128]{3,2,1,0:T(8,128)S(1)} %get-tuple-element.19.col0, f32[2,34,8,128]{3,2,1,0:T(8,128)S(1)} %shard_map.78.col1, f32[2,34,8,128]{3,2,1,0:T(8,128)S(1)} %get-tuple-element.20.col2, f32[2,34,8,128]{3,2,1,0:T(8,128)S(1)} %collective-permute-done.6.west_halo, ...), custom_call_target="tpu_custom_call" | custom-call | flops 10000000 | bytes 1000000 | tf_op jit(solution)/shard_map/pallas_call | solution.py:47
Async XLA Ops:
  0.0 1.1 %copy-start = (f32[2,4,3,34,256]{4,1,3,2,0:T(4,128)S(1)}, f32[2,4,3,34,256]{4,1,3,2,0:T(4,128)}, u32[]{:S(2)}) copy-start(f32[2,4,3,34,256]{4,1,3,2,0:T(4,128)} %param.7) | copy-start | bytes 2506756
  1.2 0.9 %copy-start.1 = (s32[2,3,34,256]{3,0,2,1:T(2,128)S(1)}, s32[2,3,34,256]{3,0,2,1:T(2,128)}, u32[]{:S(2)}) copy-start(s32[2,3,34,256]{3,0,2,1:T(2,128)} %param.9) | copy-start | bytes 626692
  2.1 0.8 %copy-start.4 = (f32[3,34,64]{2,1,0:T(8,128)S(1)}, f32[3,34,64]{2,1,0:T(8,128)}, u32[]{:S(2)}) copy-start(f32[3,34,64]{2,1,0:T(8,128)} %xf.3) | copy-start | bytes 78340
  2.9 18.1 %copy-start.3 = (s32[2,2,3,34,256]{4,1,3,2,0:T(2,128)S(1)}, s32[2,2,3,34,256]{4,1,3,2,0:T(2,128)}, u32[]{:S(2)}) copy-start(s32[2,2,3,34,256]{4,1,3,2,0:T(2,128)} %param.8) | copy-start | bytes 1253380
  2.9 24.1 %copy-start.2 = (s32[2,3,34,256]{3,0,2,1:T(2,128)S(1)}, s32[2,3,34,256]{3,0,2,1:T(2,128)}, u32[]{:S(2)}) copy-start(s32[2,3,34,256]{3,0,2,1:T(2,128)} %param.9) | copy-start | bytes 626692
  4.2 23.5 %collective-permute-start.1 = (f32[2,34,8,128]{3,2,1,0:T(8,128)S(1)}, f32[2,34,8,128]{3,2,1,0:T(8,128)S(1)}, u32[]{:S(2)}, u32[]{:S(2)}) collective-permute-start(f32[2,34,8,128]{3,2,1,0:T(8,128)S(1)} %get-tuple-element.13.col0), channel_id=1, source_target_pairs={{0,28},{4,0},{8,4},{12,8},{16,12},{20,16},{24,20},{28,24},{1,29},{... | collective-permute-start | bytes 835592 | tf_op jit(solution)/shard_map/ppermute | solution.py:38
  10.3 17.5 %collective-permute-start = (f32[2,34,8,128]{3,2,1,0:T(8,128)S(1)}, f32[2,34,8,128]{3,2,1,0:T(8,128)S(1)}, u32[]{:S(2)}, u32[]{:S(2)}) collective-permute-start(f32[2,34,8,128]{3,2,1,0:T(8,128)S(1)} %get-tuple-element.15.col2), channel_id=1, source_target_pairs={{0,4},{4,8},{8,12},{12,16},{16,20},{20,24},{24,28},{28,0},{1,5},{5... | collective-permute-start | bytes 835592 | tf_op jit(solution)/shard_map/ppermute | solution.py:38
  10.3 6.2 %collective-permute-start.2 = (f32[17,128]{1,0:T(8,128)S(1)}, f32[17,128]{1,0:T(8,128)S(1)}, u32[]{:S(2)}, u32[]{:S(2)}) collective-permute-start(f32[17,128]{1,0:T(8,128)S(1)} %get-tuple-element.16), channel_id=1, source_target_pairs={{0,28},{4,0},{8,4},{12,8},{16,12},{20,16},{24,20},{28,24},{1,29},{... | collective-permute-start | bytes 26120 | tf_op jit(solution)/shard_map/ppermute | solution.py:38
  16.4 0.8 %copy-start.5 = (f32[3,34,64]{2,1,0:T(8,128)S(1)}, f32[3,34,64]{2,1,0:T(8,128)}, u32[]{:S(2)}) copy-start(f32[3,34,64]{2,1,0:T(8,128)} %mass.1) | copy-start | bytes 78340
  17.3 0.8 %copy-start.6 = (f32[3,34,64]{2,1,0:T(8,128)S(1)}, f32[3,34,64]{2,1,0:T(8,128)}, u32[]{:S(2)}) copy-start(f32[3,34,64]{2,1,0:T(8,128)} %yf.1) | copy-start | bytes 78340
  18.1 0.8 %copy-start.7 = (f32[3,33,64]{2,1,0:T(8,128)S(1)}, f32[3,33,64]{2,1,0:T(8,128)}, u32[]{:S(2)}) copy-start(f32[3,33,64]{2,1,0:T(8,128)} %km.1) | copy-start | bytes 76036
  19.0 5.5 %collective-permute-start.5 = (f32[224,128]{1,0:T(8,128)S(1)}, f32[224,128]{1,0:T(8,128)S(1)}, u32[]{:S(2)}, u32[]{:S(2)}) collective-permute-start(f32[224,128]{1,0:T(8,128)S(1)} %shard_map.74.own), channel_id=1, source_target_pairs={{0,3},{1,2},{2,1},{3,0},{4,7},{5,6},{6,5},{7,4},{8,11},{9,10},{10,... | collective-permute-start | bytes 344072 | tf_op jit(solution)/shard_map/ppermute | solution.py:43
  19.2 7.8 %collective-permute-start.4 = (f32[224,128]{1,0:T(8,128)S(1)}, f32[224,128]{1,0:T(8,128)S(1)}, u32[]{:S(2)}, u32[]{:S(2)}) collective-permute-start(f32[224,128]{1,0:T(8,128)S(1)} %shard_map.74.own), channel_id=1, source_target_pairs={{0,2},{1,3},{2,0},{3,1},{4,6},{5,7},{6,4},{7,5},{8,10},{9,11},{10,... | collective-permute-start | bytes 344072 | tf_op jit(solution)/shard_map/ppermute | solution.py:43
  20.7 6.3 %collective-permute-start.3 = (f32[224,128]{1,0:T(8,128)S(1)}, f32[224,128]{1,0:T(8,128)S(1)}, u32[]{:S(2)}, u32[]{:S(2)}) collective-permute-start(f32[224,128]{1,0:T(8,128)S(1)} %shard_map.74.own), channel_id=1, source_target_pairs={{0,1},{1,0},{2,3},{3,2},{4,5},{5,4},{6,7},{7,6},{8,9},{9,8},{10,11... | collective-permute-start | bytes 344072 | tf_op jit(solution)/shard_map/ppermute | solution.py:43
  29.3 12.7 %collective-permute-start.7 = (f32[2,34,8,128]{3,2,1,0:T(8,128)S(1)}, f32[2,34,8,128]{3,2,1,0:T(8,128)S(1)}, u32[]{:S(2)}, u32[]{:S(2)}) collective-permute-start(f32[2,34,8,128]{3,2,1,0:T(8,128)S(1)} %get-tuple-element.19.col0), channel_id=1, source_target_pairs={{0,28},{4,0},{8,4},{12,8},{16,12},{20,16},{24,20},{28,24},{1,29},{... | collective-permute-start | bytes 835592 | tf_op jit(solution)/shard_map/ppermute | solution.py:38
  35.8 11.0 %collective-permute-start.6 = (f32[2,34,8,128]{3,2,1,0:T(8,128)S(1)}, f32[2,34,8,128]{3,2,1,0:T(8,128)S(1)}, u32[]{:S(2)}, u32[]{:S(2)}) collective-permute-start(f32[2,34,8,128]{3,2,1,0:T(8,128)S(1)} %get-tuple-element.20.col2), channel_id=1, source_target_pairs={{0,4},{4,8},{8,12},{12,16},{16,20},{20,24},{24,28},{28,0},{1,5},{5... | collective-permute-start | bytes 835592 | tf_op jit(solution)/shard_map/ppermute | solution.py:38

commit v2 on v1

v2 whole, which is shorter than its diff:
```python
import jax
import jax.numpy as jnp
from jax import lax
from jax.experimental import pallas as pl
from jax.experimental.pallas import tpu as pltpu
from jax.sharding import PartitionSpec as P

LANES = 128
MOMENTS = 4
VMEM = pl.BlockSpec(memory_space=pltpu.VMEM)
SMEM = pl.BlockSpec(memory_space=pltpu.SMEM)
HBM = pl.BlockSpec(memory_space=pltpu.HBM)


def state_view(x):
    t, m, c, l, n = x.shape
    b = n // LANES
    x = x.reshape(t, m, c, l, b, LANES).transpose(0, 2, 3, 4, 1, 5)
    return x.reshape(t, c, l, b * m, LANES)


def pair_view(x):
    t, d, c, l, n = x.shape
    b = n // LANES
    x = x.reshape(t, d, c, l, b, LANES).transpose(0, 2, 3, 4, 1, 5)
    return x.reshape(t, c, l * b * d, LANES)


def state_back(y):
    t, c, l, rows, _ = y.shape
    b = rows // MOMENTS
    y = y.reshape(t, c, l, b, MOMENTS, LANES).transpose(0, 4, 1, 2, 3, 5)
    return y.reshape(t, MOMENTS, c, l, b * LANES)


def shifted(value, axis, by):
    count = lax.axis_size(axis)
    return lax.ppermute(value, axis, [(i, (i + by) % count) for i in range(count)])


def swapped(value, axis, mask):
    count = lax.axis_size(axis)
    return lax.ppermute(value, axis, [(i, i ^ mask) for i in range(count)])


def call(kernel, out, in_specs, scratch, flops, moved, *args, out_specs=None, aliases=None):
    return pl.pallas_call(
        kernel,
        out_shape=out,
        in_specs=in_specs,
        out_specs=jax.tree.map(lambda _: VMEM, out) if out_specs is None else out_specs,
        scratch_shapes=scratch,
        input_output_aliases=aliases or {},
        compiler_params=pltpu.CompilerParams(vmem_limit_bytes=24 * 1024 * 1024),
        cost_estimate=pl.CostEstimate(flops=flops, bytes_accessed=moved, transcendentals=0),
    )(*args)


def stay(x):
    return pltpu.with_memory_space_constraint(x, pltpu.HBM)


def f32(*shape):
    return jax.ShapeDtypeStruct(shape, jnp.float32)


def tile_masks(slope):
    row = lax.broadcasted_iota(jnp.int32, (8, LANES), 0) % MOMENTS
    return row == 0, row == slope


def head_kernel(state, flags, mass, xf, yf, km, message, col1, col2, packed, flags_v, mass_v, xf_v, yf_v, km_v, sems, column_sems):
    tracers, columns, levels = state.shape[0], mass.shape[0], mass.shape[1]
    half = LANES // 2
    pairs = ((mass, mass_v), (xf, xf_v), (yf, yf_v), (km, km_v), (flags, flags_v))
    copies = [pltpu.make_async_copy(src, dst, sems.at[i]) for i, (src, dst) in enumerate(pairs)]
    for t in range(tracers):
        for c, place in ((2, col2.at[t]), (0, message.at[pl.ds(t * levels, levels)]), (1, col1.at[t])):
            copies.append(pltpu.make_async_copy(state.at[t, c], place, column_sems.at[c, t]))
    for copy in copies:
        copy.start()
    for copy in copies[:4]:
        copy.wait()
    for c in range(columns):
        low, top = c * levels, (columns + c) * levels
        packed[low : low + levels, :half] = mass_v[c]
        packed[low : low + levels, half:] = xf_v[c]
        packed[top : top + levels, :half] = yf_v[c]
        packed[top : top + levels - 1, half:] = km_v[c]
        packed[top + levels - 1 : top + levels, half:] = jnp.zeros((1, half), jnp.float32)
    for copy in copies[4:]:
        copy.wait()


def spread(upper_block, ref, *where):
    blocks = [jnp.broadcast_to(ref[(*index, pl.ds(r, 1), slice(None))], (8, LANES)) for index, r in where]
    return jnp.where(upper_block, blocks[1], blocks[0])


def face_row(rows, levels, b):
    return rows - -(-2 * levels // 8) * 8 + b * levels


def turn_kernel(switches, turn):
    tracers, columns = switches.shape[:2]
    levels = switches.shape[2] // 4
    row = lax.broadcasted_iota(jnp.int32, (8, LANES), 0)
    moment = row % MOMENTS
    for t in range(tracers):
        for c in range(columns):
            for l in range(levels):
                for d in range(2):
                    base = l * 4 + d
                    sw = spread(row >= MOMENTS, switches, ((t, c), base), ((t, c), base + 2))
                    take = jnp.where(sw == 1, 1.0, jnp.where(sw == 2, -1.0, 0.0))
                    keep = jnp.where(sw == 0, 1.0, 0.0)
                    turn[d, t, c, l] = jnp.where(moment == 0, take, jnp.where(moment == 1 + d, keep, 1.0))


def pre_kernel(own, first, second, third, flags, order, begun, before, also, rates, factors, message, fields):
    columns, levels = rates.shape[1], rates.shape[2]
    half = LANES // 2
    odd = order[0] % 2 == 1
    high = order[0] >= 2
    lane = lax.broadcasted_iota(jnp.int32, (8, LANES), 1)
    row = lax.broadcasted_iota(jnp.int32, (8, LANES), 0)
    upper_block = row >= MOMENTS
    lane_low = lax.broadcasted_iota(jnp.int32, (levels, LANES), 1) < half

    def sorted_shards(start, count):
        a, b, c, d = (ref[start : start + count] for ref in (own, first, second, third))
        a, b, c, d = (jnp.where(odd, b, a), jnp.where(odd, a, b), jnp.where(odd, d, c), jnp.where(odd, c, d))
        return (jnp.where(high, c, a), jnp.where(high, d, b), jnp.where(high, a, c), jnp.where(high, b, d))

    for pair in range(2):
        for c in range(columns):
            shards = sorted_shards((pair * columns + c) * levels, levels)
            for b in range(2):
                lo, hi = shards[2 * b], shards[2 * b + 1]
                fields[2 * pair, c, b] = jnp.where(lane_low, lo, pltpu.roll(hi, half, 1))
                flux = jnp.where(lane_low, pltpu.roll(lo, half, 1), hi)
                fields[2 * pair + 1, c, b] = flux
                if pair == 0 and c == 0:
                    eastward = flags[0, pl.ds(2 * b, levels, stride=4), :].astype(jnp.float32)
                    start = face_row(message.shape[0], levels, b)
                    message[start : start + levels] = (2.0 * eastward - 1.0) * flux

    def field(f, c, l):
        return spread(upper_block, fields, ((f, c, 0), l), ((f, c, 1), l))

    def flag(c, l, d):
        base = l * 4 + d
        return spread(upper_block, flags, ((c,), base), ((c,), base + 2)).astype(jnp.float32)

    first_row = (lane == 0) & (row < MOMENTS)
    last_row = (lane == LANES - 1) & (row >= MOMENTS)
    for l in range(levels):
        flux_x = [field(1, c, l) for c in range(columns)]
        flag_x = [flag(c, l, 0) for c in range(columns)]
        east = [flag_x[c] * flux_x[c] for c in range(columns)]
        west = [flux_x[c] - east[c] for c in range(columns)]
        east.append(1.0)
        for c in range(columns):
            share = 1.0 / field(0, c, l)
            rates[0, c, l] = east[c + 1] * share
            rates[1, c, l] = west[c] * share
            flux_y = field(2, c, l)
            north = flag(c, l, 1) * flux_y
            south = pltpu.roll(flux_y - north, 1, 1)
            south = jnp.where(lane == 0, pltpu.roll(south, 4, 0), south)
            rates[2, c, l] = jnp.where(last_row, 0.0, north) * share
            rates[3, c, l] = jnp.where(first_row, 0.0, south) * share

    fixed = row % MOMENTS == 3
    zero = jnp.zeros((8, LANES), jnp.float32)
    below, upper = [None] * columns, [None] * columns
    for l in range(levels):
        for c in range(columns):
            diagonal = zero + 1.0
            if l > 0:
                diagonal = diagonal + below[c]
            if l < levels - 1:
                above = field(3, c, l)
                diagonal = diagonal + above
            if l > 0:
                diagonal = diagonal + below[c] * upper[c]
            inverse = 1.0 / diagonal
            factors[0, c, l] = jnp.where(fixed, 1.0, inverse)
            factors[2, c, l] = jnp.where(fixed, 0.0, below[c] * inverse) if l > 0 else zero
            if l < levels - 1:
                upper[c] = -above * inverse
                factors[1, c, l] = jnp.where(fixed, 0.0, upper[c])
                below[c] = above
            else:
                factors[1, c, l] = zero


def advect(own, east_side, west_side, east, west, turns, slope, masks):
    is_mass, is_slope = masks
    stay = 1.0 - (east + west)
    east_part = east * jnp.where(is_slope, east, 1.0)
    west_part = west * jnp.where(is_slope, west, 1.0)
    east_cross = east * (1.0 - east)
    west_cross = west * (1.0 - west)
    out = []
    for s, e, w, z in zip(own, east_side, west_side, turns):
        total = stay * s + east_part * e + west_part * w
        cross = east_cross * (e - s) - west_cross * (w - s)
        total = total + jnp.where(is_slope, pltpu.roll(cross, slope, 0), 0.0)
        slope_up = pltpu.roll(total, 8 - slope, 0)
        out.append(z * jnp.where(is_mass, slope_up, total) + jnp.where(is_mass, total, 0.0))
    return out


def middle(todo, own, east_side, west_side, east_rate, rates, factors, turn, out):
    tracers, levels = out.shape[0], out.shape[1]
    lane = lax.broadcasted_iota(jnp.int32, (8, LANES), 1)
    at_first, at_last = lane == 0, lane == LANES - 1
    x_masks, y_masks = tile_masks(1), tile_masks(2)
    every = range(tracers)
    c = todo

    def prev(v):
        r = pltpu.roll(v, 1, 1)
        return jnp.where(at_first, pltpu.roll(r, 4, 0), r)

    def following(v):
        r = pltpu.roll(v, LANES - 1, 1)
        return jnp.where(at_last, pltpu.roll(r, 4, 0), r)

    def y_step(values, l):
        return advect(values, [following(v) for v in values], [prev(v) for v in values],
                      rates[2, c, l], rates[3, c, l], [turn[1, t, c, l] for t in every], 2, y_masks)

    carried = [None] * tracers
    for l in range(levels):
        sides = [[side(t, l) for t in every] for side in (own, east_side, west_side)]
        values = advect(*sides, east_rate(l), rates[1, c, l], [turn[0, t, c, l] for t in every], 1, x_masks)
        values = y_step(values, l)
        for t in every:
            v = values[t] * factors[0, c, l]
            if l > 0:
                v = v + factors[2, c, l] * carried[t]
            carried[t] = v
            out[t, l] = v
    for l in range(levels - 1, -1, -1):
        if l < levels - 1:
            for t in every:
                carried[t] = out[t, l] - factors[1, c, l] * carried[t]
        values = y_step(carried, l)
        for t in every:
            out[t, l] = values[t]


def tiles(ref, levels):
    if len(ref.shape) == 4:
        return lambda t, l: ref[t, l]
    return lambda t, l: ref[(t * levels + l) * 8 : (t * levels + l + 1) * 8]


def west_kernel(message, col1, west_halo, rates, factors, turn, out):
    levels = out.shape[1]
    middle(0, tiles(message, levels), tiles(col1, levels), tiles(west_halo, levels),
           lambda l: rates[0, 0, l], rates, factors, turn, out)


def inner_kernel(message, col1, col2, rates, factors, turn, out):
    levels = out.shape[1]
    middle(1, tiles(col1, levels), tiles(col2, levels), tiles(message, levels),
           lambda l: rates[0, 1, l], rates, factors, turn, out)


def east_kernel(col1, col2, halo, rates, factors, turn, before, out, east):
    levels = out.shape[1]
    upper_block = lax.broadcasted_iota(jnp.int32, (8, LANES), 0) >= MOMENTS
    rows = [face_row(halo.shape[0], levels, b) for b in range(2)]

    def east_rate(l):
        flux = spread(upper_block, halo, ((), rows[0] + l), ((), rows[1] + l))
        east[l] = jnp.maximum(flux, 0.0) * rates[0, 2, l]
        return east[l]

    middle(2, tiles(col2, levels), tiles(halo, levels), tiles(col1, levels), east_rate, rates, factors, turn, out)


def finish(c, own, east_side, west_side, east_rate, rates, turn, out, buf, sems):
    tracers, levels = buf.shape[0], buf.shape[1]
    masks = tile_masks(1)
    every = range(tracers)
    copies = []
    for part in range(2):
        low, high = part * levels // 2, (part + 1) * levels // 2
        for l in range(low, high):
            values = advect(*([side[t, l] for t in every] for side in (own, east_side, west_side)),
                            east_rate(l), rates[1, c, l], [turn[0, t, c, l] for t in every], 1, masks)
            for t in every:
                buf[t, l] = values[t]
        for t in every:
            span = pl.ds(low, high - low)
            copies.append(pltpu.make_async_copy(buf.at[t, span], out.at[t, c, span], sems.at[part, t]))
            copies[-1].start()
    for copy in copies:
        copy.wait()


def last_inner_kernel(mid0, mid1, mid2, rates, turn, out, buf, sems):
    finish(1, mid1, mid2, mid0, lambda l: rates[0, 1, l], rates, turn, out, buf, sems)


def last_east_kernel(begun, mid1, mid2, halo, east, rates, turn, out, buf, sems):
    finish(2, mid2, halo, mid1, lambda l: east[l], rates, turn, out, buf, sems)


def last_west_kernel(begun, mid0, mid1, halo, rates, turn, out, buf, sems):
    finish(0, mid0, mid1, halo, lambda l: rates[0, 0, l], rates, turn, out, buf, sems)


def body(state_adjoint, switches, flags, air_mass, x_flux, y_flux, vertical_mixing):
    state = state_view(state_adjoint)
    switch = pair_view(switches)
    flag = pair_view(flags[None])[0]
    tracers, columns, levels = state.shape[:3]
    order = lax.axis_index("trc").astype(jnp.int32).reshape(1)
    column = f32(tracers, levels, 8, LANES)
    rows = -(-2 * columns * levels // 8) * 8
    length = tracers * levels + -(-2 * levels // 8)
    dma = pltpu.SemaphoreType.DMA
    fields = tuple(stay(x) for x in (air_mass, x_flux, y_flux, vertical_mixing))

    message, col1, col2, packed, flag = call(
        head_kernel,
        (f32(length, 8, LANES), column, column, f32(rows, LANES), jax.ShapeDtypeStruct(flag.shape, flag.dtype)),
        (HBM,) * 6, [pltpu.VMEM(x.shape, x.dtype) for x in fields] + [dma((5,)), dma((columns, tracers))],
        10**5, 10**6, stay(state), stay(flag), *fields)
    west_halo = shifted(col2, "lon", 1)
    others = [swapped(packed, "trc", mask) for mask in (1, 2, 3)]
    turn = call(turn_kernel, f32(2, tracers, columns, levels, 8, LANES), (VMEM,), (), 10**6, 10**6, switch)
    rates, factors, message = call(
        pre_kernel,
        (f32(4, columns, levels, 8, LANES), f32(3, columns, levels, 8, LANES), f32(length * 8, LANES)),
        (VMEM,) * 5 + (SMEM, VMEM, VMEM, VMEM), [pltpu.VMEM((4, columns, 2, levels, LANES), jnp.float32)],
        10**6, 10**6, packed, *others, flag, order, message.reshape(length * 8, LANES), west_halo, turn, aliases={6: 2})
    east_message = shifted(message, "lon", -1)
    mid0 = call(west_kernel, column, (VMEM,) * 6, (), 10**6, 10**6, message, col1, west_halo, rates, factors, turn)
    east_halo = shifted(mid0, "lon", -1)
    mid1 = call(inner_kernel, column, (VMEM,) * 6, (), 10**6, 10**6, message, col1, col2, rates, factors, turn)
    mid2, east = call(east_kernel, (column, f32(levels, 8, LANES)), (VMEM,) * 7, (), 10**6, 10**6,
                      col1, col2, east_message, rates, factors, turn, mid0)
    west_halo = shifted(mid2, "lon", 1)

    def last(kernel, aliases, *args):
        first = (HBM,) * len(aliases)
        return call(kernel, f32(*state.shape), first + (VMEM,) * (len(args) - len(first)),
                    [pltpu.VMEM(column.shape, jnp.float32), dma((2, tracers))], 10**6, 10**6,
                    *args, out_specs=HBM, aliases=aliases)

    out = last(last_inner_kernel, {}, mid0, mid1, mid2, rates, turn)
    out = last(last_east_kernel, {0: 0}, out, mid1, mid2, east_halo, east, rates, turn)
    out = last(last_west_kernel, {0: 0}, out, mid0, mid1, west_halo, rates, turn)
    return state_back(out)


def solution(mesh):
    placed = (
        P("trc", None, "lon", None, None),
        P("trc", None, "lon", None, None),
        P(None, "lon", None, None),
        P("lon", None, "trc"),
        P("lon", None, "trc"),
        P("lon", None, "trc"),
        P("lon", None, "trc"),
    )
    return jax.shard_map(
        body,
        mesh=mesh,
        in_specs=placed,
        out_specs=P("trc", None, "lon", None, None),
        check_vma=False,
    )
```

time: 48.8 us -> 36.6 us (0.75)
  starting transfers between devices: 19.2 us -> 8.19 us
  local copies, waits for them, and re-layouts: 5.4 us -> 1 us
  waiting for transfers between devices: 17.3 us -> 19.4 us
  Pallas kernels: 6.47 us -> 7.76 us
    ppermute x5 -> x4, starting transfers between devices: 17.3 us -> 6.33 us  [shifted(): lax.ppermute(value, axis, [(i, (i + by) % count) for i in range(count)])]
    unnamed x16 -> x2, local copies, waits for them, and re-layouts: 5.4 us -> 1 us
    ppermute x5 -> x4, waiting for transfers between devices: 11.7 us -> 15.5 us  [shifted(): lax.ppermute(value, axis, [(i, (i + by) % count) for i in range(count)])]
    ppermute x3, waiting for transfers between devices: 5.55 us -> 3.91 us  [swapped(): return lax.ppermute(value, axis, [(i, i ^ mask) for i in range(count)])]
    pallas_call x7 -> x9, Pallas kernels: 6.47 us -> 7.76 us  [call(): pl.pallas_call(kernel, out_shape=out, in_specs=in_specs, out_specs=jax.tr...]
  transfers between devices with their start and end apart: 8 -> 7, of which waited for: 5 -> 6; matrix products, arithmetic and copies ran while one was open for 0% -> 0% of each run, Pallas kernels for 4% -> 13%
where the time goes in v2:
time: 36.6 us; the launch traced here: 36.4 us
  waiting for transfers between devices  19.4 us (53%)
  starting transfers between devices  8.19 us (22%)
  Pallas kernels  7.76 us (21%)
  local copies, waits for them, and re-layouts  1 us (3%)
    ppermute x4, waiting for transfers between devices, shifted(): lax.ppermute(value, axis, [(i, (i + by) % count) for i in range(count)])  15.5 us
    pallas_call x9, Pallas kernels, call(): pl.pallas_call(kernel, out_shape=out, in_specs=in_specs, out_specs=jax.tr...  7.76 us
    ppermute x4, starting transfers between devices, shifted(): lax.ppermute(value, axis, [(i, (i + by) % count) for i in range(count)])  6.33 us
    ppermute x3, waiting for transfers between devices, swapped(): return lax.ppermute(value, axis, [(i, i ^ mask) for i in range(count)])  3.91 us
    ppermute x3, starting transfers between devices, swapped(): return lax.ppermute(value, axis, [(i, i ^ mask) for i in range(count)])  1.86 us
    unnamed x2, local copies, waits for them, and re-layouts  1 us
  transfers between devices with their start and end apart: 7, of which 6 were waited for; matrix products, arithmetic and copies ran while one was open for 0% of the time, Pallas kernels for 13%

profile of v2, /device:TPU:0, one launch (start us, length us, event | category | flops | bytes accessed | tf_op | source)
XLA Modules:
  0.0 36.4 jit_solution(11166616853134856362)
XLA Ops:
  0.0 1.5 %shard_map.73 = (f32[77,8,128]{2,1,0:T(8,128)S(1)}, f32[2,34,8,128]{3,2,1,0:T(8,128)S(1)}, f32[2,34,8,128]{3,2,1,0:T(8,128)S(1)}, f32[208,128]{1,0:T(8,128)S(1)}, s32[3,136,128]{2,1,0:T(8,128)S(1)}) custom-call(f32[2,3,34,8,128]{4,3,2,1,0:T(8,128)} %bitcast.24, s32[3,136,128]{2,1,0:T(8,128)} %bitcast.25, f32[3,34,64]{2,1,0:T(8,128)} %mass.1, ...), custom_call_target="tpu_custom_call" | custom-call | flops 100000 | bytes 1000000 | tf_op jit(solution)/shard_map/pallas_call | solution.py:47
  1.5 3.0 %collective-permute-start.3 = (f32[2,34,8,128]{3,2,1,0:T(8,128)S(1)}, f32[2,34,8,128]{3,2,1,0:T(8,128)S(1)}, u32[]{:S(2)}, u32[]{:S(2)}) collective-permute-start(f32[2,34,8,128]{3,2,1,0:T(8,128)S(1)} %get-tuple-element.18.col2), channel_id=1, source_target_pairs={{0,4},{4,8},{8,12},{12,16},{16,20},{20,24},{24,28},{28,0},{1,5},{5... | collective-permute-start | bytes 835592 | tf_op jit(solution)/shard_map/ppermute | solution.py:38
  4.5 0.0 collective-permute-start
  4.5 1.5 %collective-permute-start.1 = (f32[208,128]{1,0:T(8,128)S(1)}, f32[208,128]{1,0:T(8,128)S(1)}, u32[]{:S(2)}, u32[]{:S(2)}) collective-permute-start(f32[208,128]{1,0:T(8,128)S(1)} %get-tuple-element.15.own), channel_id=1, source_target_pairs={{0,2},{1,3},{2,0},{3,1},{4,6},{5,7},{6,4},{7,5},{8,10},{9,11},{10,... | collective-permute-start | bytes 319496 | tf_op jit(solution)/shard_map/ppermute | solution.py:43
  6.0 0.4 %collective-permute-start.2 = (f32[208,128]{1,0:T(8,128)S(1)}, f32[208,128]{1,0:T(8,128)S(1)}, u32[]{:S(2)}, u32[]{:S(2)}) collective-permute-start(f32[208,128]{1,0:T(8,128)S(1)} %get-tuple-element.15.own), channel_id=1, source_target_pairs={{0,3},{1,2},{2,1},{3,0},{4,7},{5,6},{6,5},{7,4},{8,11},{9,10},{10,... | collective-permute-start | bytes 319496 | tf_op jit(solution)/shard_map/ppermute | solution.py:43
  6.3 0.0 copy-start
  6.3 1.0 %copy-done = s32[2,2,3,34,256]{4,1,3,2,0:T(2,128)S(1)} copy-done((s32[2,2,3,34,256]{4,1,3,2,0:T(2,128)S(1)}, s32[2,2,3,34,256]{4,1,3,2,0:T(2,128)}, u32[]{:S(2)}) %copy-start) | copy-done | bytes 417816
  7.3 0.5 %shard_map.74.also.turn = f32[2,2,3,34,8,128]{5,4,3,2,1,0:T(8,128)S(1)} custom-call(s32[2,3,136,128]{3,2,1,0:T(8,128)S(1)} %bitcast.23), custom_call_target="tpu_custom_call" | custom-call | flops 1000000 | bytes 1000000 | tf_op jit(solution)/shard_map/pallas_call | solution.py:47
  7.8 0.0 collective-permute-done.first
  7.8 2.4 %collective-permute-done.1.second = f32[208,128]{1,0:T(8,128)S(1)} collective-permute-done((f32[208,128]{1,0:T(8,128)S(1)}, f32[208,128]{1,0:T(8,128)S(1)}, u32[]{:S(2)}, u32[]{:S(2)}) %collective-permute-start.1) | collective-permute-done | bytes 106528 | tf_op jit(solution)/shard_map/ppermute | solution.py:43
  10.3 1.5 %collective-permute-done.2.third = f32[208,128]{1,0:T(8,128)S(1)} collective-permute-done((f32[208,128]{1,0:T(8,128)S(1)}, f32[208,128]{1,0:T(8,128)S(1)}, u32[]{:S(2)}, u32[]{:S(2)}) %collective-permute-start.2) | collective-permute-done | bytes 106528 | tf_op jit(solution)/shard_map/ppermute | solution.py:43
  11.8 2.4 %collective-permute-done.3.before.west_halo = f32[2,34,8,128]{3,2,1,0:T(8,128)S(1)} collective-permute-done((f32[2,34,8,128]{3,2,1,0:T(8,128)S(1)}, f32[2,34,8,128]{3,2,1,0:T(8,128)S(1)}, u32[]{:S(2)}, u32[]{:S(2)}) %collective-permute-start.3) | collective-permute-done | bytes 278560 | tf_op jit(solution)/shard_map/ppermute | solution.py:38
  14.2 0.7 %shard_map.75 = (f32[4,3,34,8,128]{4,3,2,1,0:T(8,128)S(1)}, f32[3,3,34,8,128]{4,3,2,1,0:T(8,128)S(1)}, f32[616,128]{1,0:T(8,128)S(1)}) custom-call(f32[208,128]{1,0:T(8,128)S(1)} %get-tuple-element.15.own, f32[208,128]{1,0:T(8,128)S(1)} %collective-permute-done.first, f32[208,128]{1,0:T(8,128)S(1)} %collective-permute-done.1.second, ...), custom_call_target="tpu_custom_call", output_to_operand_aliasing={{2}: (6, {})} | custom-call | flops 1000000 | bytes 1000000 | tf_op jit(solution)/shard_map/pallas_call | solution.py:47
  14.9 1.8 %collective-permute-start.4 = (f32[616,128]{1,0:T(8,128)S(1)}, f32[616,128]{1,0:T(8,128)S(1)}, u32[]{:S(2)}, u32[]{:S(2)}) collective-permute-start(f32[616,128]{1,0:T(8,128)S(1)} %get-tuple-element.19.message), channel_id=1, source_target_pairs={{0,28},{4,0},{8,4},{12,8},{16,12},{20,16},{24,20},{28,24},{1,29},{... | collective-permute-start | bytes 946184 | tf_op jit(solution)/shard_map/ppermute | solution.py:38
  16.7 0.8 %shard_map.76.before.mid0 = f32[2,34,8,128]{3,2,1,0:T(8,128)S(1)} custom-call(f32[616,128]{1,0:T(8,128)S(1)} %get-tuple-element.19.message, f32[2,34,8,128]{3,2,1,0:T(8,128)S(1)} %get-tuple-element.20.col1, f32[2,34,8,128]{3,2,1,0:T(8,128)S(1)} %collective-permute-done.3.before.west_halo, f32[4,3,34,8,128]{4,3,2,1,0:T(8,128)S(1)} %get-tuple-element.21.rates, ...), custom_call_target="tpu_custom_call" | custom-call | flops 1000000 | bytes 1000000 | tf_op jit(solution)/shard_map/pallas_call | solution.py:47
  17.5 1.5 %collective-permute-start.5 = (f32[2,34,8,128]{3,2,1,0:T(8,128)S(1)}, f32[2,34,8,128]{3,2,1,0:T(8,128)S(1)}, u32[]{:S(2)}, u32[]{:S(2)}) collective-permute-start(f32[2,34,8,128]{3,2,1,0:T(8,128)S(1)} %shard_map.76.before.mid0), channel_id=1, source_target_pairs={{0,28},{4,0},{8,4},{12,8},{16,12},{20,16},{24,20},{28,24},{1,29},{... | collective-permute-start | bytes 835592 | tf_op jit(solution)/shard_map/ppermute | solution.py:38
  18.9 6.4 %collective-permute-done.4.halo = f32[616,128]{1,0:T(8,128)S(1)} collective-permute-done((f32[616,128]{1,0:T(8,128)S(1)}, f32[616,128]{1,0:T(8,128)S(1)}, u32[]{:S(2)}, u32[]{:S(2)}) %collective-permute-start.4) | collective-permute-done | bytes 315424 | tf_op jit(solution)/shard_map/ppermute | solution.py:38
  25.3 0.8 %shard_map.78 = (f32[2,34,8,128]{3,2,1,0:T(8,128)S(1)}, f32[34,8,128]{2,1,0:T(8,128)S(1)}) custom-call(f32[2,34,8,128]{3,2,1,0:T(8,128)S(1)} %get-tuple-element.20.col1, f32[2,34,8,128]{3,2,1,0:T(8,128)S(1)} %get-tuple-element.18.col2, f32[616,128]{1,0:T(8,128)S(1)} %collective-permute-done.4.halo, f32[4,3,34,8,128]{4,3,2,1,0:T(8,128)S(1)} %get-tuple-element.21.rates, ...), custom_call_target="tpu_custom_call" | custom-call | flops 1000000 | bytes 1000000 | tf_op jit(solution)/shard_map/pallas_call | solution.py:47
  26.1 0.1 collective-permute-start.6
  26.2 0.8 %shard_map.77.mid1 = f32[2,34,8,128]{3,2,1,0:T(8,128)S(1)} custom-call(f32[616,128]{1,0:T(8,128)S(1)} %get-tuple-element.19.message, f32[2,34,8,128]{3,2,1,0:T(8,128)S(1)} %get-tuple-element.20.col1, f32[2,34,8,128]{3,2,1,0:T(8,128)S(1)} %get-tuple-element.18.col2, f32[4,3,34,8,128]{4,3,2,1,0:T(8,128)S(1)} %get-tuple-element.21.rates, ...), custom_call_target="tpu_custom_call" | custom-call | flops 1000000 | bytes 1000000 | tf_op jit(solution)/shard_map/pallas_call | solution.py:47
  27.0 0.9 %shard_map.79.begun = f32[2,3,34,8,128]{4,3,2,1,0:T(8,128)} custom-call(f32[2,34,8,128]{3,2,1,0:T(8,128)S(1)} %shard_map.76.before.mid0, f32[2,34,8,128]{3,2,1,0:T(8,128)S(1)} %shard_map.77.mid1, f32[2,34,8,128]{3,2,1,0:T(8,128)S(1)} %get-tuple-element.23.mid2, f32[4,3,34,8,128]{4,3,2,1,0:T(8,128)S(1)} %get-tuple-element.21.rates, ...), custom_call_target="tpu_custom_call" | custom-call | flops 1000000 | bytes 1000000 | tf_op jit(solution)/shard_map/pallas_call | solution.py:47
  27.9 4.6 %collective-permute-done.5.halo = f32[2,34,8,128]{3,2,1,0:T(8,128)S(1)} collective-permute-done((f32[2,34,8,128]{3,2,1,0:T(8,128)S(1)}, f32[2,34,8,128]{3,2,1,0:T(8,128)S(1)}, u32[]{:S(2)}, u32[]{:S(2)}) %collective-permute-start.5) | collective-permute-done | bytes 278560 | tf_op jit(solution)/shard_map/ppermute | solution.py:38
  32.5 0.9 %shard_map.80.begun = f32[2,3,34,8,128]{4,3,2,1,0:T(8,128)} custom-call(f32[2,3,34,8,128]{4,3,2,1,0:T(8,128)} %shard_map.79.begun, f32[2,34,8,128]{3,2,1,0:T(8,128)S(1)} %shard_map.77.mid1, f32[2,34,8,128]{3,2,1,0:T(8,128)S(1)} %get-tuple-element.23.mid2, f32[2,34,8,128]{3,2,1,0:T(8,128)S(1)} %collective-permute-done.5.halo, ...), custom_call_target="tpu_custom_call", output_to_operand_aliasing={{}: (0, {})} | custom-call | flops 1000000 | bytes 1000000 | tf_op jit(solution)/shard_map/pallas_call | solution.py:47
  33.4 2.1 %collective-permute-done.6.halo = f32[2,34,8,128]{3,2,1,0:T(8,128)S(1)} collective-permute-done((f32[2,34,8,128]{3,2,1,0:T(8,128)S(1)}, f32[2,34,8,128]{3,2,1,0:T(8,128)S(1)}, u32[]{:S(2)}, u32[]{:S(2)}) %collective-permute-start.6) | collective-permute-done | bytes 278560 | tf_op jit(solution)/shard_map/ppermute | solution.py:38
  35.5 0.9 %shard_map.81 = f32[2,3,34,8,128]{4,3,2,1,0:T(8,128)} custom-call(f32[2,3,34,8,128]{4,3,2,1,0:T(8,128)} %shard_map.80.begun, f32[2,34,8,128]{3,2,1,0:T(8,128)S(1)} %shard_map.76.before.mid0, f32[2,34,8,128]{3,2,1,0:T(8,128)S(1)} %shard_map.77.mid1, f32[2,34,8,128]{3,2,1,0:T(8,128)S(1)} %collective-permute-done.6.halo, ...), custom_call_target="tpu_custom_call", output_to_operand_aliasing={{}: (0, {})} | custom-call | flops 1000000 | bytes 1000000 | tf_op jit(solution)/shard_map/pallas_call | solution.py:47
Async XLA Ops:
  1.5 12.7 %collective-permute-start.3 = (f32[2,34,8,128]{3,2,1,0:T(8,128)S(1)}, f32[2,34,8,128]{3,2,1,0:T(8,128)S(1)}, u32[]{:S(2)}, u32[]{:S(2)}) collective-permute-start(f32[2,34,8,128]{3,2,1,0:T(8,128)S(1)} %get-tuple-element.18.col2), channel_id=1, source_target_pairs={{0,4},{4,8},{8,12},{12,16},{16,20},{20,24},{24,28},{28,0},{1,5},{5... | collective-permute-start | bytes 835592 | tf_op jit(solution)/shard_map/ppermute | solution.py:38
  4.5 3.4 %collective-permute-start = (f32[208,128]{1,0:T(8,128)S(1)}, f32[208,128]{1,0:T(8,128)S(1)}, u32[]{:S(2)}, u32[]{:S(2)}) collective-permute-start(f32[208,128]{1,0:T(8,128)S(1)} %get-tuple-element.15.own), channel_id=1, source_target_pairs={{0,1},{1,0},{2,3},{3,2},{4,5},{5,4},{6,7},{7,6},{8,9},{9,8},{10,11... | collective-permute-start | bytes 319496 | tf_op jit(solution)/shard_map/ppermute | solution.py:43
  4.5 5.8 %collective-permute-start.1 = (f32[208,128]{1,0:T(8,128)S(1)}, f32[208,128]{1,0:T(8,128)S(1)}, u32[]{:S(2)}, u32[]{:S(2)}) collective-permute-start(f32[208,128]{1,0:T(8,128)S(1)} %get-tuple-element.15.own), channel_id=1, source_target_pairs={{0,2},{1,3},{2,0},{3,1},{4,6},{5,7},{6,4},{7,5},{8,10},{9,11},{10,... | collective-permute-start | bytes 319496 | tf_op jit(solution)/shard_map/ppermute | solution.py:43
  6.0 5.8 %collective-permute-start.2 = (f32[208,128]{1,0:T(8,128)S(1)}, f32[208,128]{1,0:T(8,128)S(1)}, u32[]{:S(2)}, u32[]{:S(2)}) collective-permute-start(f32[208,128]{1,0:T(8,128)S(1)} %get-tuple-element.15.own), channel_id=1, source_target_pairs={{0,3},{1,2},{2,1},{3,0},{4,7},{5,6},{6,5},{7,4},{8,11},{9,10},{10,... | collective-permute-start | bytes 319496 | tf_op jit(solution)/shard_map/ppermute | solution.py:43
  6.3 1.0 %copy-start = (s32[2,2,3,34,256]{4,1,3,2,0:T(2,128)S(1)}, s32[2,2,3,34,256]{4,1,3,2,0:T(2,128)}, u32[]{:S(2)}) copy-start(s32[2,2,3,34,256]{4,1,3,2,0:T(2,128)} %param.8) | copy-start | bytes 1253380
  14.9 10.4 %collective-permute-start.4 = (f32[616,128]{1,0:T(8,128)S(1)}, f32[616,128]{1,0:T(8,128)S(1)}, u32[]{:S(2)}, u32[]{:S(2)}) collective-permute-start(f32[616,128]{1,0:T(8,128)S(1)} %get-tuple-element.19.message), channel_id=1, source_target_pairs={{0,28},{4,0},{8,4},{12,8},{16,12},{20,16},{24,20},{28,24},{1,29},{... | collective-permute-start | bytes 946184 | tf_op jit(solution)/shard_map/ppermute | solution.py:38
  17.5 15.1 %collective-permute-start.5 = (f32[2,34,8,128]{3,2,1,0:T(8,128)S(1)}, f32[2,34,8,128]{3,2,1,0:T(8,128)S(1)}, u32[]{:S(2)}, u32[]{:S(2)}) collective-permute-start(f32[2,34,8,128]{3,2,1,0:T(8,128)S(1)} %shard_map.76.before.mid0), channel_id=1, source_target_pairs={{0,28},{4,0},{8,4},{12,8},{16,12},{20,16},{24,20},{28,24},{1,29},{... | collective-permute-start | bytes 835592 | tf_op jit(solution)/shard_map/ppermute | solution.py:38
  26.1 9.4 %collective-permute-start.6 = (f32[2,34,8,128]{3,2,1,0:T(8,128)S(1)}, f32[2,34,8,128]{3,2,1,0:T(8,128)S(1)}, u32[]{:S(2)}, u32[]{:S(2)}) collective-permute-start(f32[2,34,8,128]{3,2,1,0:T(8,128)S(1)} %get-tuple-element.23.mid2), channel_id=1, source_target_pairs={{0,4},{4,8},{8,12},{12,16},{16,20},{20,24},{24,28},{28,0},{1,5},{5... | collective-permute-start | bytes 835592 | tf_op jit(solution)/shard_map/ppermute | solution.py:38

commit v3 on v2

--- a/solution.py
+++ b/solution.py
@@ -333,7 +333,8 @@
         (HBM,) * 6, [pltpu.VMEM(x.shape, x.dtype) for x in fields] + [dma((5,)), dma((columns, tracers))],
         10**5, 10**6, stay(state), stay(flag), *fields)
     west_halo = shifted(col2, "lon", 1)
-    others = [swapped(packed, "trc", mask) for mask in (1, 2, 3)]
+    across = swapped(packed, "trc", 2)
+    others = [swapped(packed, "trc", 1), across, swapped(across, "trc", 1)]
     turn = call(turn_kernel, f32(2, tracers, columns, levels, 8, LANES), (VMEM,), (), 10**6, 10**6, switch)
     rates, factors, message = call(
         pre_kernel,

time: 36.6 us -> 36.6 us (level)
  waiting for transfers between devices: 19.4 us -> 19.8 us
  starting transfers between devices: 8.19 us -> 7.82 us
    ppermute x4, waiting for transfers between devices: 15.5 us -> 16.5 us  [shifted(): lax.ppermute(value, axis, [(i, (i + by) % count) for i in range(count)])]
    ppermute x3, waiting for transfers between devices: 3.91 us -> 3.22 us  [swapped(): return lax.ppermute(value, axis, [(i, i ^ mask) for i in range(count)])]
  transfers between devices with their start and end apart: 7 -> 7, of which waited for: 6 -> 5; matrix products, arithmetic and copies ran while one was open for 0% -> 0% of each run, Pallas kernels for 13% -> 13%
where the time goes in v3:
time: 36.6 us; the launch traced here: 36.4 us
  waiting for transfers between devices  19.8 us (54%)
  starting transfers between devices  7.82 us (21%)
  Pallas kernels  7.76 us (21%)
  local copies, waits for them, and re-layouts  1 us (3%)
    ppermute x4, waiting for transfers between devices, shifted(): lax.ppermute(value, axis, [(i, (i + by) % count) for i in range(count)])  16.5 us
    pallas_call x9, Pallas kernels, call(): pl.pallas_call(kernel, out_shape=out, in_specs=in_specs, out_specs=jax.tr...  7.76 us
    ppermute x4, starting transfers between devices, shifted(): lax.ppermute(value, axis, [(i, (i + by) % count) for i in range(count)])  6.33 us
    ppermute x3, waiting for transfers between devices, swapped(): return lax.ppermute(value, axis, [(i, i ^ mask) for i in range(count)])  3.22 us
    ppermute x3, starting transfers between devices, swapped(): return lax.ppermute(value, axis, [(i, i ^ mask) for i in range(count)])  1.5 us
    unnamed x2, local copies, waits for them, and re-layouts  1 us
  transfers between devices with their start and end apart: 7, of which 5 were waited for; matrix products, arithmetic and copies ran while one was open for 0% of the time, Pallas kernels for 13%

profile of v3, /device:TPU:0, one launch (start us, length us, event | category | flops | bytes accessed | tf_op | source)
XLA Modules:
  0.0 36.4 jit_solution(6662737910894719543)
XLA Ops:
  0.0 1.5 %shard_map.73 = (f32[77,8,128]{2,1,0:T(8,128)S(1)}, f32[2,34,8,128]{3,2,1,0:T(8,128)S(1)}, f32[2,34,8,128]{3,2,1,0:T(8,128)S(1)}, f32[208,128]{1,0:T(8,128)S(1)}, s32[3,136,128]{2,1,0:T(8,128)S(1)}) custom-call(f32[2,3,34,8,128]{4,3,2,1,0:T(8,128)} %bitcast.24, s32[3,136,128]{2,1,0:T(8,128)} %bitcast.25, f32[3,34,64]{2,1,0:T(8,128)} %mass.1, ...), custom_call_target="tpu_custom_call" | custom-call | flops 100000 | bytes 1000000 | tf_op jit(solution)/shard_map/pallas_call | solution.py:47
  1.5 3.0 %collective-permute-start.3 = (f32[2,34,8,128]{3,2,1,0:T(8,128)S(1)}, f32[2,34,8,128]{3,2,1,0:T(8,128)S(1)}, u32[]{:S(2)}, u32[]{:S(2)}) collective-permute-start(f32[2,34,8,128]{3,2,1,0:T(8,128)S(1)} %get-tuple-element.18.col2), channel_id=1, source_target_pairs={{0,4},{4,8},{8,12},{12,16},{16,20},{20,24},{24,28},{28,0},{1,5},{5... | collective-permute-start | bytes 835592 | tf_op jit(solution)/shard_map/ppermute | solution.py:38
  4.5 1.5 %collective-permute-start.1 = (f32[208,128]{1,0:T(8,128)S(1)}, f32[208,128]{1,0:T(8,128)S(1)}, u32[]{:S(2)}, u32[]{:S(2)}) collective-permute-start(f32[208,128]{1,0:T(8,128)S(1)} %get-tuple-element.15.own), channel_id=1, source_target_pairs={{0,2},{1,3},{2,0},{3,1},{4,6},{5,7},{6,4},{7,5},{8,10},{9,11},{10,... | collective-permute-start | bytes 319496 | tf_op jit(solution)/shard_map/ppermute | solution.py:43
  6.0 0.0 collective-permute-start
  6.0 3.2 %collective-permute-done.1.second = f32[208,128]{1,0:T(8,128)S(1)} collective-permute-done((f32[208,128]{1,0:T(8,128)S(1)}, f32[208,128]{1,0:T(8,128)S(1)}, u32[]{:S(2)}, u32[]{:S(2)}) %collective-permute-start.1) | collective-permute-done | bytes 106528 | tf_op jit(solution)/shard_map/ppermute | solution.py:43
  9.2 0.0 collective-permute-start.2
  9.2 0.0 copy-start
  9.2 1.0 %copy-done = s32[2,2,3,34,256]{4,1,3,2,0:T(2,128)S(1)} copy-done((s32[2,2,3,34,256]{4,1,3,2,0:T(2,128)S(1)}, s32[2,2,3,34,256]{4,1,3,2,0:T(2,128)}, u32[]{:S(2)}) %copy-start) | copy-done | bytes 417816
  10.2 0.5 %shard_map.74.also.turn = f32[2,2,3,34,8,128]{5,4,3,2,1,0:T(8,128)S(1)} custom-call(s32[2,3,136,128]{3,2,1,0:T(8,128)S(1)} %bitcast.23), custom_call_target="tpu_custom_call" | custom-call | flops 1000000 | bytes 1000000 | tf_op jit(solution)/shard_map/pallas_call | solution.py:47
  10.7 0.0 collective-permute-done.first
  10.7 0.0 collective-permute-done.2.third
  10.7 3.5 %collective-permute-done.3.before.west_halo = f32[2,34,8,128]{3,2,1,0:T(8,128)S(1)} collective-permute-done((f32[2,34,8,128]{3,2,1,0:T(8,128)S(1)}, f32[2,34,8,128]{3,2,1,0:T(8,128)S(1)}, u32[]{:S(2)}, u32[]{:S(2)}) %collective-permute-start.3) | collective-permute-done | bytes 278560 | tf_op jit(solution)/shard_map/ppermute | solution.py:38
  14.2 0.7 %shard_map.75 = (f32[4,3,34,8,128]{4,3,2,1,0:T(8,128)S(1)}, f32[3,3,34,8,128]{4,3,2,1,0:T(8,128)S(1)}, f32[616,128]{1,0:T(8,128)S(1)}) custom-call(f32[208,128]{1,0:T(8,128)S(1)} %get-tuple-element.15.own, f32[208,128]{1,0:T(8,128)S(1)} %collective-permute-done.first, f32[208,128]{1,0:T(8,128)S(1)} %collective-permute-done.1.second, ...), custom_call_target="tpu_custom_call", output_to_operand_aliasing={{2}: (6, {})} | custom-call | flops 1000000 | bytes 1000000 | tf_op jit(solution)/shard_map/pallas_call | solution.py:47
  14.9 1.8 %collective-permute-start.4 = (f32[616,128]{1,0:T(8,128)S(1)}, f32[616,128]{1,0:T(8,128)S(1)}, u32[]{:S(2)}, u32[]{:S(2)}) collective-permute-start(f32[616,128]{1,0:T(8,128)S(1)} %get-tuple-element.19.message), channel_id=1, source_target_pairs={{0,28},{4,0},{8,4},{12,8},{16,12},{20,16},{24,20},{28,24},{1,29},{... | collective-permute-start | bytes 946184 | tf_op jit(solution)/shard_map/ppermute | solution.py:38
  16.7 0.8 %shard_map.76.before.mid0 = f32[2,34,8,128]{3,2,1,0:T(8,128)S(1)} custom-call(f32[616,128]{1,0:T(8,128)S(1)} %get-tuple-element.19.message, f32[2,34,8,128]{3,2,1,0:T(8,128)S(1)} %get-tuple-element.20.col1, f32[2,34,8,128]{3,2,1,0:T(8,128)S(1)} %collective-permute-done.3.before.west_halo, f32[4,3,34,8,128]{4,3,2,1,0:T(8,128)S(1)} %get-tuple-element.21.rates, ...), custom_call_target="tpu_custom_call" | custom-call | flops 1000000 | bytes 1000000 | tf_op jit(solution)/shard_map/pallas_call | solution.py:47
  17.5 1.5 %collective-permute-start.5 = (f32[2,34,8,128]{3,2,1,0:T(8,128)S(1)}, f32[2,34,8,128]{3,2,1,0:T(8,128)S(1)}, u32[]{:S(2)}, u32[]{:S(2)}) collective-permute-start(f32[2,34,8,128]{3,2,1,0:T(8,128)S(1)} %shard_map.76.before.mid0), channel_id=1, source_target_pairs={{0,28},{4,0},{8,4},{12,8},{16,12},{20,16},{24,20},{28,24},{1,29},{... | collective-permute-start | bytes 835592 | tf_op jit(solution)/shard_map/ppermute | solution.py:38
  18.9 6.4 %collective-permute-done.4.halo = f32[616,128]{1,0:T(8,128)S(1)} collective-permute-done((f32[616,128]{1,0:T(8,128)S(1)}, f32[616,128]{1,0:T(8,128)S(1)}, u32[]{:S(2)}, u32[]{:S(2)}) %collective-permute-start.4) | collective-permute-done | bytes 315424 | tf_op jit(solution)/shard_map/ppermute | solution.py:38
  25.3 0.8 %shard_map.78 = (f32[2,34,8,128]{3,2,1,0:T(8,128)S(1)}, f32[34,8,128]{2,1,0:T(8,128)S(1)}) custom-call(f32[2,34,8,128]{3,2,1,0:T(8,128)S(1)} %get-tuple-element.20.col1, f32[2,34,8,128]{3,2,1,0:T(8,128)S(1)} %get-tuple-element.18.col2, f32[616,128]{1,0:T(8,128)S(1)} %collective-permute-done.4.halo, f32[4,3,34,8,128]{4,3,2,1,0:T(8,128)S(1)} %get-tuple-element.21.rates, ...), custom_call_target="tpu_custom_call" | custom-call | flops 1000000 | bytes 1000000 | tf_op jit(solution)/shard_map/pallas_call | solution.py:47
  26.1 0.1 collective-permute-start.6
  26.2 0.8 %shard_map.77.mid1 = f32[2,34,8,128]{3,2,1,0:T(8,128)S(1)} custom-call(f32[616,128]{1,0:T(8,128)S(1)} %get-tuple-element.19.message, f32[2,34,8,128]{3,2,1,0:T(8,128)S(1)} %get-tuple-element.20.col1, f32[2,34,8,128]{3,2,1,0:T(8,128)S(1)} %get-tuple-element.18.col2, f32[4,3,34,8,128]{4,3,2,1,0:T(8,128)S(1)} %get-tuple-element.21.rates, ...), custom_call_target="tpu_custom_call" | custom-call | flops 1000000 | bytes 1000000 | tf_op jit(solution)/shard_map/pallas_call | solution.py:47
  27.0 0.9 %shard_map.79.begun = f32[2,3,34,8,128]{4,3,2,1,0:T(8,128)} custom-call(f32[2,34,8,128]{3,2,1,0:T(8,128)S(1)} %shard_map.76.before.mid0, f32[2,34,8,128]{3,2,1,0:T(8,128)S(1)} %shard_map.77.mid1, f32[2,34,8,128]{3,2,1,0:T(8,128)S(1)} %get-tuple-element.23.mid2, f32[4,3,34,8,128]{4,3,2,1,0:T(8,128)S(1)} %get-tuple-element.21.rates, ...), custom_call_target="tpu_custom_call" | custom-call | flops 1000000 | bytes 1000000 | tf_op jit(solution)/shard_map/pallas_call | solution.py:47
  27.9 4.6 %collective-permute-done.5.halo = f32[2,34,8,128]{3,2,1,0:T(8,128)S(1)} collective-permute-done((f32[2,34,8,128]{3,2,1,0:T(8,128)S(1)}, f32[2,34,8,128]{3,2,1,0:T(8,128)S(1)}, u32[]{:S(2)}, u32[]{:S(2)}) %collective-permute-start.5) | collective-permute-done | bytes 278560 | tf_op jit(solution)/shard_map/ppermute | solution.py:38
  32.5 0.9 %shard_map.80.begun = f32[2,3,34,8,128]{4,3,2,1,0:T(8,128)} custom-call(f32[2,3,34,8,128]{4,3,2,1,0:T(8,128)} %shard_map.79.begun, f32[2,34,8,128]{3,2,1,0:T(8,128)S(1)} %shard_map.77.mid1, f32[2,34,8,128]{3,2,1,0:T(8,128)S(1)} %get-tuple-element.23.mid2, f32[2,34,8,128]{3,2,1,0:T(8,128)S(1)} %collective-permute-done.5.halo, ...), custom_call_target="tpu_custom_call", output_to_operand_aliasing={{}: (0, {})} | custom-call | flops 1000000 | bytes 1000000 | tf_op jit(solution)/shard_map/pallas_call | solution.py:47
  33.4 2.1 %collective-permute-done.6.halo = f32[2,34,8,128]{3,2,1,0:T(8,128)S(1)} collective-permute-done((f32[2,34,8,128]{3,2,1,0:T(8,128)S(1)}, f32[2,34,8,128]{3,2,1,0:T(8,128)S(1)}, u32[]{:S(2)}, u32[]{:S(2)}) %collective-permute-start.6) | collective-permute-done | bytes 278560 | tf_op jit(solution)/shard_map/ppermute | solution.py:38
  35.5 0.9 %shard_map.81 = f32[2,3,34,8,128]{4,3,2,1,0:T(8,128)} custom-call(f32[2,3,34,8,128]{4,3,2,1,0:T(8,128)} %shard_map.80.begun, f32[2,34,8,128]{3,2,1,0:T(8,128)S(1)} %shard_map.76.before.mid0, f32[2,34,8,128]{3,2,1,0:T(8,128)S(1)} %shard_map.77.mid1, f32[2,34,8,128]{3,2,1,0:T(8,128)S(1)} %collective-permute-done.6.halo, ...), custom_call_target="tpu_custom_call", output_to_operand_aliasing={{}: (0, {})} | custom-call | flops 1000000 | bytes 1000000 | tf_op jit(solution)/shard_map/pallas_call | solution.py:47
Async XLA Ops:
  1.5 12.7 %collective-permute-start.3 = (f32[2,34,8,128]{3,2,1,0:T(8,128)S(1)}, f32[2,34,8,128]{3,2,1,0:T(8,128)S(1)}, u32[]{:S(2)}, u32[]{:S(2)}) collective-permute-start(f32[2,34,8,128]{3,2,1,0:T(8,128)S(1)} %get-tuple-element.18.col2), channel_id=1, source_target_pairs={{0,4},{4,8},{8,12},{12,16},{16,20},{20,24},{24,28},{28,0},{1,5},{5... | collective-permute-start | bytes 835592 | tf_op jit(solution)/shard_map/ppermute | solution.py:38
  4.5 4.7 %collective-permute-start.1 = (f32[208,128]{1,0:T(8,128)S(1)}, f32[208,128]{1,0:T(8,128)S(1)}, u32[]{:S(2)}, u32[]{:S(2)}) collective-permute-start(f32[208,128]{1,0:T(8,128)S(1)} %get-tuple-element.15.own), channel_id=1, source_target_pairs={{0,2},{1,3},{2,0},{3,1},{4,6},{5,7},{6,4},{7,5},{8,10},{9,11},{10,... | collective-permute-start | bytes 319496 | tf_op jit(solution)/shard_map/ppermute | solution.py:43
  6.0 4.7 %collective-permute-start = (f32[208,128]{1,0:T(8,128)S(1)}, f32[208,128]{1,0:T(8,128)S(1)}, u32[]{:S(2)}, u32[]{:S(2)}) collective-permute-start(f32[208,128]{1,0:T(8,128)S(1)} %get-tuple-element.15.own), channel_id=1, source_target_pairs={{0,1},{1,0},{2,3},{3,2},{4,5},{5,4},{6,7},{7,6},{8,9},{9,8},{10,11... | collective-permute-start | bytes 319496 | tf_op jit(solution)/shard_map/ppermute | solution.py:43
  9.2 1.5 %collective-permute-start.2 = (f32[208,128]{1,0:T(8,128)S(1)}, f32[208,128]{1,0:T(8,128)S(1)}, u32[]{:S(2)}, u32[]{:S(2)}) collective-permute-start(f32[208,128]{1,0:T(8,128)S(1)} %collective-permute-done.1.second), channel_id=1, source_target_pairs={{0,1},{1,0},{2,3},{3,2},{4,5},{5,4},{6,7},{7,6},{8,9},{9,8},{10,11... | collective-permute-start | bytes 319496 | tf_op jit(solution)/shard_map/ppermute | solution.py:43
  9.2 1.0 %copy-start = (s32[2,2,3,34,256]{4,1,3,2,0:T(2,128)S(1)}, s32[2,2,3,34,256]{4,1,3,2,0:T(2,128)}, u32[]{:S(2)}) copy-start(s32[2,2,3,34,256]{4,1,3,2,0:T(2,128)} %param.8) | copy-start | bytes 1253380
  14.9 10.4 %collective-permute-start.4 = (f32[616,128]{1,0:T(8,128)S(1)}, f32[616,128]{1,0:T(8,128)S(1)}, u32[]{:S(2)}, u32[]{:S(2)}) collective-permute-start(f32[616,128]{1,0:T(8,128)S(1)} %get-tuple-element.19.message), channel_id=1, source_target_pairs={{0,28},{4,0},{8,4},{12,8},{16,12},{20,16},{24,20},{28,24},{1,29},{... | collective-permute-start | bytes 946184 | tf_op jit(solution)/shard_map/ppermute | solution.py:38
  17.5 15.1 %collective-permute-start.5 = (f32[2,34,8,128]{3,2,1,0:T(8,128)S(1)}, f32[2,34,8,128]{3,2,1,0:T(8,128)S(1)}, u32[]{:S(2)}, u32[]{:S(2)}) collective-permute-start(f32[2,34,8,128]{3,2,1,0:T(8,128)S(1)} %shard_map.76.before.mid0), channel_id=1, source_target_pairs={{0,28},{4,0},{8,4},{12,8},{16,12},{20,16},{24,20},{28,24},{1,29},{... | collective-permute-start | bytes 835592 | tf_op jit(solution)/shard_map/ppermute | solution.py:38
  26.1 9.4 %collective-permute-start.6 = (f32[2,34,8,128]{3,2,1,0:T(8,128)S(1)}, f32[2,34,8,128]{3,2,1,0:T(8,128)S(1)}, u32[]{:S(2)}, u32[]{:S(2)}) collective-permute-start(f32[2,34,8,128]{3,2,1,0:T(8,128)S(1)} %get-tuple-element.23.mid2), channel_id=1, source_target_pairs={{0,4},{4,8},{8,12},{12,16},{16,20},{20,24},{24,28},{28,0},{1,5},{5... | collective-permute-start | bytes 835592 | tf_op jit(solution)/shard_map/ppermute | solution.py:38

commit v4 on v3

--- a/solution.py
+++ b/solution.py
@@ -69,13 +69,13 @@
     return row == 0, row == slope
 
 
-def head_kernel(state, flags, mass, xf, yf, km, message, col1, col2, packed, flags_v, mass_v, xf_v, yf_v, km_v, sems, column_sems):
+def head_kernel(state, flags, mass, xf, yf, km, col0, col1, col2, packed, flags_v, mass_v, xf_v, yf_v, km_v, sems, column_sems):
     tracers, columns, levels = state.shape[0], mass.shape[0], mass.shape[1]
     half = LANES // 2
     pairs = ((mass, mass_v), (xf, xf_v), (yf, yf_v), (km, km_v), (flags, flags_v))
     copies = [pltpu.make_async_copy(src, dst, sems.at[i]) for i, (src, dst) in enumerate(pairs)]
     for t in range(tracers):
-        for c, place in ((2, col2.at[t]), (0, message.at[pl.ds(t * levels, levels)]), (1, col1.at[t])):
+        for c, place in ((2, col2.at[t]), (0, col0.at[t]), (1, col1.at[t])):
             copies.append(pltpu.make_async_copy(state.at[t, c], place, column_sems.at[c, t]))
     for copy in copies:
         copy.start()
@@ -97,10 +97,6 @@
     return jnp.where(upper_block, blocks[1], blocks[0])
 
 
-def face_row(rows, levels, b):
-    return rows - -(-2 * levels // 8) * 8 + b * levels
-
-
 def turn_kernel(switches, turn):
     tracers, columns = switches.shape[:2]
     levels = switches.shape[2] // 4
@@ -117,7 +113,7 @@
                     turn[d, t, c, l] = jnp.where(moment == 0, take, jnp.where(moment == 1 + d, keep, 1.0))
 
 
-def pre_kernel(own, first, second, third, flags, order, begun, before, also, rates, factors, message, fields):
+def pre_kernel(own, first, second, third, flags, order, before, also, rates, factors, face, fields):
     columns, levels = rates.shape[1], rates.shape[2]
     half = LANES // 2
     odd = order[0] % 2 == 1
@@ -142,8 +138,7 @@
                 fields[2 * pair + 1, c, b] = flux
                 if pair == 0 and c == 0:
                     eastward = flags[0, pl.ds(2 * b, levels, stride=4), :].astype(jnp.float32)
-                    start = face_row(message.shape[0], levels, b)
-                    message[start : start + levels] = (2.0 * eastward - 1.0) * flux
+                    face[b * levels : (b + 1) * levels] = (2.0 * eastward - 1.0) * flux
 
     def field(f, c, l):
         return spread(upper_block, fields, ((f, c, 0), l), ((f, c, 1), l))
@@ -252,35 +247,28 @@
             out[t, l] = values[t]
 
 
-def tiles(ref, levels):
-    if len(ref.shape) == 4:
-        return lambda t, l: ref[t, l]
-    return lambda t, l: ref[(t * levels + l) * 8 : (t * levels + l + 1) * 8]
-
-
-def west_kernel(message, col1, west_halo, rates, factors, turn, out):
-    levels = out.shape[1]
-    middle(0, tiles(message, levels), tiles(col1, levels), tiles(west_halo, levels),
-           lambda l: rates[0, 0, l], rates, factors, turn, out)
-
-
-def inner_kernel(message, col1, col2, rates, factors, turn, out):
-    levels = out.shape[1]
-    middle(1, tiles(col1, levels), tiles(col2, levels), tiles(message, levels),
-           lambda l: rates[0, 1, l], rates, factors, turn, out)
-
-
-def east_kernel(col1, col2, halo, rates, factors, turn, before, out, east):
+def tiles(ref):
+    return lambda t, l: ref[t, l]
+
+
+def west_kernel(col0, col1, west_halo, rates, factors, turn, out):
+    middle(0, tiles(col0), tiles(col1), tiles(west_halo), lambda l: rates[0, 0, l], rates, factors, turn, out)
+
+
+def inner_kernel(col0, col1, col2, rates, factors, turn, out):
+    middle(1, tiles(col1), tiles(col2), tiles(col0), lambda l: rates[0, 1, l], rates, factors, turn, out)
+
+
+def east_kernel(col1, col2, east_halo, face, rates, factors, turn, before, out, east):
     levels = out.shape[1]
     upper_block = lax.broadcasted_iota(jnp.int32, (8, LANES), 0) >= MOMENTS
-    rows = [face_row(halo.shape[0], levels, b) for b in range(2)]
 
     def east_rate(l):
-        flux = spread(upper_block, halo, ((), rows[0] + l), ((), rows[1] + l))
+        flux = spread(upper_block, face, ((), l), ((), levels + l))
         east[l] = jnp.maximum(flux, 0.0) * rates[0, 2, l]
         return east[l]
 
-    middle(2, tiles(col2, levels), tiles(halo, levels), tiles(col1, levels), east_rate, rates, factors, turn, out)
+    middle(2, tiles(col2), tiles(east_halo), tiles(col1), east_rate, rates, factors, turn, out)
 
 
 def finish(c, own, east_side, west_side, east_rate, rates, turn, out, buf, sems):
@@ -323,31 +311,31 @@
     order = lax.axis_index("trc").astype(jnp.int32).reshape(1)
     column = f32(tracers, levels, 8, LANES)
     rows = -(-2 * columns * levels // 8) * 8
-    length = tracers * levels + -(-2 * levels // 8)
     dma = pltpu.SemaphoreType.DMA
     fields = tuple(stay(x) for x in (air_mass, x_flux, y_flux, vertical_mixing))
 
-    message, col1, col2, packed, flag = call(
+    col0, col1, col2, packed, flag = call(
         head_kernel,
-        (f32(length, 8, LANES), column, column, f32(rows, LANES), jax.ShapeDtypeStruct(flag.shape, flag.dtype)),
+        (column, column, column, f32(rows, LANES), jax.ShapeDtypeStruct(flag.shape, flag.dtype)),
         (HBM,) * 6, [pltpu.VMEM(x.shape, x.dtype) for x in fields] + [dma((5,)), dma((columns, tracers))],
         10**5, 10**6, stay(state), stay(flag), *fields)
     west_halo = shifted(col2, "lon", 1)
+    east_halo = shifted(col0, "lon", -1)
     across = swapped(packed, "trc", 2)
     others = [swapped(packed, "trc", 1), across, swapped(across, "trc", 1)]
     turn = call(turn_kernel, f32(2, tracers, columns, levels, 8, LANES), (VMEM,), (), 10**6, 10**6, switch)
-    rates, factors, message = call(
+    rates, factors, face = call(
         pre_kernel,
-        (f32(4, columns, levels, 8, LANES), f32(3, columns, levels, 8, LANES), f32(length * 8, LANES)),
-        (VMEM,) * 5 + (SMEM, VMEM, VMEM, VMEM), [pltpu.VMEM((4, columns, 2, levels, LANES), jnp.float32)],
-        10**6, 10**6, packed, *others, flag, order, message.reshape(length * 8, LANES), west_halo, turn, aliases={6: 2})
-    east_message = shifted(message, "lon", -1)
-    mid0 = call(west_kernel, column, (VMEM,) * 6, (), 10**6, 10**6, message, col1, west_halo, rates, factors, turn)
-    east_halo = shifted(mid0, "lon", -1)
-    mid1 = call(inner_kernel, column, (VMEM,) * 6, (), 10**6, 10**6, message, col1, col2, rates, factors, turn)
-    mid2, east = call(east_kernel, (column, f32(levels, 8, LANES)), (VMEM,) * 7, (), 10**6, 10**6,
-                      col1, col2, east_message, rates, factors, turn, mid0)
-    west_halo = shifted(mid2, "lon", 1)
+        (f32(4, columns, levels, 8, LANES), f32(3, columns, levels, 8, LANES), f32(2 * levels, LANES)),
+        (VMEM,) * 5 + (SMEM, VMEM, VMEM), [pltpu.VMEM((4, columns, 2, levels, LANES), jnp.float32)],
+        10**6, 10**6, packed, *others, flag, order, west_halo, turn)
+    face = shifted(face, "lon", -1)
+    mid0 = call(west_kernel, column, (VMEM,) * 6, (), 10**6, 10**6, col0, col1, west_halo, rates, factors, turn)
+    east_mid = shifted(mid0, "lon", -1)
+    mid1 = call(inner_kernel, column, (VMEM,) * 6, (), 10**6, 10**6, col0, col1, col2, rates, factors, turn)
+    mid2, east = call(east_kernel, (column, f32(levels, 8, LANES)), (VMEM,) * 8, (), 10**6, 10**6,
+                      col1, col2, east_halo, face, rates, factors, turn, mid0)
+    west_mid = shifted(mid2, "lon", 1)
 
     def last(kernel, aliases, *args):
         first = (HBM,) * len(aliases)
@@ -356,8 +344,8 @@
                     *args, out_specs=HBM, aliases=aliases)
 
     out = last(last_inner_kernel, {}, mid0, mid1, mid2, rates, turn)
-    out = last(last_east_kernel, {0: 0}, out, mid1, mid2, east_halo, east, rates, turn)
-    out = last(last_west_kernel, {0: 0}, out, mid0, mid1, west_halo, rates, turn)
+    out = last(last_east_kernel, {0: 0}, out, mid1, mid2, east_mid, east, rates, turn)
+    out = last(last_west_kernel, {0: 0}, out, mid0, mid1, west_mid, rates, turn)
     return state_back(out)
 
 

time: 36.6 us -> 38.7 us (1.057)
  starting transfers between devices: 7.82 us -> 14.4 us
  waiting for transfers between devices: 19.8 us -> 15.3 us
    ppermute x4 -> x5, starting transfers between devices: 6.33 us -> 12.8 us  [shifted(): lax.ppermute(value, axis, [(i, (i + by) % count) for i in range(count)])]
    ppermute x4 -> x5, waiting for transfers between devices: 16.5 us -> 12.1 us  [shifted(): lax.ppermute(value, axis, [(i, (i + by) % count) for i in range(count)])]
  transfers between devices with their start and end apart: 7 -> 8, of which waited for: 5 -> 4; matrix products, arithmetic and copies ran while one was open for 0% -> 0% of each run, Pallas kernels for 13% -> 14%
where the time goes in v4:
time: 38.7 us; the launch traced here: 38.5 us
  waiting for transfers between devices  15.3 us (40%)
  starting transfers between devices  14.4 us (37%)
  Pallas kernels  7.79 us (20%)
  local copies, waits for them, and re-layouts  1 us (3%)
    ppermute x5, starting transfers between devices, shifted(): lax.ppermute(value, axis, [(i, (i + by) % count) for i in range(count)])  12.8 us
    ppermute x5, waiting for transfers between devices, shifted(): lax.ppermute(value, axis, [(i, (i + by) % count) for i in range(count)])  12.1 us
    pallas_call x9, Pallas kernels, call(): pl.pallas_call(kernel, out_shape=out, in_specs=in_specs, out_specs=jax.tr...  7.79 us
    ppermute x3, waiting for transfers between devices, swapped(): return lax.ppermute(value, axis, [(i, i ^ mask) for i in range(count)])  3.12 us
    ppermute x3, starting transfers between devices, swapped(): return lax.ppermute(value, axis, [(i, i ^ mask) for i in range(count)])  1.6 us
    unnamed x2, local copies, waits for them, and re-layouts  1 us
  transfers between devices with their start and end apart: 8, of which 4 were waited for; matrix products, arithmetic and copies ran while one was open for 0% of the time, Pallas kernels for 14%

profile of v4, /device:TPU:0, one launch (start us, length us, event | category | flops | bytes accessed | tf_op | source)
XLA Modules:
  0.0 38.5 jit_solution(5956063924839710625)
XLA Ops:
  0.0 1.5 %shard_map.73 = (f32[2,34,8,128]{3,2,1,0:T(8,128)S(1)}, f32[2,34,8,128]{3,2,1,0:T(8,128)S(1)}, f32[2,34,8,128]{3,2,1,0:T(8,128)S(1)}, f32[208,128]{1,0:T(8,128)S(1)}, s32[3,136,128]{2,1,0:T(8,128)S(1)}) custom-call(f32[2,3,34,8,128]{4,3,2,1,0:T(8,128)} %bitcast.22, s32[3,136,128]{2,1,0:T(8,128)} %bitcast.23, f32[3,34,64]{2,1,0:T(8,128)} %mass.1, ...), custom_call_target="tpu_custom_call" | custom-call | flops 100000 | bytes 1000000 | tf_op jit(solution)/shard_map/pallas_call | solution.py:47
  1.5 3.0 %collective-permute-start = (f32[2,34,8,128]{3,2,1,0:T(8,128)S(1)}, f32[2,34,8,128]{3,2,1,0:T(8,128)S(1)}, u32[]{:S(2)}, u32[]{:S(2)}) collective-permute-start(f32[2,34,8,128]{3,2,1,0:T(8,128)S(1)} %get-tuple-element.17.col2), channel_id=1, source_target_pairs={{0,4},{4,8},{8,12},{12,16},{16,20},{20,24},{24,28},{28,0},{1,5},{5... | collective-permute-start | bytes 835592 | tf_op jit(solution)/shard_map/ppermute | solution.py:38
  4.5 3.1 %collective-permute-start.4 = (f32[2,34,8,128]{3,2,1,0:T(8,128)S(1)}, f32[2,34,8,128]{3,2,1,0:T(8,128)S(1)}, u32[]{:S(2)}, u32[]{:S(2)}) collective-permute-start(f32[2,34,8,128]{3,2,1,0:T(8,128)S(1)} %get-tuple-element.15.col0), channel_id=1, source_target_pairs={{0,28},{4,0},{8,4},{12,8},{16,12},{20,16},{24,20},{28,24},{1,29},{... | collective-permute-start | bytes 835592 | tf_op jit(solution)/shard_map/ppermute | solution.py:38
  7.6 1.6 %collective-permute-start.2 = (f32[208,128]{1,0:T(8,128)S(1)}, f32[208,128]{1,0:T(8,128)S(1)}, u32[]{:S(2)}, u32[]{:S(2)}) collective-permute-start(f32[208,128]{1,0:T(8,128)S(1)} %get-tuple-element.18.own), channel_id=1, source_target_pairs={{0,2},{1,3},{2,0},{3,1},{4,6},{5,7},{6,4},{7,5},{8,10},{9,11},{10,... | collective-permute-start | bytes 319496 | tf_op jit(solution)/shard_map/ppermute | solution.py:43
  9.2 0.0 collective-permute-start.1
  9.2 3.1 %collective-permute-done.2.second = f32[208,128]{1,0:T(8,128)S(1)} collective-permute-done((f32[208,128]{1,0:T(8,128)S(1)}, f32[208,128]{1,0:T(8,128)S(1)}, u32[]{:S(2)}, u32[]{:S(2)}) %collective-permute-start.2) | collective-permute-done | bytes 106528 | tf_op jit(solution)/shard_map/ppermute | solution.py:43
  12.3 0.0 collective-permute-start.3
  12.3 0.0 copy-start
  12.3 1.0 %copy-done = s32[2,2,3,34,256]{4,1,3,2,0:T(2,128)S(1)} copy-done((s32[2,2,3,34,256]{4,1,3,2,0:T(2,128)S(1)}, s32[2,2,3,34,256]{4,1,3,2,0:T(2,128)}, u32[]{:S(2)}) %copy-start) | copy-done | bytes 417816
  13.3 0.5 %shard_map.74.also.turn = f32[2,2,3,34,8,128]{5,4,3,2,1,0:T(8,128)S(1)} custom-call(s32[2,3,136,128]{3,2,1,0:T(8,128)S(1)} %bitcast.21), custom_call_target="tpu_custom_call" | custom-call | flops 1000000 | bytes 1000000 | tf_op jit(solution)/shard_map/pallas_call | solution.py:47
  13.8 0.0 collective-permute-done.1.first
  13.8 0.0 collective-permute-done.3.third
  13.8 2.6 %collective-permute-done.before.west_halo = f32[2,34,8,128]{3,2,1,0:T(8,128)S(1)} collective-permute-done((f32[2,34,8,128]{3,2,1,0:T(8,128)S(1)}, f32[2,34,8,128]{3,2,1,0:T(8,128)S(1)}, u32[]{:S(2)}, u32[]{:S(2)}) %collective-permute-start) | collective-permute-done | bytes 278560 | tf_op jit(solution)/shard_map/ppermute | solution.py:38
  16.4 0.7 %shard_map.75 = (f32[4,3,34,8,128]{4,3,2,1,0:T(8,128)S(1)}, f32[3,3,34,8,128]{4,3,2,1,0:T(8,128)S(1)}, f32[68,128]{1,0:T(8,128)S(1)}) custom-call(f32[208,128]{1,0:T(8,128)S(1)} %get-tuple-element.18.own, f32[208,128]{1,0:T(8,128)S(1)} %collective-permute-done.1.first, f32[208,128]{1,0:T(8,128)S(1)} %collective-permute-done.2.second, ...), custom_call_target="tpu_custom_call" | custom-call | flops 1000000 | bytes 1000000 | tf_op jit(solution)/shard_map/pallas_call | solution.py:47
  17.1 5.6 %collective-permute-start.5 = (f32[68,128]{1,0:T(8,128)S(1)}, f32[68,128]{1,0:T(8,128)S(1)}, u32[]{:S(2)}, u32[]{:S(2)}) collective-permute-start(f32[68,128]{1,0:T(8,128)S(1)} %get-tuple-element.22), channel_id=1, source_target_pairs={{0,28},{4,0},{8,4},{12,8},{16,12},{20,16},{24,20},{28,24},{1,29},{... | collective-permute-start | bytes 104456 | tf_op jit(solution)/shard_map/ppermute | solution.py:38
  22.6 0.8 %shard_map.76.before.mid0 = f32[2,34,8,128]{3,2,1,0:T(8,128)S(1)} custom-call(f32[2,34,8,128]{3,2,1,0:T(8,128)S(1)} %get-tuple-element.15.col0, f32[2,34,8,128]{3,2,1,0:T(8,128)S(1)} %get-tuple-element.16.col1, f32[2,34,8,128]{3,2,1,0:T(8,128)S(1)} %collective-permute-done.before.west_halo, f32[4,3,34,8,128]{4,3,2,1,0:T(8,128)S(1)} %get-tuple-element.20.rates, ...), custom_call_target="tpu_custom_call" | custom-call | flops 1000000 | bytes 1000000 | tf_op jit(solution)/shard_map/pallas_call | solution.py:47
  23.4 0.1 collective-permute-start.6
  23.5 0.0 collective-permute-done.4.east_halo
  23.5 1.0 %collective-permute-done.5.face = f32[68,128]{1,0:T(8,128)S(1)} collective-permute-done((f32[68,128]{1,0:T(8,128)S(1)}, f32[68,128]{1,0:T(8,128)S(1)}, u32[]{:S(2)}, u32[]{:S(2)}) %collective-permute-start.5) | collective-permute-done | bytes 34848 | tf_op jit(solution)/shard_map/ppermute | solution.py:38
  24.5 0.8 %shard_map.78 = (f32[2,34,8,128]{3,2,1,0:T(8,128)S(1)}, f32[34,8,128]{2,1,0:T(8,128)S(1)}) custom-call(f32[2,34,8,128]{3,2,1,0:T(8,128)S(1)} %get-tuple-element.16.col1, f32[2,34,8,128]{3,2,1,0:T(8,128)S(1)} %get-tuple-element.17.col2, f32[2,34,8,128]{3,2,1,0:T(8,128)S(1)} %collective-permute-done.4.east_halo, f32[68,128]{1,0:T(8,128)S(1)} %collective-permute-done.5.face, ...), custom_call_target="tpu_custom_call" | custom-call | flops 1000000 | bytes 1000000 | tf_op jit(solution)/shard_map/pallas_call | solution.py:47
  25.3 1.1 %collective-permute-start.7 = (f32[2,34,8,128]{3,2,1,0:T(8,128)S(1)}, f32[2,34,8,128]{3,2,1,0:T(8,128)S(1)}, u32[]{:S(2)}, u32[]{:S(2)}) collective-permute-start(f32[2,34,8,128]{3,2,1,0:T(8,128)S(1)} %get-tuple-element.23.mid2), channel_id=1, source_target_pairs={{0,4},{4,8},{8,12},{12,16},{16,20},{20,24},{24,28},{28,0},{1,5},{5... | collective-permute-start | bytes 835592 | tf_op jit(solution)/shard_map/ppermute | solution.py:38
  26.4 0.8 %shard_map.77.mid1 = f32[2,34,8,128]{3,2,1,0:T(8,128)S(1)} custom-call(f32[2,34,8,128]{3,2,1,0:T(8,128)S(1)} %get-tuple-element.15.col0, f32[2,34,8,128]{3,2,1,0:T(8,128)S(1)} %get-tuple-element.16.col1, f32[2,34,8,128]{3,2,1,0:T(8,128)S(1)} %get-tuple-element.17.col2, f32[4,3,34,8,128]{4,3,2,1,0:T(8,128)S(1)} %get-tuple-element.20.rates, ...), custom_call_target="tpu_custom_call" | custom-call | flops 1000000 | bytes 1000000 | tf_op jit(solution)/shard_map/pallas_call | solution.py:47
  27.2 0.9 %shard_map.79.begun = f32[2,3,34,8,128]{4,3,2,1,0:T(8,128)} custom-call(f32[2,34,8,128]{3,2,1,0:T(8,128)S(1)} %shard_map.76.before.mid0, f32[2,34,8,128]{3,2,1,0:T(8,128)S(1)} %shard_map.77.mid1, f32[2,34,8,128]{3,2,1,0:T(8,128)S(1)} %get-tuple-element.23.mid2, f32[4,3,34,8,128]{4,3,2,1,0:T(8,128)S(1)} %get-tuple-element.20.rates, ...), custom_call_target="tpu_custom_call" | custom-call | flops 1000000 | bytes 1000000 | tf_op jit(solution)/shard_map/pallas_call | solution.py:47
  28.1 8.6 %collective-permute-done.6.halo = f32[2,34,8,128]{3,2,1,0:T(8,128)S(1)} collective-permute-done((f32[2,34,8,128]{3,2,1,0:T(8,128)S(1)}, f32[2,34,8,128]{3,2,1,0:T(8,128)S(1)}, u32[]{:S(2)}, u32[]{:S(2)}) %collective-permute-start.6) | collective-permute-done | bytes 278560 | tf_op jit(solution)/shard_map/ppermute | solution.py:38
  36.7 0.9 %shard_map.80.begun = f32[2,3,34,8,128]{4,3,2,1,0:T(8,128)} custom-call(f32[2,3,34,8,128]{4,3,2,1,0:T(8,128)} %shard_map.79.begun, f32[2,34,8,128]{3,2,1,0:T(8,128)S(1)} %shard_map.77.mid1, f32[2,34,8,128]{3,2,1,0:T(8,128)S(1)} %get-tuple-element.23.mid2, f32[2,34,8,128]{3,2,1,0:T(8,128)S(1)} %collective-permute-done.6.halo, ...), custom_call_target="tpu_custom_call", output_to_operand_aliasing={{}: (0, {})} | custom-call | flops 1000000 | bytes 1000000 | tf_op jit(solution)/shard_map/pallas_call | solution.py:47
  37.6 0.0 collective-permute-done.7.halo
  37.6 0.9 %shard_map.81 = f32[2,3,34,8,128]{4,3,2,1,0:T(8,128)} custom-call(f32[2,3,34,8,128]{4,3,2,1,0:T(8,128)} %shard_map.80.begun, f32[2,34,8,128]{3,2,1,0:T(8,128)S(1)} %shard_map.76.before.mid0, f32[2,34,8,128]{3,2,1,0:T(8,128)S(1)} %shard_map.77.mid1, f32[2,34,8,128]{3,2,1,0:T(8,128)S(1)} %collective-permute-done.7.halo, ...), custom_call_target="tpu_custom_call", output_to_operand_aliasing={{}: (0, {})} | custom-call | flops 1000000 | bytes 1000000 | tf_op jit(solution)/shard_map/pallas_call | solution.py:47
Async XLA Ops:
  1.5 14.9 %collective-permute-start = (f32[2,34,8,128]{3,2,1,0:T(8,128)S(1)}, f32[2,34,8,128]{3,2,1,0:T(8,128)S(1)}, u32[]{:S(2)}, u32[]{:S(2)}) collective-permute-start(f32[2,34,8,128]{3,2,1,0:T(8,128)S(1)} %get-tuple-element.17.col2), channel_id=1, source_target_pairs={{0,4},{4,8},{8,12},{12,16},{16,20},{20,24},{24,28},{28,0},{1,5},{5... | collective-permute-start | bytes 835592 | tf_op jit(solution)/shard_map/ppermute | solution.py:38
  4.5 19.0 %collective-permute-start.4 = (f32[2,34,8,128]{3,2,1,0:T(8,128)S(1)}, f32[2,34,8,128]{3,2,1,0:T(8,128)S(1)}, u32[]{:S(2)}, u32[]{:S(2)}) collective-permute-start(f32[2,34,8,128]{3,2,1,0:T(8,128)S(1)} %get-tuple-element.15.col0), channel_id=1, source_target_pairs={{0,28},{4,0},{8,4},{12,8},{16,12},{20,16},{24,20},{28,24},{1,29},{... | collective-permute-start | bytes 835592 | tf_op jit(solution)/shard_map/ppermute | solution.py:38
  7.6 4.7 %collective-permute-start.2 = (f32[208,128]{1,0:T(8,128)S(1)}, f32[208,128]{1,0:T(8,128)S(1)}, u32[]{:S(2)}, u32[]{:S(2)}) collective-permute-start(f32[208,128]{1,0:T(8,128)S(1)} %get-tuple-element.18.own), channel_id=1, source_target_pairs={{0,2},{1,3},{2,0},{3,1},{4,6},{5,7},{6,4},{7,5},{8,10},{9,11},{10,... | collective-permute-start | bytes 319496 | tf_op jit(solution)/shard_map/ppermute | solution.py:43
  9.2 4.6 %collective-permute-start.1 = (f32[208,128]{1,0:T(8,128)S(1)}, f32[208,128]{1,0:T(8,128)S(1)}, u32[]{:S(2)}, u32[]{:S(2)}) collective-permute-start(f32[208,128]{1,0:T(8,128)S(1)} %get-tuple-element.18.own), channel_id=1, source_target_pairs={{0,1},{1,0},{2,3},{3,2},{4,5},{5,4},{6,7},{7,6},{8,9},{9,8},{10,11... | collective-permute-start | bytes 319496 | tf_op jit(solution)/shard_map/ppermute | solution.py:43
  12.3 1.5 %collective-permute-start.3 = (f32[208,128]{1,0:T(8,128)S(1)}, f32[208,128]{1,0:T(8,128)S(1)}, u32[]{:S(2)}, u32[]{:S(2)}) collective-permute-start(f32[208,128]{1,0:T(8,128)S(1)} %collective-permute-done.2.second), channel_id=1, source_target_pairs={{0,1},{1,0},{2,3},{3,2},{4,5},{5,4},{6,7},{7,6},{8,9},{9,8},{10,11... | collective-permute-start | bytes 319496 | tf_op jit(solution)/shard_map/ppermute | solution.py:43
  12.3 1.0 %copy-start = (s32[2,2,3,34,256]{4,1,3,2,0:T(2,128)S(1)}, s32[2,2,3,34,256]{4,1,3,2,0:T(2,128)}, u32[]{:S(2)}) copy-start(s32[2,2,3,34,256]{4,1,3,2,0:T(2,128)} %param.8) | copy-start | bytes 1253380
  17.1 7.5 %collective-permute-start.5 = (f32[68,128]{1,0:T(8,128)S(1)}, f32[68,128]{1,0:T(8,128)S(1)}, u32[]{:S(2)}, u32[]{:S(2)}) collective-permute-start(f32[68,128]{1,0:T(8,128)S(1)} %get-tuple-element.22), channel_id=1, source_target_pairs={{0,28},{4,0},{8,4},{12,8},{16,12},{20,16},{24,20},{28,24},{1,29},{... | collective-permute-start | bytes 104456 | tf_op jit(solution)/shard_map/ppermute | solution.py:38
  23.4 13.3 %collective-permute-start.6 = (f32[2,34,8,128]{3,2,1,0:T(8,128)S(1)}, f32[2,34,8,128]{3,2,1,0:T(8,128)S(1)}, u32[]{:S(2)}, u32[]{:S(2)}) collective-permute-start(f32[2,34,8,128]{3,2,1,0:T(8,128)S(1)} %shard_map.76.before.mid0), channel_id=1, source_target_pairs={{0,28},{4,0},{8,4},{12,8},{16,12},{20,16},{24,20},{28,24},{1,29},{... | collective-permute-start | bytes 835592 | tf_op jit(solution)/shard_map/ppermute | solution.py:38
  25.3 12.3 %collective-permute-start.7 = (f32[2,34,8,128]{3,2,1,0:T(8,128)S(1)}, f32[2,34,8,128]{3,2,1,0:T(8,128)S(1)}, u32[]{:S(2)}, u32[]{:S(2)}) collective-permute-start(f32[2,34,8,128]{3,2,1,0:T(8,128)S(1)} %get-tuple-element.23.mid2), channel_id=1, source_target_pairs={{0,4},{4,8},{8,12},{12,16},{16,20},{20,24},{24,28},{28,0},{1,5},{5... | collective-permute-start | bytes 835592 | tf_op jit(solution)/shard_map/ppermute | solution.py:38

commit v5 on v3

--- a/solution.py
+++ b/solution.py
@@ -69,13 +69,14 @@
     return row == 0, row == slope
 
 
-def head_kernel(state, flags, mass, xf, yf, km, message, col1, col2, packed, flags_v, mass_v, xf_v, yf_v, km_v, sems, column_sems):
+def head_kernel(state, flags, mass, xf, yf, km, col0, message, col1, col2, packed, flags_v, mass_v, xf_v, yf_v, km_v, sems, column_sems):
     tracers, columns, levels = state.shape[0], mass.shape[0], mass.shape[1]
     half = LANES // 2
     pairs = ((mass, mass_v), (xf, xf_v), (yf, yf_v), (km, km_v), (flags, flags_v))
     copies = [pltpu.make_async_copy(src, dst, sems.at[i]) for i, (src, dst) in enumerate(pairs)]
     for t in range(tracers):
-        for c, place in ((2, col2.at[t]), (0, message.at[pl.ds(t * levels, levels)]), (1, col1.at[t])):
+        first = message.at[pl.ds((t - 1) * levels, levels)] if t else col0.at[t]
+        for c, place in ((2, col2.at[t]), (0, first), (1, col1.at[t])):
             copies.append(pltpu.make_async_copy(state.at[t, c], place, column_sems.at[c, t]))
     for copy in copies:
         copy.start()
@@ -252,25 +253,23 @@
             out[t, l] = values[t]
 
 
-def tiles(ref, levels):
-    if len(ref.shape) == 4:
+def tiles(ref, message=None):
+    if message is None:
         return lambda t, l: ref[t, l]
-    return lambda t, l: ref[(t * levels + l) * 8 : (t * levels + l + 1) * 8]
-
-
-def west_kernel(message, col1, west_halo, rates, factors, turn, out):
-    levels = out.shape[1]
-    middle(0, tiles(message, levels), tiles(col1, levels), tiles(west_halo, levels),
-           lambda l: rates[0, 0, l], rates, factors, turn, out)
-
-
-def inner_kernel(message, col1, col2, rates, factors, turn, out):
-    levels = out.shape[1]
-    middle(1, tiles(col1, levels), tiles(col2, levels), tiles(message, levels),
-           lambda l: rates[0, 1, l], rates, factors, turn, out)
-
-
-def east_kernel(col1, col2, halo, rates, factors, turn, before, out, east):
+    levels = ref.shape[1]
+    start = lambda t, l: ((t - 1) * levels + l) * 8
+    return lambda t, l: message[start(t, l) : start(t, l) + 8] if t else ref[0, l]
+
+
+def west_kernel(col0, message, col1, west_halo, rates, factors, turn, out):
+    middle(0, tiles(col0, message), tiles(col1), tiles(west_halo), lambda l: rates[0, 0, l], rates, factors, turn, out)
+
+
+def inner_kernel(col0, message, col1, col2, rates, factors, turn, out):
+    middle(1, tiles(col1), tiles(col2), tiles(col0, message), lambda l: rates[0, 1, l], rates, factors, turn, out)
+
+
+def east_kernel(col1, col2, halo0, halo, rates, factors, turn, before, out, east):
     levels = out.shape[1]
     upper_block = lax.broadcasted_iota(jnp.int32, (8, LANES), 0) >= MOMENTS
     rows = [face_row(halo.shape[0], levels, b) for b in range(2)]
@@ -280,7 +279,7 @@
         east[l] = jnp.maximum(flux, 0.0) * rates[0, 2, l]
         return east[l]
 
-    middle(2, tiles(col2, levels), tiles(halo, levels), tiles(col1, levels), east_rate, rates, factors, turn, out)
+    middle(2, tiles(col2), tiles(halo0, halo), tiles(col1), east_rate, rates, factors, turn, out)
 
 
 def finish(c, own, east_side, west_side, east_rate, rates, turn, out, buf, sems):
@@ -323,16 +322,17 @@
     order = lax.axis_index("trc").astype(jnp.int32).reshape(1)
     column = f32(tracers, levels, 8, LANES)
     rows = -(-2 * columns * levels // 8) * 8
-    length = tracers * levels + -(-2 * levels // 8)
+    length = (tracers - 1) * levels + -(-2 * levels // 8)
     dma = pltpu.SemaphoreType.DMA
     fields = tuple(stay(x) for x in (air_mass, x_flux, y_flux, vertical_mixing))
 
-    message, col1, col2, packed, flag = call(
+    col0, message, col1, col2, packed, flag = call(
         head_kernel,
-        (f32(length, 8, LANES), column, column, f32(rows, LANES), jax.ShapeDtypeStruct(flag.shape, flag.dtype)),
+        (f32(1, levels, 8, LANES), f32(length, 8, LANES), column, column, f32(rows, LANES), jax.ShapeDtypeStruct(flag.shape, flag.dtype)),
         (HBM,) * 6, [pltpu.VMEM(x.shape, x.dtype) for x in fields] + [dma((5,)), dma((columns, tracers))],
         10**5, 10**6, stay(state), stay(flag), *fields)
     west_halo = shifted(col2, "lon", 1)
+    east_halo = shifted(col0, "lon", -1)
     across = swapped(packed, "trc", 2)
     others = [swapped(packed, "trc", 1), across, swapped(across, "trc", 1)]
     turn = call(turn_kernel, f32(2, tracers, columns, levels, 8, LANES), (VMEM,), (), 10**6, 10**6, switch)
@@ -340,14 +340,14 @@
         pre_kernel,
         (f32(4, columns, levels, 8, LANES), f32(3, columns, levels, 8, LANES), f32(length * 8, LANES)),
         (VMEM,) * 5 + (SMEM, VMEM, VMEM, VMEM), [pltpu.VMEM((4, columns, 2, levels, LANES), jnp.float32)],
-        10**6, 10**6, packed, *others, flag, order, message.reshape(length * 8, LANES), west_halo, turn, aliases={6: 2})
+        10**6, 10**6, packed, *others, flag, order, message.reshape(length * 8, LANES), east_halo, turn, aliases={6: 2})
     east_message = shifted(message, "lon", -1)
-    mid0 = call(west_kernel, column, (VMEM,) * 6, (), 10**6, 10**6, message, col1, west_halo, rates, factors, turn)
-    east_halo = shifted(mid0, "lon", -1)
-    mid1 = call(inner_kernel, column, (VMEM,) * 6, (), 10**6, 10**6, message, col1, col2, rates, factors, turn)
-    mid2, east = call(east_kernel, (column, f32(levels, 8, LANES)), (VMEM,) * 7, (), 10**6, 10**6,
-                      col1, col2, east_message, rates, factors, turn, mid0)
-    west_halo = shifted(mid2, "lon", 1)
+    mid0 = call(west_kernel, column, (VMEM,) * 7, (), 10**6, 10**6, col0, message, col1, west_halo, rates, factors, turn)
+    east_mid = shifted(mid0, "lon", -1)
+    mid1 = call(inner_kernel, column, (VMEM,) * 7, (), 10**6, 10**6, col0, message, col1, col2, rates, factors, turn)
+    mid2, east = call(east_kernel, (column, f32(levels, 8, LANES)), (VMEM,) * 8, (), 10**6, 10**6,
+                      col1, col2, east_halo, east_message, rates, factors, turn, mid0)
+    west_mid = shifted(mid2, "lon", 1)
 
     def last(kernel, aliases, *args):
         first = (HBM,) * len(aliases)
@@ -356,8 +356,8 @@
                     *args, out_specs=HBM, aliases=aliases)
 
     out = last(last_inner_kernel, {}, mid0, mid1, mid2, rates, turn)
-    out = last(last_east_kernel, {0: 0}, out, mid1, mid2, east_halo, east, rates, turn)
-    out = last(last_west_kernel, {0: 0}, out, mid0, mid1, west_halo, rates, turn)
+    out = last(last_east_kernel, {0: 0}, out, mid1, mid2, east_mid, east, rates, turn)
+    out = last(last_west_kernel, {0: 0}, out, mid0, mid1, west_mid, rates, turn)
     return state_back(out)
 
 

time: 36.6 us -> 40.5 us (1.11)
  starting transfers between devices: 7.82 us -> 19.2 us
  waiting for transfers between devices: 19.8 us -> 12.2 us
    ppermute x4 -> x5, starting transfers between devices: 6.33 us -> 15.7 us  [shifted(): lax.ppermute(value, axis, [(i, (i + by) % count) for i in range(count)])]
    ppermute x4 -> x5, waiting for transfers between devices: 16.5 us -> 12.2 us  [shifted(): lax.ppermute(value, axis, [(i, (i + by) % count) for i in range(count)])]
    ppermute x3, waiting for transfers between devices: 3.22 us -> 0.01 us  [swapped(): return lax.ppermute(value, axis, [(i, i ^ mask) for i in range(count)])]
    ppermute x3, starting transfers between devices: 1.5 us -> 3.51 us  [swapped(): return lax.ppermute(value, axis, [(i, i ^ mask) for i in range(count)])]
  transfers between devices with their start and end apart: 7 -> 8, of which waited for: 5 -> 4; matrix products, arithmetic and copies ran while one was open for 0% -> 0% of each run, Pallas kernels for 13% -> 13%
where the time goes in v5:
time: 40.5 us; the launch traced here: 40.3 us
  starting transfers between devices  19.2 us (47%)
  waiting for transfers between devices  12.2 us (30%)
  Pallas kernels  7.8 us (19%)
  local copies, waits for them, and re-layouts  1 us (2%)
    ppermute x5, starting transfers between devices, shifted(): lax.ppermute(value, axis, [(i, (i + by) % count) for i in range(count)])  15.7 us
    ppermute x5, waiting for transfers between devices, shifted(): lax.ppermute(value, axis, [(i, (i + by) % count) for i in range(count)])  12.2 us
    pallas_call x9, Pallas kernels, call(): pl.pallas_call(kernel, out_shape=out, in_specs=in_specs, out_specs=jax.tr...  7.8 us
    ppermute x3, starting transfers between devices, swapped(): return lax.ppermute(value, axis, [(i, i ^ mask) for i in range(count)])  3.51 us
    unnamed x2, local copies, waits for them, and re-layouts  1 us
  transfers between devices with their start and end apart: 8, of which 4 were waited for; matrix products, arithmetic and copies ran while one was open for 0% of the time, Pallas kernels for 13%

profile of v5, /device:TPU:0, one launch (start us, length us, event | category | flops | bytes accessed | tf_op | source)
XLA Modules:
  0.0 40.3 jit_solution(1165859707337113653)
XLA Ops:
  0.0 1.5 %shard_map.73 = (f32[1,34,8,128]{3,2,1,0:T(8,128)S(1)}, f32[43,8,128]{2,1,0:T(8,128)S(1)}, f32[2,34,8,128]{3,2,1,0:T(8,128)S(1)}, f32[2,34,8,128]{3,2,1,0:T(8,12...) custom-call(f32[2,3,34,8,128]{4,3,2,1,0:T(8,128)} %bitcast.24, s32[3,136,128]{2,1,0:T(8,128)} %bitcast.25, ...), custom_call_target="tpu_custom_call" | custom-call | flops 100000 | bytes 1000000 | tf_op jit(solution)/shard_map/pallas_call | solution.py:47
  1.5 3.0 %collective-permute-start.1 = (f32[208,128]{1,0:T(8,128)S(1)}, f32[208,128]{1,0:T(8,128)S(1)}, u32[]{:S(2)}, u32[]{:S(2)}) collective-permute-start(f32[208,128]{1,0:T(8,128)S(1)} %get-tuple-element.17.own), channel_id=1, source_target_pairs={{0,2},{1,3},{2,0},{3,1},{4,6},{5,7},{6,4},{7,5},{8,10},{9,11},{10,... | collective-permute-start | bytes 319496 | tf_op jit(solution)/shard_map/ppermute | solution.py:43
  4.5 4.6 %collective-permute-start.3 = (f32[1,34,8,128]{3,2,1,0:T(8,128)S(1)}, f32[1,34,8,128]{3,2,1,0:T(8,128)S(1)}, u32[]{:S(2)}, u32[]{:S(2)}) collective-permute-start(f32[1,34,8,128]{3,2,1,0:T(8,128)S(1)} %get-tuple-element.16.col0), channel_id=1, source_target_pairs={{0,28},{4,0},{8,4},{12,8},{16,12},{20,16},{24,20},{28,24},{1,29},{... | collective-permute-start | bytes 417800 | tf_op jit(solution)/shard_map/ppermute | solution.py:38
  9.0 0.0 collective-permute-start
  9.0 0.0 collective-permute-done.1.second
  9.0 0.5 %collective-permute-start.2 = (f32[208,128]{1,0:T(8,128)S(1)}, f32[208,128]{1,0:T(8,128)S(1)}, u32[]{:S(2)}, u32[]{:S(2)}) collective-permute-start(f32[208,128]{1,0:T(8,128)S(1)} %collective-permute-done.1.second), channel_id=1, source_target_pairs={{0,1},{1,0},{2,3},{3,2},{4,5},{5,4},{6,7},{7,6},{8,9},{9,8},{10,11... | collective-permute-start | bytes 319496 | tf_op jit(solution)/shard_map/ppermute | solution.py:43
  9.5 0.0 collective-permute-start.4
  9.5 0.0 copy-start
  9.5 1.0 %copy-done = s32[2,2,3,34,256]{4,1,3,2,0:T(2,128)S(1)} copy-done((s32[2,2,3,34,256]{4,1,3,2,0:T(2,128)S(1)}, s32[2,2,3,34,256]{4,1,3,2,0:T(2,128)}, u32[]{:S(2)}) %copy-start) | copy-done | bytes 417816
  10.5 0.5 %shard_map.74.also.turn = f32[2,2,3,34,8,128]{5,4,3,2,1,0:T(8,128)S(1)} custom-call(s32[2,3,136,128]{3,2,1,0:T(8,128)S(1)} %bitcast.23), custom_call_target="tpu_custom_call" | custom-call | flops 1000000 | bytes 1000000 | tf_op jit(solution)/shard_map/pallas_call | solution.py:47
  11.0 0.0 collective-permute-done.first
  11.0 0.6 %collective-permute-done.3.before.halo0 = f32[1,34,8,128]{3,2,1,0:T(8,128)S(1)} collective-permute-done((f32[1,34,8,128]{3,2,1,0:T(8,128)S(1)}, f32[1,34,8,128]{3,2,1,0:T(8,128)S(1)}, u32[]{:S(2)}, u32[]{:S(2)}) %collective-permute-start.3) | collective-permute-done | bytes 139296 | tf_op jit(solution)/shard_map/ppermute | solution.py:38
  11.7 0.0 collective-permute-done.2.third
  11.7 0.7 %shard_map.75 = (f32[4,3,34,8,128]{4,3,2,1,0:T(8,128)S(1)}, f32[3,3,34,8,128]{4,3,2,1,0:T(8,128)S(1)}, f32[344,128]{1,0:T(8,128)S(1)}) custom-call(f32[208,128]{1,0:T(8,128)S(1)} %get-tuple-element.17.own, f32[208,128]{1,0:T(8,128)S(1)} %collective-permute-done.first, f32[208,128]{1,0:T(8,128)S(1)} %collective-permute-done.1.second, ...), custom_call_target="tpu_custom_call", output_to_operand_aliasing={{2}: (6, {})} | custom-call | flops 1000000 | bytes 1000000 | tf_op jit(solution)/shard_map/pallas_call | solution.py:47
  12.4 5.3 %collective-permute-start.5 = (f32[344,128]{1,0:T(8,128)S(1)}, f32[344,128]{1,0:T(8,128)S(1)}, u32[]{:S(2)}, u32[]{:S(2)}) collective-permute-start(f32[344,128]{1,0:T(8,128)S(1)} %get-tuple-element.20.message), channel_id=1, source_target_pairs={{0,28},{4,0},{8,4},{12,8},{16,12},{20,16},{24,20},{28,24},{1,29},{... | collective-permute-start | bytes 528392 | tf_op jit(solution)/shard_map/ppermute | solution.py:38
  17.7 3.2 %collective-permute-done.4.west_halo = f32[2,34,8,128]{3,2,1,0:T(8,128)S(1)} collective-permute-done((f32[2,34,8,128]{3,2,1,0:T(8,128)S(1)}, f32[2,34,8,128]{3,2,1,0:T(8,128)S(1)}, u32[]{:S(2)}, u32[]{:S(2)}) %collective-permute-start.4) | collective-permute-done | bytes 278560 | tf_op jit(solution)/shard_map/ppermute | solution.py:38
  20.9 0.8 %shard_map.76.before.mid0 = f32[2,34,8,128]{3,2,1,0:T(8,128)S(1)} custom-call(f32[1,34,8,128]{3,2,1,0:T(8,128)S(1)} %get-tuple-element.16.col0, f32[344,128]{1,0:T(8,128)S(1)} %get-tuple-element.20.message, f32[2,34,8,128]{3,2,1,0:T(8,128)S(1)} %get-tuple-element.21.col1, f32[2,34,8,128]{3,2,1,0:T(8,128)S(1)} %collective-permute-done.4.west_halo, ...), custom_call_target="tpu_custom_call" | custom-call | flops 1000000 | bytes 1000000 | tf_op jit(solution)/shard_map/pallas_call | solution.py:47
  21.7 5.7 %collective-permute-start.6 = (f32[2,34,8,128]{3,2,1,0:T(8,128)S(1)}, f32[2,34,8,128]{3,2,1,0:T(8,128)S(1)}, u32[]{:S(2)}, u32[]{:S(2)}) collective-permute-start(f32[2,34,8,128]{3,2,1,0:T(8,128)S(1)} %shard_map.76.before.mid0), channel_id=1, source_target_pairs={{0,28},{4,0},{8,4},{12,8},{16,12},{20,16},{24,20},{28,24},{1,29},{... | collective-permute-start | bytes 835592 | tf_op jit(solution)/shard_map/ppermute | solution.py:38
  27.4 0.0 collective-permute-done.5.halo
  27.4 0.8 %shard_map.78 = (f32[2,34,8,128]{3,2,1,0:T(8,128)S(1)}, f32[34,8,128]{2,1,0:T(8,128)S(1)}) custom-call(f32[2,34,8,128]{3,2,1,0:T(8,128)S(1)} %get-tuple-element.21.col1, f32[2,34,8,128]{3,2,1,0:T(8,128)S(1)} %get-tuple-element.22.col2, f32[1,34,8,128]{3,2,1,0:T(8,128)S(1)} %collective-permute-done.3.before.halo0, ...), custom_call_target="tpu_custom_call" | custom-call | flops 1000000 | bytes 1000000 | tf_op jit(solution)/shard_map/pallas_call | solution.py:47
  28.3 0.1 collective-permute-start.7
  28.3 0.8 %shard_map.77.mid1 = f32[2,34,8,128]{3,2,1,0:T(8,128)S(1)} custom-call(f32[1,34,8,128]{3,2,1,0:T(8,128)S(1)} %get-tuple-element.16.col0, f32[344,128]{1,0:T(8,128)S(1)} %get-tuple-element.20.message, f32[2,34,8,128]{3,2,1,0:T(8,128)S(1)} %get-tuple-element.21.col1, f32[2,34,8,128]{3,2,1,0:T(8,128)S(1)} %get-tuple-element.22.col2, ...), custom_call_target="tpu_custom_call" | custom-call | flops 1000000 | bytes 1000000 | tf_op jit(solution)/shard_map/pallas_call | solution.py:47
  29.1 0.9 %shard_map.79.begun = f32[2,3,34,8,128]{4,3,2,1,0:T(8,128)} custom-call(f32[2,34,8,128]{3,2,1,0:T(8,128)S(1)} %shard_map.76.before.mid0, f32[2,34,8,128]{3,2,1,0:T(8,128)S(1)} %shard_map.77.mid1, f32[2,34,8,128]{3,2,1,0:T(8,128)S(1)} %get-tuple-element.25.mid2, f32[4,3,34,8,128]{4,3,2,1,0:T(8,128)S(1)} %get-tuple-element.23.rates, ...), custom_call_target="tpu_custom_call" | custom-call | flops 1000000 | bytes 1000000 | tf_op jit(solution)/shard_map/pallas_call | solution.py:47
  30.1 3.5 %collective-permute-done.6.halo = f32[2,34,8,128]{3,2,1,0:T(8,128)S(1)} collective-permute-done((f32[2,34,8,128]{3,2,1,0:T(8,128)S(1)}, f32[2,34,8,128]{3,2,1,0:T(8,128)S(1)}, u32[]{:S(2)}, u32[]{:S(2)}) %collective-permute-start.6) | collective-permute-done | bytes 278560 | tf_op jit(solution)/shard_map/ppermute | solution.py:38
  33.6 0.9 %shard_map.80.begun = f32[2,3,34,8,128]{4,3,2,1,0:T(8,128)} custom-call(f32[2,3,34,8,128]{4,3,2,1,0:T(8,128)} %shard_map.79.begun, f32[2,34,8,128]{3,2,1,0:T(8,128)S(1)} %shard_map.77.mid1, f32[2,34,8,128]{3,2,1,0:T(8,128)S(1)} %get-tuple-element.25.mid2, f32[2,34,8,128]{3,2,1,0:T(8,128)S(1)} %collective-permute-done.6.halo, ...), custom_call_target="tpu_custom_call", output_to_operand_aliasing={{}: (0, {})} | custom-call | flops 1000000 | bytes 1000000 | tf_op jit(solution)/shard_map/pallas_call | solution.py:47
  34.5 4.9 %collective-permute-done.7.halo = f32[2,34,8,128]{3,2,1,0:T(8,128)S(1)} collective-permute-done((f32[2,34,8,128]{3,2,1,0:T(8,128)S(1)}, f32[2,34,8,128]{3,2,1,0:T(8,128)S(1)}, u32[]{:S(2)}, u32[]{:S(2)}) %collective-permute-start.7) | collective-permute-done | bytes 278560 | tf_op jit(solution)/shard_map/ppermute | solution.py:38
  39.4 0.9 %shard_map.81 = f32[2,3,34,8,128]{4,3,2,1,0:T(8,128)} custom-call(f32[2,3,34,8,128]{4,3,2,1,0:T(8,128)} %shard_map.80.begun, f32[2,34,8,128]{3,2,1,0:T(8,128)S(1)} %shard_map.76.before.mid0, f32[2,34,8,128]{3,2,1,0:T(8,128)S(1)} %shard_map.77.mid1, f32[2,34,8,128]{3,2,1,0:T(8,128)S(1)} %collective-permute-done.7.halo, ...), custom_call_target="tpu_custom_call", output_to_operand_aliasing={{}: (0, {})} | custom-call | flops 1000000 | bytes 1000000 | tf_op jit(solution)/shard_map/pallas_call | solution.py:47
Async XLA Ops:
  1.5 7.6 %collective-permute-start.1 = (f32[208,128]{1,0:T(8,128)S(1)}, f32[208,128]{1,0:T(8,128)S(1)}, u32[]{:S(2)}, u32[]{:S(2)}) collective-permute-start(f32[208,128]{1,0:T(8,128)S(1)} %get-tuple-element.17.own), channel_id=1, source_target_pairs={{0,2},{1,3},{2,0},{3,1},{4,6},{5,7},{6,4},{7,5},{8,10},{9,11},{10,... | collective-permute-start | bytes 319496 | tf_op jit(solution)/shard_map/ppermute | solution.py:43
  4.5 7.2 %collective-permute-start.3 = (f32[1,34,8,128]{3,2,1,0:T(8,128)S(1)}, f32[1,34,8,128]{3,2,1,0:T(8,128)S(1)}, u32[]{:S(2)}, u32[]{:S(2)}) collective-permute-start(f32[1,34,8,128]{3,2,1,0:T(8,128)S(1)} %get-tuple-element.16.col0), channel_id=1, source_target_pairs={{0,28},{4,0},{8,4},{12,8},{16,12},{20,16},{24,20},{28,24},{1,29},{... | collective-permute-start | bytes 417800 | tf_op jit(solution)/shard_map/ppermute | solution.py:38
  9.0 2.0 %collective-permute-start = (f32[208,128]{1,0:T(8,128)S(1)}, f32[208,128]{1,0:T(8,128)S(1)}, u32[]{:S(2)}, u32[]{:S(2)}) collective-permute-start(f32[208,128]{1,0:T(8,128)S(1)} %get-tuple-element.17.own), channel_id=1, source_target_pairs={{0,1},{1,0},{2,3},{3,2},{4,5},{5,4},{6,7},{7,6},{8,9},{9,8},{10,11... | collective-permute-start | bytes 319496 | tf_op jit(solution)/shard_map/ppermute | solution.py:43
  9.0 2.6 %collective-permute-start.2 = (f32[208,128]{1,0:T(8,128)S(1)}, f32[208,128]{1,0:T(8,128)S(1)}, u32[]{:S(2)}, u32[]{:S(2)}) collective-permute-start(f32[208,128]{1,0:T(8,128)S(1)} %collective-permute-done.1.second), channel_id=1, source_target_pairs={{0,1},{1,0},{2,3},{3,2},{4,5},{5,4},{6,7},{7,6},{8,9},{9,8},{10,11... | collective-permute-start | bytes 319496 | tf_op jit(solution)/shard_map/ppermute | solution.py:43
  9.5 11.4 %collective-permute-start.4 = (f32[2,34,8,128]{3,2,1,0:T(8,128)S(1)}, f32[2,34,8,128]{3,2,1,0:T(8,128)S(1)}, u32[]{:S(2)}, u32[]{:S(2)}) collective-permute-start(f32[2,34,8,128]{3,2,1,0:T(8,128)S(1)} %get-tuple-element.22.col2), channel_id=1, source_target_pairs={{0,4},{4,8},{8,12},{12,16},{16,20},{20,24},{24,28},{28,0},{1,5},{5... | collective-permute-start | bytes 835592 | tf_op jit(solution)/shard_map/ppermute | solution.py:38
  9.5 1.0 %copy-start = (s32[2,2,3,34,256]{4,1,3,2,0:T(2,128)S(1)}, s32[2,2,3,34,256]{4,1,3,2,0:T(2,128)}, u32[]{:S(2)}) copy-start(s32[2,2,3,34,256]{4,1,3,2,0:T(2,128)} %param.8) | copy-start | bytes 1253380
  12.4 15.1 %collective-permute-start.5 = (f32[344,128]{1,0:T(8,128)S(1)}, f32[344,128]{1,0:T(8,128)S(1)}, u32[]{:S(2)}, u32[]{:S(2)}) collective-permute-start(f32[344,128]{1,0:T(8,128)S(1)} %get-tuple-element.20.message), channel_id=1, source_target_pairs={{0,28},{4,0},{8,4},{12,8},{16,12},{20,16},{24,20},{28,24},{1,29},{... | collective-permute-start | bytes 528392 | tf_op jit(solution)/shard_map/ppermute | solution.py:38
  21.7 11.9 %collective-permute-start.6 = (f32[2,34,8,128]{3,2,1,0:T(8,128)S(1)}, f32[2,34,8,128]{3,2,1,0:T(8,128)S(1)}, u32[]{:S(2)}, u32[]{:S(2)}) collective-permute-start(f32[2,34,8,128]{3,2,1,0:T(8,128)S(1)} %shard_map.76.before.mid0), channel_id=1, source_target_pairs={{0,28},{4,0},{8,4},{12,8},{16,12},{20,16},{24,20},{28,24},{1,29},{... | collective-permute-start | bytes 835592 | tf_op jit(solution)/shard_map/ppermute | solution.py:38
  28.3 11.1 %collective-permute-start.7 = (f32[2,34,8,128]{3,2,1,0:T(8,128)S(1)}, f32[2,34,8,128]{3,2,1,0:T(8,128)S(1)}, u32[]{:S(2)}, u32[]{:S(2)}) collective-permute-start(f32[2,34,8,128]{3,2,1,0:T(8,128)S(1)} %get-tuple-element.25.mid2), channel_id=1, source_target_pairs={{0,4},{4,8},{8,12},{12,16},{16,20},{20,24},{24,28},{28,0},{1,5},{5... | collective-permute-start | bytes 835592 | tf_op jit(solution)/shard_map/ppermute | solution.py:38

commit v6 on v3

--- a/solution.py
+++ b/solution.py
@@ -7,6 +7,7 @@
 
 LANES = 128
 MOMENTS = 4
+PARTS = 4
 VMEM = pl.BlockSpec(memory_space=pltpu.VMEM)
 SMEM = pl.BlockSpec(memory_space=pltpu.SMEM)
 HBM = pl.BlockSpec(memory_space=pltpu.HBM)
@@ -117,24 +118,27 @@
                     turn[d, t, c, l] = jnp.where(moment == 0, take, jnp.where(moment == 1 + d, keep, 1.0))
 
 
-def pre_kernel(own, first, second, third, flags, order, begun, before, also, rates, factors, message, fields):
+def sorted_shards(refs, order, start, count):
+    odd, high = order[0] % 2 == 1, order[0] >= 2
+    a, b, c, d = (ref[start : start + count] for ref in refs)
+    a, b, c, d = (jnp.where(odd, b, a), jnp.where(odd, a, b), jnp.where(odd, d, c), jnp.where(odd, c, d))
+    return (jnp.where(high, c, a), jnp.where(high, d, b), jnp.where(high, a, c), jnp.where(high, b, d))
+
+
+def gate_kernel(message, before, out):
+    pass
+
+
+def pre_kernel(own, first, second, third, flags, order, begun, also, rates, factors, message, fields):
     columns, levels = rates.shape[1], rates.shape[2]
     half = LANES // 2
-    odd = order[0] % 2 == 1
-    high = order[0] >= 2
     lane = lax.broadcasted_iota(jnp.int32, (8, LANES), 1)
     row = lax.broadcasted_iota(jnp.int32, (8, LANES), 0)
     upper_block = row >= MOMENTS
     lane_low = lax.broadcasted_iota(jnp.int32, (levels, LANES), 1) < half
-
-    def sorted_shards(start, count):
-        a, b, c, d = (ref[start : start + count] for ref in (own, first, second, third))
-        a, b, c, d = (jnp.where(odd, b, a), jnp.where(odd, a, b), jnp.where(odd, d, c), jnp.where(odd, c, d))
-        return (jnp.where(high, c, a), jnp.where(high, d, b), jnp.where(high, a, c), jnp.where(high, b, d))
-
     for pair in range(2):
         for c in range(columns):
-            shards = sorted_shards((pair * columns + c) * levels, levels)
+            shards = sorted_shards((own, first, second, third), order, (pair * columns + c) * levels, levels)
             for b in range(2):
                 lo, hi = shards[2 * b], shards[2 * b + 1]
                 fields[2 * pair, c, b] = jnp.where(lane_low, lo, pltpu.roll(hi, half, 1))
@@ -288,8 +292,8 @@
     masks = tile_masks(1)
     every = range(tracers)
     copies = []
-    for part in range(2):
-        low, high = part * levels // 2, (part + 1) * levels // 2
+    for part in range(PARTS):
+        low, high = part * levels // PARTS, (part + 1) * levels // PARTS
         for l in range(low, high):
             values = advect(*([side[t, l] for t in every] for side in (own, east_side, west_side)),
                             east_rate(l), rates[1, c, l], [turn[0, t, c, l] for t in every], 1, masks)
@@ -339,8 +343,9 @@
     rates, factors, message = call(
         pre_kernel,
         (f32(4, columns, levels, 8, LANES), f32(3, columns, levels, 8, LANES), f32(length * 8, LANES)),
-        (VMEM,) * 5 + (SMEM, VMEM, VMEM, VMEM), [pltpu.VMEM((4, columns, 2, levels, LANES), jnp.float32)],
-        10**6, 10**6, packed, *others, flag, order, message.reshape(length * 8, LANES), west_halo, turn, aliases={6: 2})
+        (VMEM,) * 5 + (SMEM,) + (VMEM,) * 2, [pltpu.VMEM((4, columns, 2, levels, LANES), jnp.float32)], 1, 1,
+        packed, *others, flag, order, message.reshape(length * 8, LANES), turn, aliases={6: 2})
+    message = call(gate_kernel, f32(length * 8, LANES), (VMEM,) * 2, (), 1, 1, message, west_halo, aliases={0: 0})
     east_message = shifted(message, "lon", -1)
     mid0 = call(west_kernel, column, (VMEM,) * 6, (), 10**6, 10**6, message, col1, west_halo, rates, factors, turn)
     east_halo = shifted(mid0, "lon", -1)
@@ -352,7 +357,7 @@
     def last(kernel, aliases, *args):
         first = (HBM,) * len(aliases)
         return call(kernel, f32(*state.shape), first + (VMEM,) * (len(args) - len(first)),
-                    [pltpu.VMEM(column.shape, jnp.float32), dma((2, tracers))], 10**6, 10**6,
+                    [pltpu.VMEM(column.shape, jnp.float32), dma((PARTS, tracers))], 10**6, 10**6,
                     *args, out_specs=HBM, aliases=aliases)
 
     out = last(last_inner_kernel, {}, mid0, mid1, mid2, rates, turn)

time: 36.6 us -> 35.8 us (0.978)
  waiting for transfers between devices: 19.8 us -> 19 us
    ppermute x4, waiting for transfers between devices: 16.5 us -> 15.8 us  [shifted(): lax.ppermute(value, axis, [(i, (i + by) % count) for i in range(count)])]
    pallas_call x9 -> x10, Pallas kernels: 7.76 us -> 7.82 us  [call(): pl.pallas_call(kernel, out_shape=out, in_specs=in_specs, out_specs=jax.tr...]
  transfers between devices with their start and end apart: 7 -> 7, of which waited for: 5 -> 5; matrix products, arithmetic and copies ran while one was open for 0% -> 0% of each run, Pallas kernels for 13% -> 15%
where the time goes in v6:
time: 35.8 us; the launch traced here: 35.7 us
  waiting for transfers between devices  19 us (53%)
  Pallas kernels  7.82 us (22%)
  starting transfers between devices  7.77 us (22%)
  local copies, waits for them, and re-layouts  1 us (3%)
    ppermute x4, waiting for transfers between devices, shifted(): lax.ppermute(value, axis, [(i, (i + by) % count) for i in range(count)])  15.8 us
    pallas_call x10, Pallas kernels, call(): pl.pallas_call(kernel, out_shape=out, in_specs=in_specs, out_specs=jax.tr...  7.82 us
    ppermute x4, starting transfers between devices, shifted(): lax.ppermute(value, axis, [(i, (i + by) % count) for i in range(count)])  6.28 us
    ppermute x3, waiting for transfers between devices, swapped(): return lax.ppermute(value, axis, [(i, i ^ mask) for i in range(count)])  3.22 us
    ppermute x3, starting transfers between devices, swapped(): return lax.ppermute(value, axis, [(i, i ^ mask) for i in range(count)])  1.5 us
    unnamed x2, local copies, waits for them, and re-layouts  1 us
  transfers between devices with their start and end apart: 7, of which 5 were waited for; matrix products, arithmetic and copies ran while one was open for 0% of the time, Pallas kernels for 15%

profile of v6, /device:TPU:0, one launch (start us, length us, event | category | flops | bytes accessed | tf_op | source)
XLA Modules:
  0.0 35.7 jit_solution(15778335012289333112)
XLA Ops:
  0.0 1.5 %shard_map.73 = (f32[77,8,128]{2,1,0:T(8,128)S(1)}, f32[2,34,8,128]{3,2,1,0:T(8,128)S(1)}, f32[2,34,8,128]{3,2,1,0:T(8,128)S(1)}, f32[208,128]{1,0:T(8,128)S(1)}, s32[3,136,128]{2,1,0:T(8,128)S(1)}) custom-call(f32[2,3,34,8,128]{4,3,2,1,0:T(8,128)} %bitcast.24, s32[3,136,128]{2,1,0:T(8,128)} %bitcast.25, f32[3,34,64]{2,1,0:T(8,128)} %mass.1, ...), custom_call_target="tpu_custom_call" | custom-call | flops 100000 | bytes 1000000 | tf_op jit(solution)/shard_map/pallas_call | solution.py:48
  1.5 3.0 %collective-permute-start.3 = (f32[2,34,8,128]{3,2,1,0:T(8,128)S(1)}, f32[2,34,8,128]{3,2,1,0:T(8,128)S(1)}, u32[]{:S(2)}, u32[]{:S(2)}) collective-permute-start(f32[2,34,8,128]{3,2,1,0:T(8,128)S(1)} %get-tuple-element.19.col2), channel_id=1, source_target_pairs={{0,4},{4,8},{8,12},{12,16},{16,20},{20,24},{24,28},{28,0},{1,5},{5... | collective-permute-start | bytes 835592 | tf_op jit(solution)/shard_map/ppermute | solution.py:39
  4.5 1.5 %collective-permute-start.1 = (f32[208,128]{1,0:T(8,128)S(1)}, f32[208,128]{1,0:T(8,128)S(1)}, u32[]{:S(2)}, u32[]{:S(2)}) collective-permute-start(f32[208,128]{1,0:T(8,128)S(1)} %get-tuple-element.15.own), channel_id=1, source_target_pairs={{0,2},{1,3},{2,0},{3,1},{4,6},{5,7},{6,4},{7,5},{8,10},{9,11},{10,... | collective-permute-start | bytes 319496 | tf_op jit(solution)/shard_map/ppermute | solution.py:44
  6.0 0.0 collective-permute-start
  6.0 3.2 %collective-permute-done.1.second = f32[208,128]{1,0:T(8,128)S(1)} collective-permute-done((f32[208,128]{1,0:T(8,128)S(1)}, f32[208,128]{1,0:T(8,128)S(1)}, u32[]{:S(2)}, u32[]{:S(2)}) %collective-permute-start.1) | collective-permute-done | bytes 106528 | tf_op jit(solution)/shard_map/ppermute | solution.py:44
  9.2 0.0 collective-permute-start.2
  9.2 0.0 copy-start
  9.2 1.0 %copy-done = s32[2,2,3,34,256]{4,1,3,2,0:T(2,128)S(1)} copy-done((s32[2,2,3,34,256]{4,1,3,2,0:T(2,128)S(1)}, s32[2,2,3,34,256]{4,1,3,2,0:T(2,128)}, u32[]{:S(2)}) %copy-start) | copy-done | bytes 417816
  10.2 0.5 %shard_map.74.also.turn = f32[2,2,3,34,8,128]{5,4,3,2,1,0:T(8,128)S(1)} custom-call(s32[2,3,136,128]{3,2,1,0:T(8,128)S(1)} %bitcast.23), custom_call_target="tpu_custom_call" | custom-call | flops 1000000 | bytes 1000000 | tf_op jit(solution)/shard_map/pallas_call | solution.py:48
  10.7 0.0 collective-permute-done.first
  10.7 0.0 collective-permute-done.2.third
  10.7 0.7 %shard_map.75 = (f32[4,3,34,8,128]{4,3,2,1,0:T(8,128)S(1)}, f32[3,3,34,8,128]{4,3,2,1,0:T(8,128)S(1)}, f32[616,128]{1,0:T(8,128)S(1)}) custom-call(f32[208,128]{1,0:T(8,128)S(1)} %get-tuple-element.15.own, f32[208,128]{1,0:T(8,128)S(1)} %collective-permute-done.first, f32[208,128]{1,0:T(8,128)S(1)} %collective-permute-done.1.second, ...), custom_call_target="tpu_custom_call", output_to_operand_aliasing={{2}: (6, {})} | custom-call | flops 1 | bytes 1 | tf_op jit(solution)/shard_map/pallas_call | solution.py:48
  11.4 2.8 %collective-permute-done.3.before.west_halo = f32[2,34,8,128]{3,2,1,0:T(8,128)S(1)} collective-permute-done((f32[2,34,8,128]{3,2,1,0:T(8,128)S(1)}, f32[2,34,8,128]{3,2,1,0:T(8,128)S(1)}, u32[]{:S(2)}, u32[]{:S(2)}) %collective-permute-start.3) | collective-permute-done | bytes 278560 | tf_op jit(solution)/shard_map/ppermute | solution.py:39
  14.2 1.7 %collective-permute-start.4 = (f32[616,128]{1,0:T(8,128)S(1)}, f32[616,128]{1,0:T(8,128)S(1)}, u32[]{:S(2)}, u32[]{:S(2)}) collective-permute-start(f32[616,128]{1,0:T(8,128)S(1)} %shard_map.76.message), channel_id=1, source_target_pairs={{0,28},{4,0},{8,4},{12,8},{16,12},{20,16},{24,20},{28,24},{1,29},{... | collective-permute-start | bytes 946184 | tf_op jit(solution)/shard_map/ppermute | solution.py:39
  15.9 0.8 %shard_map.77.before.mid0 = f32[2,34,8,128]{3,2,1,0:T(8,128)S(1)} custom-call(f32[616,128]{1,0:T(8,128)S(1)} %shard_map.76.message, f32[2,34,8,128]{3,2,1,0:T(8,128)S(1)} %get-tuple-element.20.col1, f32[2,34,8,128]{3,2,1,0:T(8,128)S(1)} %collective-permute-done.3.before.west_halo, f32[4,3,34,8,128]{4,3,2,1,0:T(8,128)S(1)} %get-tuple-element.21.rates, ...), custom_call_target="tpu_custom_call" | custom-call | flops 1000000 | bytes 1000000 | tf_op jit(solution)/shard_map/pallas_call | solution.py:48
  16.7 1.5 %collective-permute-start.5 = (f32[2,34,8,128]{3,2,1,0:T(8,128)S(1)}, f32[2,34,8,128]{3,2,1,0:T(8,128)S(1)}, u32[]{:S(2)}, u32[]{:S(2)}) collective-permute-start(f32[2,34,8,128]{3,2,1,0:T(8,128)S(1)} %shard_map.77.before.mid0), channel_id=1, source_target_pairs={{0,28},{4,0},{8,4},{12,8},{16,12},{20,16},{24,20},{28,24},{1,29},{... | collective-permute-start | bytes 835592 | tf_op jit(solution)/shard_map/ppermute | solution.py:39
  18.2 6.4 %collective-permute-done.4.halo = f32[616,128]{1,0:T(8,128)S(1)} collective-permute-done((f32[616,128]{1,0:T(8,128)S(1)}, f32[616,128]{1,0:T(8,128)S(1)}, u32[]{:S(2)}, u32[]{:S(2)}) %collective-permute-start.4) | collective-permute-done | bytes 315424 | tf_op jit(solution)/shard_map/ppermute | solution.py:39
  24.6 0.8 %shard_map.79 = (f32[2,34,8,128]{3,2,1,0:T(8,128)S(1)}, f32[34,8,128]{2,1,0:T(8,128)S(1)}) custom-call(f32[2,34,8,128]{3,2,1,0:T(8,128)S(1)} %get-tuple-element.20.col1, f32[2,34,8,128]{3,2,1,0:T(8,128)S(1)} %get-tuple-element.19.col2, f32[616,128]{1,0:T(8,128)S(1)} %collective-permute-done.4.halo, f32[4,3,34,8,128]{4,3,2,1,0:T(8,128)S(1)} %get-tuple-element.21.rates, ...), custom_call_target="tpu_custom_call" | custom-call | flops 1000000 | bytes 1000000 | tf_op jit(solution)/shard_map/pallas_call | solution.py:48
  25.4 0.1 collective-permute-start.6
  25.4 0.8 %shard_map.78.mid1 = f32[2,34,8,128]{3,2,1,0:T(8,128)S(1)} custom-call(f32[616,128]{1,0:T(8,128)S(1)} %shard_map.76.message, f32[2,34,8,128]{3,2,1,0:T(8,128)S(1)} %get-tuple-element.20.col1, f32[2,34,8,128]{3,2,1,0:T(8,128)S(1)} %get-tuple-element.19.col2, f32[4,3,34,8,128]{4,3,2,1,0:T(8,128)S(1)} %get-tuple-element.21.rates, ...), custom_call_target="tpu_custom_call" | custom-call | flops 1000000 | bytes 1000000 | tf_op jit(solution)/shard_map/pallas_call | solution.py:48
  26.2 0.9 %shard_map.80.begun = f32[2,3,34,8,128]{4,3,2,1,0:T(8,128)} custom-call(f32[2,34,8,128]{3,2,1,0:T(8,128)S(1)} %shard_map.77.before.mid0, f32[2,34,8,128]{3,2,1,0:T(8,128)S(1)} %shard_map.78.mid1, f32[2,34,8,128]{3,2,1,0:T(8,128)S(1)} %get-tuple-element.23.mid2, f32[4,3,34,8,128]{4,3,2,1,0:T(8,128)S(1)} %get-tuple-element.21.rates, ...), custom_call_target="tpu_custom_call" | custom-call | flops 1000000 | bytes 1000000 | tf_op jit(solution)/shard_map/pallas_call | solution.py:48
  27.2 4.6 %collective-permute-done.5.halo = f32[2,34,8,128]{3,2,1,0:T(8,128)S(1)} collective-permute-done((f32[2,34,8,128]{3,2,1,0:T(8,128)S(1)}, f32[2,34,8,128]{3,2,1,0:T(8,128)S(1)}, u32[]{:S(2)}, u32[]{:S(2)}) %collective-permute-start.5) | collective-permute-done | bytes 278560 | tf_op jit(solution)/shard_map/ppermute | solution.py:39
  31.8 0.9 %shard_map.81.begun = f32[2,3,34,8,128]{4,3,2,1,0:T(8,128)} custom-call(f32[2,3,34,8,128]{4,3,2,1,0:T(8,128)} %shard_map.80.begun, f32[2,34,8,128]{3,2,1,0:T(8,128)S(1)} %shard_map.78.mid1, f32[2,34,8,128]{3,2,1,0:T(8,128)S(1)} %get-tuple-element.23.mid2, f32[2,34,8,128]{3,2,1,0:T(8,128)S(1)} %collective-permute-done.5.halo, ...), custom_call_target="tpu_custom_call", output_to_operand_aliasing={{}: (0, {})} | custom-call | flops 1000000 | bytes 1000000 | tf_op jit(solution)/shard_map/pallas_call | solution.py:48
  32.7 2.0 %collective-permute-done.6.halo = f32[2,34,8,128]{3,2,1,0:T(8,128)S(1)} collective-permute-done((f32[2,34,8,128]{3,2,1,0:T(8,128)S(1)}, f32[2,34,8,128]{3,2,1,0:T(8,128)S(1)}, u32[]{:S(2)}, u32[]{:S(2)}) %collective-permute-start.6) | collective-permute-done | bytes 278560 | tf_op jit(solution)/shard_map/ppermute | solution.py:39
  34.7 0.9 %shard_map.82 = f32[2,3,34,8,128]{4,3,2,1,0:T(8,128)} custom-call(f32[2,3,34,8,128]{4,3,2,1,0:T(8,128)} %shard_map.81.begun, f32[2,34,8,128]{3,2,1,0:T(8,128)S(1)} %shard_map.77.before.mid0, f32[2,34,8,128]{3,2,1,0:T(8,128)S(1)} %shard_map.78.mid1, f32[2,34,8,128]{3,2,1,0:T(8,128)S(1)} %collective-permute-done.6.halo, ...), custom_call_target="tpu_custom_call", output_to_operand_aliasing={{}: (0, {})} | custom-call | flops 1000000 | bytes 1000000 | tf_op jit(solution)/shard_map/pallas_call | solution.py:48
  (1 shorter events, 0.0 us)
Async XLA Ops:
  1.5 12.7 %collective-permute-start.3 = (f32[2,34,8,128]{3,2,1,0:T(8,128)S(1)}, f32[2,34,8,128]{3,2,1,0:T(8,128)S(1)}, u32[]{:S(2)}, u32[]{:S(2)}) collective-permute-start(f32[2,34,8,128]{3,2,1,0:T(8,128)S(1)} %get-tuple-element.19.col2), channel_id=1, source_target_pairs={{0,4},{4,8},{8,12},{12,16},{16,20},{20,24},{24,28},{28,0},{1,5},{5... | collective-permute-start | bytes 835592 | tf_op jit(solution)/shard_map/ppermute | solution.py:39
  4.5 4.7 %collective-permute-start.1 = (f32[208,128]{1,0:T(8,128)S(1)}, f32[208,128]{1,0:T(8,128)S(1)}, u32[]{:S(2)}, u32[]{:S(2)}) collective-permute-start(f32[208,128]{1,0:T(8,128)S(1)} %get-tuple-element.15.own), channel_id=1, source_target_pairs={{0,2},{1,3},{2,0},{3,1},{4,6},{5,7},{6,4},{7,5},{8,10},{9,11},{10,... | collective-permute-start | bytes 319496 | tf_op jit(solution)/shard_map/ppermute | solution.py:44
  6.0 4.7 %collective-permute-start = (f32[208,128]{1,0:T(8,128)S(1)}, f32[208,128]{1,0:T(8,128)S(1)}, u32[]{:S(2)}, u32[]{:S(2)}) collective-permute-start(f32[208,128]{1,0:T(8,128)S(1)} %get-tuple-element.15.own), channel_id=1, source_target_pairs={{0,1},{1,0},{2,3},{3,2},{4,5},{5,4},{6,7},{7,6},{8,9},{9,8},{10,11... | collective-permute-start | bytes 319496 | tf_op jit(solution)/shard_map/ppermute | solution.py:44
  9.2 1.5 %collective-permute-start.2 = (f32[208,128]{1,0:T(8,128)S(1)}, f32[208,128]{1,0:T(8,128)S(1)}, u32[]{:S(2)}, u32[]{:S(2)}) collective-permute-start(f32[208,128]{1,0:T(8,128)S(1)} %collective-permute-done.1.second), channel_id=1, source_target_pairs={{0,1},{1,0},{2,3},{3,2},{4,5},{5,4},{6,7},{7,6},{8,9},{9,8},{10,11... | collective-permute-start | bytes 319496 | tf_op jit(solution)/shard_map/ppermute | solution.py:44
  9.2 1.0 %copy-start = (s32[2,2,3,34,256]{4,1,3,2,0:T(2,128)S(1)}, s32[2,2,3,34,256]{4,1,3,2,0:T(2,128)}, u32[]{:S(2)}) copy-start(s32[2,2,3,34,256]{4,1,3,2,0:T(2,128)} %param.8) | copy-start | bytes 1253380
  14.2 10.4 %collective-permute-start.4 = (f32[616,128]{1,0:T(8,128)S(1)}, f32[616,128]{1,0:T(8,128)S(1)}, u32[]{:S(2)}, u32[]{:S(2)}) collective-permute-start(f32[616,128]{1,0:T(8,128)S(1)} %shard_map.76.message), channel_id=1, source_target_pairs={{0,28},{4,0},{8,4},{12,8},{16,12},{20,16},{24,20},{28,24},{1,29},{... | collective-permute-start | bytes 946184 | tf_op jit(solution)/shard_map/ppermute | solution.py:39
  16.7 15.1 %collective-permute-start.5 = (f32[2,34,8,128]{3,2,1,0:T(8,128)S(1)}, f32[2,34,8,128]{3,2,1,0:T(8,128)S(1)}, u32[]{:S(2)}, u32[]{:S(2)}) collective-permute-start(f32[2,34,8,128]{3,2,1,0:T(8,128)S(1)} %shard_map.77.before.mid0), channel_id=1, source_target_pairs={{0,28},{4,0},{8,4},{12,8},{16,12},{20,16},{24,20},{28,24},{1,29},{... | collective-permute-start | bytes 835592 | tf_op jit(solution)/shard_map/ppermute | solution.py:39
  25.4 9.4 %collective-permute-start.6 = (f32[2,34,8,128]{3,2,1,0:T(8,128)S(1)}, f32[2,34,8,128]{3,2,1,0:T(8,128)S(1)}, u32[]{:S(2)}, u32[]{:S(2)}) collective-permute-start(f32[2,34,8,128]{3,2,1,0:T(8,128)S(1)} %get-tuple-element.23.mid2), channel_id=1, source_target_pairs={{0,4},{4,8},{8,12},{12,16},{16,20},{20,24},{24,28},{28,0},{1,5},{5... | collective-permute-start | bytes 835592 | tf_op jit(solution)/shard_map/ppermute | solution.py:39

commit v7 on v4

--- a/solution.py
+++ b/solution.py
@@ -92,6 +92,10 @@
         copy.wait()
 
 
+def gate_kernel(message, before, out):
+    pass
+
+
 def spread(upper_block, ref, *where):
     blocks = [jnp.broadcast_to(ref[(*index, pl.ds(r, 1), slice(None))], (8, LANES)) for index, r in where]
     return jnp.where(upper_block, blocks[1], blocks[0])
@@ -113,7 +117,7 @@
                     turn[d, t, c, l] = jnp.where(moment == 0, take, jnp.where(moment == 1 + d, keep, 1.0))
 
 
-def pre_kernel(own, first, second, third, flags, order, before, also, rates, factors, face, fields):
+def pre_kernel(own, first, second, third, flags, order, also, rates, factors, face, fields):
     columns, levels = rates.shape[1], rates.shape[2]
     half = LANES // 2
     odd = order[0] % 2 == 1
@@ -320,15 +324,17 @@
         (HBM,) * 6, [pltpu.VMEM(x.shape, x.dtype) for x in fields] + [dma((5,)), dma((columns, tracers))],
         10**5, 10**6, stay(state), stay(flag), *fields)
     west_halo = shifted(col2, "lon", 1)
+    across = swapped(packed, "trc", 2)
+    col0 = call(gate_kernel, column, (VMEM,) * 2, (), 1, 1, col0, across, aliases={0: 0})
     east_halo = shifted(col0, "lon", -1)
-    across = swapped(packed, "trc", 2)
     others = [swapped(packed, "trc", 1), across, swapped(across, "trc", 1)]
     turn = call(turn_kernel, f32(2, tracers, columns, levels, 8, LANES), (VMEM,), (), 10**6, 10**6, switch)
     rates, factors, face = call(
         pre_kernel,
         (f32(4, columns, levels, 8, LANES), f32(3, columns, levels, 8, LANES), f32(2 * levels, LANES)),
-        (VMEM,) * 5 + (SMEM, VMEM, VMEM), [pltpu.VMEM((4, columns, 2, levels, LANES), jnp.float32)],
-        10**6, 10**6, packed, *others, flag, order, west_halo, turn)
+        (VMEM,) * 5 + (SMEM, VMEM), [pltpu.VMEM((4, columns, 2, levels, LANES), jnp.float32)],
+        1, 1, packed, *others, flag, order, turn)
+    face = call(gate_kernel, f32(2 * levels, LANES), (VMEM,) * 2, (), 1, 1, face, west_halo, aliases={0: 0})
     face = shifted(face, "lon", -1)
     mid0 = call(west_kernel, column, (VMEM,) * 6, (), 10**6, 10**6, col0, col1, west_halo, rates, factors, turn)
     east_mid = shifted(mid0, "lon", -1)

time: 38.7 us -> 39.7 us (1.026)
  starting transfers between devices: 14.4 us -> 20.1 us
  waiting for transfers between devices: 15.3 us -> 11.5 us
  local copies, waits for them, and re-layouts: 1 us -> 0.01 us
    ppermute x5, starting transfers between devices: 12.8 us -> 16.6 us  [shifted(): lax.ppermute(value, axis, [(i, (i + by) % count) for i in range(count)])]
    ppermute x5, waiting for transfers between devices: 12.1 us -> 9.6 us  [shifted(): lax.ppermute(value, axis, [(i, (i + by) % count) for i in range(count)])]
    ppermute x3, starting transfers between devices: 1.6 us -> 3.51 us  [swapped(): return lax.ppermute(value, axis, [(i, i ^ mask) for i in range(count)])]
    ppermute x3, waiting for transfers between devices: 3.12 us -> 1.91 us  [swapped(): return lax.ppermute(value, axis, [(i, i ^ mask) for i in range(count)])]
    unnamed x2, local copies, waits for them, and re-layouts: 1 us -> 0.01 us
    pallas_call x9 -> x11, Pallas kernels: 7.79 us -> 7.85 us  [call(): pl.pallas_call(kernel, out_shape=out, in_specs=in_specs, out_specs=jax.tr...]
  transfers between devices with their start and end apart: 8 -> 8, of which waited for: 4 -> 7; matrix products, arithmetic and copies ran while one was open for 0% -> 0% of each run, Pallas kernels for 14% -> 14%
where the time goes in v7:
time: 39.7 us; the launch traced here: 39.5 us
  starting transfers between devices  20.1 us (51%)
  waiting for transfers between devices  11.5 us (29%)
  Pallas kernels  7.85 us (20%)
    ppermute x5, starting transfers between devices, shifted(): lax.ppermute(value, axis, [(i, (i + by) % count) for i in range(count)])  16.6 us
    ppermute x5, waiting for transfers between devices, shifted(): lax.ppermute(value, axis, [(i, (i + by) % count) for i in range(count)])  9.6 us
    pallas_call x11, Pallas kernels, call(): pl.pallas_call(kernel, out_shape=out, in_specs=in_specs, out_specs=jax.tr...  7.85 us
    ppermute x3, starting transfers between devices, swapped(): return lax.ppermute(value, axis, [(i, i ^ mask) for i in range(count)])  3.51 us
    ppermute x3, waiting for transfers between devices, swapped(): return lax.ppermute(value, axis, [(i, i ^ mask) for i in range(count)])  1.91 us
  transfers between devices with their start and end apart: 8, of which 7 were waited for; matrix products, arithmetic and copies ran while one was open for 0% of the time, Pallas kernels for 14%

profile of v7, /device:TPU:0, one launch (start us, length us, event | category | flops | bytes accessed | tf_op | source)
XLA Modules:
  0.0 39.5 jit_solution(332970776377660187)
XLA Ops:
  0.0 0.0 copy-start
  0.0 1.5 %shard_map.73 = (f32[2,34,8,128]{3,2,1,0:T(8,128)S(1)}, f32[2,34,8,128]{3,2,1,0:T(8,128)S(1)}, f32[2,34,8,128]{3,2,1,0:T(8,128)S(1)}, f32[208,128]{1,0:T(8,128)S(1)}, s32[3,136,128]{2,1,0:T(8,128)S(1)}) custom-call(f32[2,3,34,8,128]{4,3,2,1,0:T(8,128)} %bitcast.22, s32[3,136,128]{2,1,0:T(8,128)} %bitcast.23, f32[3,34,64]{2,1,0:T(8,128)} %mass.1, ...), custom_call_target="tpu_custom_call" | custom-call | flops 100000 | bytes 1000000 | tf_op jit(solution)/shard_map/pallas_call | solution.py:47
  1.5 3.0 %collective-permute-start = (f32[208,128]{1,0:T(8,128)S(1)}, f32[208,128]{1,0:T(8,128)S(1)}, u32[]{:S(2)}, u32[]{:S(2)}) collective-permute-start(f32[208,128]{1,0:T(8,128)S(1)} %get-tuple-element.16.own), channel_id=1, source_target_pairs={{0,2},{1,3},{2,0},{3,1},{4,6},{5,7},{6,4},{7,5},{8,10},{9,11},{10,... | collective-permute-start | bytes 319496 | tf_op jit(solution)/shard_map/ppermute | solution.py:43
  4.5 1.5 %collective-permute-start.1 = (f32[2,34,8,128]{3,2,1,0:T(8,128)S(1)}, f32[2,34,8,128]{3,2,1,0:T(8,128)S(1)}, u32[]{:S(2)}, u32[]{:S(2)}) collective-permute-start(f32[2,34,8,128]{3,2,1,0:T(8,128)S(1)} %get-tuple-element.18.col2), channel_id=1, source_target_pairs={{0,4},{4,8},{8,12},{12,16},{16,20},{20,24},{24,28},{28,0},{1,5},{5... | collective-permute-start | bytes 835592 | tf_op jit(solution)/shard_map/ppermute | solution.py:38
  6.0 1.4 %collective-permute-done.before.second = f32[208,128]{1,0:T(8,128)S(1)} collective-permute-done((f32[208,128]{1,0:T(8,128)S(1)}, f32[208,128]{1,0:T(8,128)S(1)}, u32[]{:S(2)}, u32[]{:S(2)}) %collective-permute-start) | collective-permute-done | bytes 106528 | tf_op jit(solution)/shard_map/ppermute | solution.py:43
  7.5 4.8 %collective-permute-start.4 = (f32[2,34,8,128]{3,2,1,0:T(8,128)S(1)}, f32[2,34,8,128]{3,2,1,0:T(8,128)S(1)}, u32[]{:S(2)}, u32[]{:S(2)}) collective-permute-start(f32[2,34,8,128]{3,2,1,0:T(8,128)S(1)} %shard_map.74.col0), channel_id=1, source_target_pairs={{0,28},{4,0},{8,4},{12,8},{16,12},{20,16},{24,20},{28,24},{1,29},{... | collective-permute-start | bytes 835592 | tf_op jit(solution)/shard_map/ppermute | solution.py:38
  12.3 0.0 collective-permute-start.2
  12.3 0.5 %collective-permute-start.3 = (f32[208,128]{1,0:T(8,128)S(1)}, f32[208,128]{1,0:T(8,128)S(1)}, u32[]{:S(2)}, u32[]{:S(2)}) collective-permute-start(f32[208,128]{1,0:T(8,128)S(1)} %collective-permute-done.before.second), channel_id=1, source_target_pairs={{0,1},{1,0},{2,3},{3,2},{4,5},{5,4},{6,7},{7,6},{8,9},{9,8},{10,11... | collective-permute-start | bytes 319496 | tf_op jit(solution)/shard_map/ppermute | solution.py:43
  12.8 0.0 copy-done
  12.8 0.5 %shard_map.75.also.turn = f32[2,2,3,34,8,128]{5,4,3,2,1,0:T(8,128)S(1)} custom-call(s32[2,3,136,128]{3,2,1,0:T(8,128)S(1)} %bitcast.21), custom_call_target="tpu_custom_call" | custom-call | flops 1000000 | bytes 1000000 | tf_op jit(solution)/shard_map/pallas_call | solution.py:47
  13.3 0.3 collective-permute-done.2.first
  13.6 0.2 collective-permute-done.3.third
  13.7 0.7 %shard_map.76 = (f32[4,3,34,8,128]{4,3,2,1,0:T(8,128)S(1)}, f32[3,3,34,8,128]{4,3,2,1,0:T(8,128)S(1)}, f32[68,128]{1,0:T(8,128)S(1)}) custom-call(f32[208,128]{1,0:T(8,128)S(1)} %get-tuple-element.16.own, f32[208,128]{1,0:T(8,128)S(1)} %collective-permute-done.2.first, f32[208,128]{1,0:T(8,128)S(1)} %collective-permute-done.before.second, ...), custom_call_target="tpu_custom_call" | custom-call | flops 1 | bytes 1 | tf_op jit(solution)/shard_map/pallas_call | solution.py:47
  14.4 3.2 %collective-permute-done.1.west_halo.before = f32[2,34,8,128]{3,2,1,0:T(8,128)S(1)} collective-permute-done((f32[2,34,8,128]{3,2,1,0:T(8,128)S(1)}, f32[2,34,8,128]{3,2,1,0:T(8,128)S(1)}, u32[]{:S(2)}, u32[]{:S(2)}) %collective-permute-start.1) | collective-permute-done | bytes 278560 | tf_op jit(solution)/shard_map/ppermute | solution.py:38
  17.6 8.9 %collective-permute-start.5 = (f32[68,128]{1,0:T(8,128)S(1)}, f32[68,128]{1,0:T(8,128)S(1)}, u32[]{:S(2)}, u32[]{:S(2)}) collective-permute-start(f32[68,128]{1,0:T(8,128)S(1)} %shard_map.79), channel_id=1, source_target_pairs={{0,28},{4,0},{8,4},{12,8},{16,12},{20,16},{24,20},{28,24},{1,29},{... | collective-permute-start | bytes 104456 | tf_op jit(solution)/shard_map/ppermute | solution.py:38
  26.5 0.8 %shard_map.77.before.mid0 = f32[2,34,8,128]{3,2,1,0:T(8,128)S(1)} custom-call(f32[2,34,8,128]{3,2,1,0:T(8,128)S(1)} %shard_map.74.col0, f32[2,34,8,128]{3,2,1,0:T(8,128)S(1)} %get-tuple-element.17.col1, f32[2,34,8,128]{3,2,1,0:T(8,128)S(1)} %collective-permute-done.1.west_halo.before, f32[4,3,34,8,128]{4,3,2,1,0:T(8,128)S(1)} %get-tuple-element.20.rates, ...), custom_call_target="tpu_custom_call" | custom-call | flops 1000000 | bytes 1000000 | tf_op jit(solution)/shard_map/pallas_call | solution.py:47
  27.3 0.1 collective-permute-start.6
  27.4 0.8 %collective-permute-done.5.face = f32[68,128]{1,0:T(8,128)S(1)} collective-permute-done((f32[68,128]{1,0:T(8,128)S(1)}, f32[68,128]{1,0:T(8,128)S(1)}, u32[]{:S(2)}, u32[]{:S(2)}) %collective-permute-start.5) | collective-permute-done | bytes 34848 | tf_op jit(solution)/shard_map/ppermute | solution.py:38
  28.2 0.0 collective-permute-done.4.east_halo
  28.2 0.8 %shard_map.80 = (f32[2,34,8,128]{3,2,1,0:T(8,128)S(1)}, f32[34,8,128]{2,1,0:T(8,128)S(1)}) custom-call(f32[2,34,8,128]{3,2,1,0:T(8,128)S(1)} %get-tuple-element.17.col1, f32[2,34,8,128]{3,2,1,0:T(8,128)S(1)} %get-tuple-element.18.col2, f32[2,34,8,128]{3,2,1,0:T(8,128)S(1)} %collective-permute-done.4.east_halo, f32[68,128]{1,0:T(8,128)S(1)} %collective-permute-done.5.face, ...), custom_call_target="tpu_custom_call" | custom-call | flops 1000000 | bytes 1000000 | tf_op jit(solution)/shard_map/pallas_call | solution.py:47
  29.0 1.3 %collective-permute-start.7 = (f32[2,34,8,128]{3,2,1,0:T(8,128)S(1)}, f32[2,34,8,128]{3,2,1,0:T(8,128)S(1)}, u32[]{:S(2)}, u32[]{:S(2)}) collective-permute-start(f32[2,34,8,128]{3,2,1,0:T(8,128)S(1)} %get-tuple-element.23.mid2), channel_id=1, source_target_pairs={{0,4},{4,8},{8,12},{12,16},{16,20},{20,24},{24,28},{28,0},{1,5},{5... | collective-permute-start | bytes 835592 | tf_op jit(solution)/shard_map/ppermute | solution.py:38
  30.3 0.8 %shard_map.78.mid1 = f32[2,34,8,128]{3,2,1,0:T(8,128)S(1)} custom-call(f32[2,34,8,128]{3,2,1,0:T(8,128)S(1)} %shard_map.74.col0, f32[2,34,8,128]{3,2,1,0:T(8,128)S(1)} %get-tuple-element.17.col1, f32[2,34,8,128]{3,2,1,0:T(8,128)S(1)} %get-tuple-element.18.col2, f32[4,3,34,8,128]{4,3,2,1,0:T(8,128)S(1)} %get-tuple-element.20.rates, ...), custom_call_target="tpu_custom_call" | custom-call | flops 1000000 | bytes 1000000 | tf_op jit(solution)/shard_map/pallas_call | solution.py:47
  31.1 0.9 %shard_map.81.begun = f32[2,3,34,8,128]{4,3,2,1,0:T(8,128)} custom-call(f32[2,34,8,128]{3,2,1,0:T(8,128)S(1)} %shard_map.77.before.mid0, f32[2,34,8,128]{3,2,1,0:T(8,128)S(1)} %shard_map.78.mid1, f32[2,34,8,128]{3,2,1,0:T(8,128)S(1)} %get-tuple-element.23.mid2, f32[4,3,34,8,128]{4,3,2,1,0:T(8,128)S(1)} %get-tuple-element.20.rates, ...), custom_call_target="tpu_custom_call" | custom-call | flops 1000000 | bytes 1000000 | tf_op jit(solution)/shard_map/pallas_call | solution.py:47
  32.0 1.9 %collective-permute-done.6.halo = f32[2,34,8,128]{3,2,1,0:T(8,128)S(1)} collective-permute-done((f32[2,34,8,128]{3,2,1,0:T(8,128)S(1)}, f32[2,34,8,128]{3,2,1,0:T(8,128)S(1)}, u32[]{:S(2)}, u32[]{:S(2)}) %collective-permute-start.6) | collective-permute-done | bytes 278560 | tf_op jit(solution)/shard_map/ppermute | solution.py:38
  33.9 0.9 %shard_map.82.begun = f32[2,3,34,8,128]{4,3,2,1,0:T(8,128)} custom-call(f32[2,3,34,8,128]{4,3,2,1,0:T(8,128)} %shard_map.81.begun, f32[2,34,8,128]{3,2,1,0:T(8,128)S(1)} %shard_map.78.mid1, f32[2,34,8,128]{3,2,1,0:T(8,128)S(1)} %get-tuple-element.23.mid2, f32[2,34,8,128]{3,2,1,0:T(8,128)S(1)} %collective-permute-done.6.halo, ...), custom_call_target="tpu_custom_call", output_to_operand_aliasing={{}: (0, {})} | custom-call | flops 1000000 | bytes 1000000 | tf_op jit(solution)/shard_map/pallas_call | solution.py:47
  34.9 3.7 %collective-permute-done.7.halo = f32[2,34,8,128]{3,2,1,0:T(8,128)S(1)} collective-permute-done((f32[2,34,8,128]{3,2,1,0:T(8,128)S(1)}, f32[2,34,8,128]{3,2,1,0:T(8,128)S(1)}, u32[]{:S(2)}, u32[]{:S(2)}) %collective-permute-start.7) | collective-permute-done | bytes 278560 | tf_op jit(solution)/shard_map/ppermute | solution.py:38
  38.6 0.9 %shard_map.83 = f32[2,3,34,8,128]{4,3,2,1,0:T(8,128)} custom-call(f32[2,3,34,8,128]{4,3,2,1,0:T(8,128)} %shard_map.82.begun, f32[2,34,8,128]{3,2,1,0:T(8,128)S(1)} %shard_map.77.before.mid0, f32[2,34,8,128]{3,2,1,0:T(8,128)S(1)} %shard_map.78.mid1, f32[2,34,8,128]{3,2,1,0:T(8,128)S(1)} %collective-permute-done.7.halo, ...), custom_call_target="tpu_custom_call", output_to_operand_aliasing={{}: (0, {})} | custom-call | flops 1000000 | bytes 1000000 | tf_op jit(solution)/shard_map/pallas_call | solution.py:47
  (2 shorter events, 0.0 us)
Async XLA Ops:
  0.0 12.8 %copy-start = (s32[2,2,3,34,256]{4,1,3,2,0:T(2,128)S(1)}, s32[2,2,3,34,256]{4,1,3,2,0:T(2,128)}, u32[]{:S(2)}) copy-start(s32[2,2,3,34,256]{4,1,3,2,0:T(2,128)} %param.8) | copy-start | bytes 1253380
  1.5 6.0 %collective-permute-start = (f32[208,128]{1,0:T(8,128)S(1)}, f32[208,128]{1,0:T(8,128)S(1)}, u32[]{:S(2)}, u32[]{:S(2)}) collective-permute-start(f32[208,128]{1,0:T(8,128)S(1)} %get-tuple-element.16.own), channel_id=1, source_target_pairs={{0,2},{1,3},{2,0},{3,1},{4,6},{5,7},{6,4},{7,5},{8,10},{9,11},{10,... | collective-permute-start | bytes 319496 | tf_op jit(solution)/shard_map/ppermute | solution.py:43
  4.5 13.1 %collective-permute-start.1 = (f32[2,34,8,128]{3,2,1,0:T(8,128)S(1)}, f32[2,34,8,128]{3,2,1,0:T(8,128)S(1)}, u32[]{:S(2)}, u32[]{:S(2)}) collective-permute-start(f32[2,34,8,128]{3,2,1,0:T(8,128)S(1)} %get-tuple-element.18.col2), channel_id=1, source_target_pairs={{0,4},{4,8},{8,12},{12,16},{16,20},{20,24},{24,28},{28,0},{1,5},{5... | collective-permute-start | bytes 835592 | tf_op jit(solution)/shard_map/ppermute | solution.py:38
  7.5 20.7 %collective-permute-start.4 = (f32[2,34,8,128]{3,2,1,0:T(8,128)S(1)}, f32[2,34,8,128]{3,2,1,0:T(8,128)S(1)}, u32[]{:S(2)}, u32[]{:S(2)}) collective-permute-start(f32[2,34,8,128]{3,2,1,0:T(8,128)S(1)} %shard_map.74.col0), channel_id=1, source_target_pairs={{0,28},{4,0},{8,4},{12,8},{16,12},{20,16},{24,20},{28,24},{1,29},{... | collective-permute-start | bytes 835592 | tf_op jit(solution)/shard_map/ppermute | solution.py:38
  12.3 1.3 %collective-permute-start.2 = (f32[208,128]{1,0:T(8,128)S(1)}, f32[208,128]{1,0:T(8,128)S(1)}, u32[]{:S(2)}, u32[]{:S(2)}) collective-permute-start(f32[208,128]{1,0:T(8,128)S(1)} %get-tuple-element.16.own), channel_id=1, source_target_pairs={{0,1},{1,0},{2,3},{3,2},{4,5},{5,4},{6,7},{7,6},{8,9},{9,8},{10,11... | collective-permute-start | bytes 319496 | tf_op jit(solution)/shard_map/ppermute | solution.py:43
  12.3 1.5 %collective-permute-start.3 = (f32[208,128]{1,0:T(8,128)S(1)}, f32[208,128]{1,0:T(8,128)S(1)}, u32[]{:S(2)}, u32[]{:S(2)}) collective-permute-start(f32[208,128]{1,0:T(8,128)S(1)} %collective-permute-done.before.second), channel_id=1, source_target_pairs={{0,1},{1,0},{2,3},{3,2},{4,5},{5,4},{6,7},{7,6},{8,9},{9,8},{10,11... | collective-permute-start | bytes 319496 | tf_op jit(solution)/shard_map/ppermute | solution.py:43
  17.6 10.5 %collective-permute-start.5 = (f32[68,128]{1,0:T(8,128)S(1)}, f32[68,128]{1,0:T(8,128)S(1)}, u32[]{:S(2)}, u32[]{:S(2)}) collective-permute-start(f32[68,128]{1,0:T(8,128)S(1)} %shard_map.79), channel_id=1, source_target_pairs={{0,28},{4,0},{8,4},{12,8},{16,12},{20,16},{24,20},{28,24},{1,29},{... | collective-permute-start | bytes 104456 | tf_op jit(solution)/shard_map/ppermute | solution.py:38
  27.3 6.6 %collective-permute-start.6 = (f32[2,34,8,128]{3,2,1,0:T(8,128)S(1)}, f32[2,34,8,128]{3,2,1,0:T(8,128)S(1)}, u32[]{:S(2)}, u32[]{:S(2)}) collective-permute-start(f32[2,34,8,128]{3,2,1,0:T(8,128)S(1)} %shard_map.77.before.mid0), channel_id=1, source_target_pairs={{0,28},{4,0},{8,4},{12,8},{16,12},{20,16},{24,20},{28,24},{1,29},{... | collective-permute-start | bytes 835592 | tf_op jit(solution)/shard_map/ppermute | solution.py:38
  29.0 9.6 %collective-permute-start.7 = (f32[2,34,8,128]{3,2,1,0:T(8,128)S(1)}, f32[2,34,8,128]{3,2,1,0:T(8,128)S(1)}, u32[]{:S(2)}, u32[]{:S(2)}) collective-permute-start(f32[2,34,8,128]{3,2,1,0:T(8,128)S(1)} %get-tuple-element.23.mid2), channel_id=1, source_target_pairs={{0,4},{4,8},{8,12},{12,16},{16,20},{20,24},{24,28},{28,0},{1,5},{5... | collective-permute-start | bytes 835592 | tf_op jit(solution)/shard_map/ppermute | solution.py:38

commit v8 on v6

--- a/solution.py
+++ b/solution.py
@@ -70,13 +70,21 @@
     return row == 0, row == slope
 
 
-def head_kernel(state, flags, mass, xf, yf, km, message, col1, col2, packed, flags_v, mass_v, xf_v, yf_v, km_v, sems, column_sems):
+def first_kernel(state, col2, sems):
+    copies = [pltpu.make_async_copy(state.at[t, 2], col2.at[t], sems.at[t]) for t in range(state.shape[0])]
+    for copy in copies:
+        copy.start()
+    for copy in copies:
+        copy.wait()
+
+
+def head_kernel(state, flags, mass, xf, yf, km, before, message, col1, packed, flags_v, mass_v, xf_v, yf_v, km_v, sems, column_sems):
     tracers, columns, levels = state.shape[0], mass.shape[0], mass.shape[1]
     half = LANES // 2
     pairs = ((mass, mass_v), (xf, xf_v), (yf, yf_v), (km, km_v), (flags, flags_v))
     copies = [pltpu.make_async_copy(src, dst, sems.at[i]) for i, (src, dst) in enumerate(pairs)]
     for t in range(tracers):
-        for c, place in ((2, col2.at[t]), (0, message.at[pl.ds(t * levels, levels)]), (1, col1.at[t])):
+        for c, place in ((0, message.at[pl.ds(t * levels, levels)]), (1, col1.at[t])):
             copies.append(pltpu.make_async_copy(state.at[t, c], place, column_sems.at[c, t]))
     for copy in copies:
         copy.start()
@@ -331,12 +339,13 @@
     dma = pltpu.SemaphoreType.DMA
     fields = tuple(stay(x) for x in (air_mass, x_flux, y_flux, vertical_mixing))
 
-    message, col1, col2, packed, flag = call(
+    col2 = call(first_kernel, column, (HBM,), [dma((tracers,))], 1, 1, stay(state))
+    west_halo = shifted(col2, "lon", 1)
+    message, col1, packed, flag = call(
         head_kernel,
-        (f32(length, 8, LANES), column, column, f32(rows, LANES), jax.ShapeDtypeStruct(flag.shape, flag.dtype)),
-        (HBM,) * 6, [pltpu.VMEM(x.shape, x.dtype) for x in fields] + [dma((5,)), dma((columns, tracers))],
-        10**5, 10**6, stay(state), stay(flag), *fields)
-    west_halo = shifted(col2, "lon", 1)
+        (f32(length, 8, LANES), column, f32(rows, LANES), jax.ShapeDtypeStruct(flag.shape, flag.dtype)),
+        (HBM,) * 6 + (VMEM,), [pltpu.VMEM(x.shape, x.dtype) for x in fields] + [dma((5,)), dma((columns, tracers))],
+        10**5, 10**6, stay(state), stay(flag), *fields, col2)
     across = swapped(packed, "trc", 2)
     others = [swapped(packed, "trc", 1), across, swapped(across, "trc", 1)]
     turn = call(turn_kernel, f32(2, tracers, columns, levels, 8, LANES), (VMEM,), (), 10**6, 10**6, switch)

time: 35.8 us -> 35.5 us (level)
  waiting for transfers between devices: 19 us -> 17.3 us
  starting transfers between devices: 7.77 us -> 9.18 us
  local copies, waits for them, and re-layouts: 1 us -> 0.01 us
  Pallas kernels: 7.82 us -> 8.78 us
    ppermute x4, waiting for transfers between devices: 15.8 us -> 13.3 us  [shifted(): lax.ppermute(value, axis, [(i, (i + by) % count) for i in range(count)])]
    ppermute x4, starting transfers between devices: 6.28 us -> 7.62 us  [shifted(): lax.ppermute(value, axis, [(i, (i + by) % count) for i in range(count)])]
    unnamed x2, local copies, waits for them, and re-layouts: 1 us -> 0.01 us
    pallas_call x10 -> x11, Pallas kernels: 7.82 us -> 8.78 us  [call(): pl.pallas_call(kernel, out_shape=out, in_specs=in_specs, out_specs=jax.tr...]
    ppermute x3, waiting for transfers between devices: 3.22 us -> 4.02 us  [swapped(): return lax.ppermute(value, axis, [(i, i ^ mask) for i in range(count)])]
  transfers between devices with their start and end apart: 7 -> 7, of which waited for: 5 -> 6; matrix products, arithmetic and copies ran while one was open for 0% -> 0% of each run, Pallas kernels for 15% -> 19%
where the time goes in v8:
time: 35.5 us; the launch traced here: 35.4 us
  waiting for transfers between devices  17.3 us (49%)
  starting transfers between devices  9.18 us (26%)
  Pallas kernels  8.78 us (25%)
    ppermute x4, waiting for transfers between devices, shifted(): lax.ppermute(value, axis, [(i, (i + by) % count) for i in range(count)])  13.3 us
    pallas_call x11, Pallas kernels, call(): pl.pallas_call(kernel, out_shape=out, in_specs=in_specs, out_specs=jax.tr...  8.78 us
    ppermute x4, starting transfers between devices, shifted(): lax.ppermute(value, axis, [(i, (i + by) % count) for i in range(count)])  7.62 us
    ppermute x3, waiting for transfers between devices, swapped(): return lax.ppermute(value, axis, [(i, i ^ mask) for i in range(count)])  4.02 us
    ppermute x3, starting transfers between devices, swapped(): return lax.ppermute(value, axis, [(i, i ^ mask) for i in range(count)])  1.56 us
  transfers between devices with their start and end apart: 7, of which 6 were waited for; matrix products, arithmetic and copies ran while one was open for 0% of the time, Pallas kernels for 19%

profile of v8, /device:TPU:0, one launch (start us, length us, event | category | flops | bytes accessed | tf_op | source)
XLA Modules:
  0.0 35.4 jit_solution(4088697729173214349)
XLA Ops:
  0.0 0.0 copy-start
  0.0 1.0 %shard_map.73.before.col2 = f32[2,34,8,128]{3,2,1,0:T(8,128)S(1)} custom-call(f32[2,3,34,8,128]{4,3,2,1,0:T(8,128)} %bitcast.24), custom_call_target="tpu_custom_call" | custom-call | flops 1 | bytes 1 | tf_op jit(solution)/shard_map/pallas_call | solution.py:48
  1.1 3.0 %collective-permute-start.3 = (f32[2,34,8,128]{3,2,1,0:T(8,128)S(1)}, f32[2,34,8,128]{3,2,1,0:T(8,128)S(1)}, u32[]{:S(2)}, u32[]{:S(2)}) collective-permute-start(f32[2,34,8,128]{3,2,1,0:T(8,128)S(1)} %shard_map.73.before.col2), channel_id=1, source_target_pairs={{0,4},{4,8},{8,12},{12,16},{16,20},{20,24},{24,28},{28,0},{1,5},{5... | collective-permute-start | bytes 835592 | tf_op jit(solution)/shard_map/ppermute | solution.py:39
  4.1 1.4 %shard_map.74 = (f32[77,8,128]{2,1,0:T(8,128)S(1)}, f32[2,34,8,128]{3,2,1,0:T(8,128)S(1)}, f32[208,128]{1,0:T(8,128)S(1)}, s32[3,136,128]{2,1,0:T(8,128)S(1)}) custom-call(f32[2,3,34,8,128]{4,3,2,1,0:T(8,128)} %bitcast.25, s32[3,136,128]{2,1,0:T(8,128)} %bitcast.26, f32[3,34,64]{2,1,0:T(8,128)} %mass.1, f32[3,34,64]{2,1,0:T(8,128)} %xf.1, f32[3,34,64]{2,1,0:T(8,128)} %yf.1, ...), custom_call_target="tpu_custom_call" | custom-call | flops 100000 | bytes 1000000 | tf_op jit(solution)/shard_map/pallas_call | solution.py:48
  5.5 1.6 %collective-permute-start.1 = (f32[208,128]{1,0:T(8,128)S(1)}, f32[208,128]{1,0:T(8,128)S(1)}, u32[]{:S(2)}, u32[]{:S(2)}) collective-permute-start(f32[208,128]{1,0:T(8,128)S(1)} %get-tuple-element.14.own), channel_id=1, source_target_pairs={{0,2},{1,3},{2,0},{3,1},{4,6},{5,7},{6,4},{7,5},{8,10},{9,11},{10,... | collective-permute-start | bytes 319496 | tf_op jit(solution)/shard_map/ppermute | solution.py:44
  7.0 0.0 collective-permute-start
  7.0 3.2 %collective-permute-done.1.second = f32[208,128]{1,0:T(8,128)S(1)} collective-permute-done((f32[208,128]{1,0:T(8,128)S(1)}, f32[208,128]{1,0:T(8,128)S(1)}, u32[]{:S(2)}, u32[]{:S(2)}) %collective-permute-start.1) | collective-permute-done | bytes 106528 | tf_op jit(solution)/shard_map/ppermute | solution.py:44
  10.2 0.0 collective-permute-start.2
  10.2 0.0 copy-done
  10.2 0.5 %shard_map.75.also.turn = f32[2,2,3,34,8,128]{5,4,3,2,1,0:T(8,128)S(1)} custom-call(s32[2,3,136,128]{3,2,1,0:T(8,128)S(1)} %bitcast.23), custom_call_target="tpu_custom_call" | custom-call | flops 1000000 | bytes 1000000 | tf_op jit(solution)/shard_map/pallas_call | solution.py:48
  10.7 0.0 collective-permute-done.first
  10.7 0.8 %collective-permute-done.2.third = f32[208,128]{1,0:T(8,128)S(1)} collective-permute-done((f32[208,128]{1,0:T(8,128)S(1)}, f32[208,128]{1,0:T(8,128)S(1)}, u32[]{:S(2)}, u32[]{:S(2)}) %collective-permute-start.2) | collective-permute-done | bytes 106528 | tf_op jit(solution)/shard_map/ppermute | solution.py:44
  11.5 0.7 %shard_map.76 = (f32[4,3,34,8,128]{4,3,2,1,0:T(8,128)S(1)}, f32[3,3,34,8,128]{4,3,2,1,0:T(8,128)S(1)}, f32[616,128]{1,0:T(8,128)S(1)}) custom-call(f32[208,128]{1,0:T(8,128)S(1)} %get-tuple-element.14.own, f32[208,128]{1,0:T(8,128)S(1)} %collective-permute-done.first, f32[208,128]{1,0:T(8,128)S(1)} %collective-permute-done.1.second, ...), custom_call_target="tpu_custom_call", output_to_operand_aliasing={{2}: (6, {})} | custom-call | flops 1 | bytes 1 | tf_op jit(solution)/shard_map/pallas_call | solution.py:48
  12.2 1.5 %collective-permute-done.3.before.west_halo = f32[2,34,8,128]{3,2,1,0:T(8,128)S(1)} collective-permute-done((f32[2,34,8,128]{3,2,1,0:T(8,128)S(1)}, f32[2,34,8,128]{3,2,1,0:T(8,128)S(1)}, u32[]{:S(2)}, u32[]{:S(2)}) %collective-permute-start.3) | collective-permute-done | bytes 278560 | tf_op jit(solution)/shard_map/ppermute | solution.py:39
  13.8 1.7 %collective-permute-start.4 = (f32[616,128]{1,0:T(8,128)S(1)}, f32[616,128]{1,0:T(8,128)S(1)}, u32[]{:S(2)}, u32[]{:S(2)}) collective-permute-start(f32[616,128]{1,0:T(8,128)S(1)} %shard_map.77.message), channel_id=1, source_target_pairs={{0,28},{4,0},{8,4},{12,8},{16,12},{20,16},{24,20},{28,24},{1,29},{... | collective-permute-start | bytes 946184 | tf_op jit(solution)/shard_map/ppermute | solution.py:39
  15.5 0.8 %shard_map.78.before.mid0 = f32[2,34,8,128]{3,2,1,0:T(8,128)S(1)} custom-call(f32[616,128]{1,0:T(8,128)S(1)} %shard_map.77.message, f32[2,34,8,128]{3,2,1,0:T(8,128)S(1)} %get-tuple-element.18.col1, f32[2,34,8,128]{3,2,1,0:T(8,128)S(1)} %collective-permute-done.3.before.west_halo, f32[4,3,34,8,128]{4,3,2,1,0:T(8,128)S(1)} %get-tuple-element.19.rates, ...), custom_call_target="tpu_custom_call" | custom-call | flops 1000000 | bytes 1000000 | tf_op jit(solution)/shard_map/pallas_call | solution.py:48
  16.3 1.9 %collective-permute-start.5 = (f32[2,34,8,128]{3,2,1,0:T(8,128)S(1)}, f32[2,34,8,128]{3,2,1,0:T(8,128)S(1)}, u32[]{:S(2)}, u32[]{:S(2)}) collective-permute-start(f32[2,34,8,128]{3,2,1,0:T(8,128)S(1)} %shard_map.78.before.mid0), channel_id=1, source_target_pairs={{0,28},{4,0},{8,4},{12,8},{16,12},{20,16},{24,20},{28,24},{1,29},{... | collective-permute-start | bytes 835592 | tf_op jit(solution)/shard_map/ppermute | solution.py:39
  18.2 5.9 %collective-permute-done.4.halo = f32[616,128]{1,0:T(8,128)S(1)} collective-permute-done((f32[616,128]{1,0:T(8,128)S(1)}, f32[616,128]{1,0:T(8,128)S(1)}, u32[]{:S(2)}, u32[]{:S(2)}) %collective-permute-start.4) | collective-permute-done | bytes 315424 | tf_op jit(solution)/shard_map/ppermute | solution.py:39
  24.2 0.8 %shard_map.80 = (f32[2,34,8,128]{3,2,1,0:T(8,128)S(1)}, f32[34,8,128]{2,1,0:T(8,128)S(1)}) custom-call(f32[2,34,8,128]{3,2,1,0:T(8,128)S(1)} %get-tuple-element.18.col1, f32[2,34,8,128]{3,2,1,0:T(8,128)S(1)} %shard_map.73.before.col2, f32[616,128]{1,0:T(8,128)S(1)} %collective-permute-done.4.halo, f32[4,3,34,8,128]{4,3,2,1,0:T(8,128)S(1)} %get-tuple-element.19.rates, ...), custom_call_target="tpu_custom_call" | custom-call | flops 1000000 | bytes 1000000 | tf_op jit(solution)/shard_map/pallas_call | solution.py:48
  25.0 0.9 %collective-permute-start.6 = (f32[2,34,8,128]{3,2,1,0:T(8,128)S(1)}, f32[2,34,8,128]{3,2,1,0:T(8,128)S(1)}, u32[]{:S(2)}, u32[]{:S(2)}) collective-permute-start(f32[2,34,8,128]{3,2,1,0:T(8,128)S(1)} %get-tuple-element.21.mid2), channel_id=1, source_target_pairs={{0,4},{4,8},{8,12},{12,16},{16,20},{20,24},{24,28},{28,0},{1,5},{5... | collective-permute-start | bytes 835592 | tf_op jit(solution)/shard_map/ppermute | solution.py:39
  25.9 0.8 %shard_map.79.mid1 = f32[2,34,8,128]{3,2,1,0:T(8,128)S(1)} custom-call(f32[616,128]{1,0:T(8,128)S(1)} %shard_map.77.message, f32[2,34,8,128]{3,2,1,0:T(8,128)S(1)} %get-tuple-element.18.col1, f32[2,34,8,128]{3,2,1,0:T(8,128)S(1)} %shard_map.73.before.col2, f32[4,3,34,8,128]{4,3,2,1,0:T(8,128)S(1)} %get-tuple-element.19.rates, ...), custom_call_target="tpu_custom_call" | custom-call | flops 1000000 | bytes 1000000 | tf_op jit(solution)/shard_map/pallas_call | solution.py:48
  26.7 0.9 %shard_map.81.begun = f32[2,3,34,8,128]{4,3,2,1,0:T(8,128)} custom-call(f32[2,34,8,128]{3,2,1,0:T(8,128)S(1)} %shard_map.78.before.mid0, f32[2,34,8,128]{3,2,1,0:T(8,128)S(1)} %shard_map.79.mid1, f32[2,34,8,128]{3,2,1,0:T(8,128)S(1)} %get-tuple-element.21.mid2, f32[4,3,34,8,128]{4,3,2,1,0:T(8,128)S(1)} %get-tuple-element.19.rates, ...), custom_call_target="tpu_custom_call" | custom-call | flops 1000000 | bytes 1000000 | tf_op jit(solution)/shard_map/pallas_call | solution.py:48
  27.6 0.7 %collective-permute-done.5.halo = f32[2,34,8,128]{3,2,1,0:T(8,128)S(1)} collective-permute-done((f32[2,34,8,128]{3,2,1,0:T(8,128)S(1)}, f32[2,34,8,128]{3,2,1,0:T(8,128)S(1)}, u32[]{:S(2)}, u32[]{:S(2)}) %collective-permute-start.5) | collective-permute-done | bytes 278560 | tf_op jit(solution)/shard_map/ppermute | solution.py:39
  28.4 0.9 %shard_map.82.begun = f32[2,3,34,8,128]{4,3,2,1,0:T(8,128)} custom-call(f32[2,3,34,8,128]{4,3,2,1,0:T(8,128)} %shard_map.81.begun, f32[2,34,8,128]{3,2,1,0:T(8,128)S(1)} %shard_map.79.mid1, f32[2,34,8,128]{3,2,1,0:T(8,128)S(1)} %get-tuple-element.21.mid2, f32[2,34,8,128]{3,2,1,0:T(8,128)S(1)} %collective-permute-done.5.halo, ...), custom_call_target="tpu_custom_call", output_to_operand_aliasing={{}: (0, {})} | custom-call | flops 1000000 | bytes 1000000 | tf_op jit(solution)/shard_map/pallas_call | solution.py:48
  29.3 5.1 %collective-permute-done.6.halo = f32[2,34,8,128]{3,2,1,0:T(8,128)S(1)} collective-permute-done((f32[2,34,8,128]{3,2,1,0:T(8,128)S(1)}, f32[2,34,8,128]{3,2,1,0:T(8,128)S(1)}, u32[]{:S(2)}, u32[]{:S(2)}) %collective-permute-start.6) | collective-permute-done | bytes 278560 | tf_op jit(solution)/shard_map/ppermute | solution.py:39
  34.4 0.9 %shard_map.83 = f32[2,3,34,8,128]{4,3,2,1,0:T(8,128)} custom-call(f32[2,3,34,8,128]{4,3,2,1,0:T(8,128)} %shard_map.82.begun, f32[2,34,8,128]{3,2,1,0:T(8,128)S(1)} %shard_map.78.before.mid0, f32[2,34,8,128]{3,2,1,0:T(8,128)S(1)} %shard_map.79.mid1, f32[2,34,8,128]{3,2,1,0:T(8,128)S(1)} %collective-permute-done.6.halo, ...), custom_call_target="tpu_custom_call", output_to_operand_aliasing={{}: (0, {})} | custom-call | flops 1000000 | bytes 1000000 | tf_op jit(solution)/shard_map/pallas_call | solution.py:48
  (1 shorter events, 0.0 us)
Async XLA Ops:
  0.0 10.2 %copy-start = (s32[2,2,3,34,256]{4,1,3,2,0:T(2,128)S(1)}, s32[2,2,3,34,256]{4,1,3,2,0:T(2,128)}, u32[]{:S(2)}) copy-start(s32[2,2,3,34,256]{4,1,3,2,0:T(2,128)} %param.8) | copy-start | bytes 1253380
  1.1 12.7 %collective-permute-start.3 = (f32[2,34,8,128]{3,2,1,0:T(8,128)S(1)}, f32[2,34,8,128]{3,2,1,0:T(8,128)S(1)}, u32[]{:S(2)}, u32[]{:S(2)}) collective-permute-start(f32[2,34,8,128]{3,2,1,0:T(8,128)S(1)} %shard_map.73.before.col2), channel_id=1, source_target_pairs={{0,4},{4,8},{8,12},{12,16},{16,20},{20,24},{24,28},{28,0},{1,5},{5... | collective-permute-start | bytes 835592 | tf_op jit(solution)/shard_map/ppermute | solution.py:39
  5.5 4.8 %collective-permute-start.1 = (f32[208,128]{1,0:T(8,128)S(1)}, f32[208,128]{1,0:T(8,128)S(1)}, u32[]{:S(2)}, u32[]{:S(2)}) collective-permute-start(f32[208,128]{1,0:T(8,128)S(1)} %get-tuple-element.14.own), channel_id=1, source_target_pairs={{0,2},{1,3},{2,0},{3,1},{4,6},{5,7},{6,4},{7,5},{8,10},{9,11},{10,... | collective-permute-start | bytes 319496 | tf_op jit(solution)/shard_map/ppermute | solution.py:44
  7.0 3.7 %collective-permute-start = (f32[208,128]{1,0:T(8,128)S(1)}, f32[208,128]{1,0:T(8,128)S(1)}, u32[]{:S(2)}, u32[]{:S(2)}) collective-permute-start(f32[208,128]{1,0:T(8,128)S(1)} %get-tuple-element.14.own), channel_id=1, source_target_pairs={{0,1},{1,0},{2,3},{3,2},{4,5},{5,4},{6,7},{7,6},{8,9},{9,8},{10,11... | collective-permute-start | bytes 319496 | tf_op jit(solution)/shard_map/ppermute | solution.py:44
  10.2 1.3 %collective-permute-start.2 = (f32[208,128]{1,0:T(8,128)S(1)}, f32[208,128]{1,0:T(8,128)S(1)}, u32[]{:S(2)}, u32[]{:S(2)}) collective-permute-start(f32[208,128]{1,0:T(8,128)S(1)} %collective-permute-done.1.second), channel_id=1, source_target_pairs={{0,1},{1,0},{2,3},{3,2},{4,5},{5,4},{6,7},{7,6},{8,9},{9,8},{10,11... | collective-permute-start | bytes 319496 | tf_op jit(solution)/shard_map/ppermute | solution.py:44
  13.8 10.4 %collective-permute-start.4 = (f32[616,128]{1,0:T(8,128)S(1)}, f32[616,128]{1,0:T(8,128)S(1)}, u32[]{:S(2)}, u32[]{:S(2)}) collective-permute-start(f32[616,128]{1,0:T(8,128)S(1)} %shard_map.77.message), channel_id=1, source_target_pairs={{0,28},{4,0},{8,4},{12,8},{16,12},{20,16},{24,20},{28,24},{1,29},{... | collective-permute-start | bytes 946184 | tf_op jit(solution)/shard_map/ppermute | solution.py:39
  16.3 12.1 %collective-permute-start.5 = (f32[2,34,8,128]{3,2,1,0:T(8,128)S(1)}, f32[2,34,8,128]{3,2,1,0:T(8,128)S(1)}, u32[]{:S(2)}, u32[]{:S(2)}) collective-permute-start(f32[2,34,8,128]{3,2,1,0:T(8,128)S(1)} %shard_map.78.before.mid0), channel_id=1, source_target_pairs={{0,28},{4,0},{8,4},{12,8},{16,12},{20,16},{24,20},{28,24},{1,29},{... | collective-permute-start | bytes 835592 | tf_op jit(solution)/shard_map/ppermute | solution.py:39
  25.0 9.5 %collective-permute-start.6 = (f32[2,34,8,128]{3,2,1,0:T(8,128)S(1)}, f32[2,34,8,128]{3,2,1,0:T(8,128)S(1)}, u32[]{:S(2)}, u32[]{:S(2)}) collective-permute-start(f32[2,34,8,128]{3,2,1,0:T(8,128)S(1)} %get-tuple-element.21.mid2), channel_id=1, source_target_pairs={{0,4},{4,8},{8,12},{12,16},{16,20},{20,24},{24,28},{28,0},{1,5},{5... | collective-permute-start | bytes 835592 | tf_op jit(solution)/shard_map/ppermute | solution.py:39

commit v9 on v8

--- a/solution.py
+++ b/solution.py
@@ -78,14 +78,11 @@
         copy.wait()
 
 
-def head_kernel(state, flags, mass, xf, yf, km, before, message, col1, packed, flags_v, mass_v, xf_v, yf_v, km_v, sems, column_sems):
-    tracers, columns, levels = state.shape[0], mass.shape[0], mass.shape[1]
+def head_kernel(flags, mass, xf, yf, km, before, packed, flags_v, mass_v, xf_v, yf_v, km_v, sems):
+    columns, levels = mass.shape[0], mass.shape[1]
     half = LANES // 2
     pairs = ((mass, mass_v), (xf, xf_v), (yf, yf_v), (km, km_v), (flags, flags_v))
     copies = [pltpu.make_async_copy(src, dst, sems.at[i]) for i, (src, dst) in enumerate(pairs)]
-    for t in range(tracers):
-        for c, place in ((0, message.at[pl.ds(t * levels, levels)]), (1, col1.at[t])):
-            copies.append(pltpu.make_async_copy(state.at[t, c], place, column_sems.at[c, t]))
     for copy in copies:
         copy.start()
     for copy in copies[:4]:
@@ -97,8 +94,7 @@
         packed[top : top + levels, :half] = yf_v[c]
         packed[top : top + levels - 1, half:] = km_v[c]
         packed[top + levels - 1 : top + levels, half:] = jnp.zeros((1, half), jnp.float32)
-    for copy in copies[4:]:
-        copy.wait()
+    copies[4].wait()
 
 
 def spread(upper_block, ref, *where):
@@ -110,9 +106,14 @@
     return rows - -(-2 * levels // 8) * 8 + b * levels
 
 
-def turn_kernel(switches, turn):
+def turn_kernel(state, switches, message, col1, turn, sems):
     tracers, columns = switches.shape[:2]
     levels = switches.shape[2] // 4
+    copies = []
+    for t in range(tracers):
+        for c, place in ((0, message.at[pl.ds(t * levels, levels)]), (1, col1.at[t])):
+            copies.append(pltpu.make_async_copy(state.at[t, c], place, sems.at[c, t]))
+            copies[-1].start()
     row = lax.broadcasted_iota(jnp.int32, (8, LANES), 0)
     moment = row % MOMENTS
     for t in range(tracers):
@@ -124,6 +125,8 @@
                     take = jnp.where(sw == 1, 1.0, jnp.where(sw == 2, -1.0, 0.0))
                     keep = jnp.where(sw == 0, 1.0, 0.0)
                     turn[d, t, c, l] = jnp.where(moment == 0, take, jnp.where(moment == 1 + d, keep, 1.0))
+    for copy in copies:
+        copy.wait()
 
 
 def sorted_shards(refs, order, start, count):
@@ -341,14 +344,14 @@
 
     col2 = call(first_kernel, column, (HBM,), [dma((tracers,))], 1, 1, stay(state))
     west_halo = shifted(col2, "lon", 1)
-    message, col1, packed, flag = call(
-        head_kernel,
-        (f32(length, 8, LANES), column, f32(rows, LANES), jax.ShapeDtypeStruct(flag.shape, flag.dtype)),
-        (HBM,) * 6 + (VMEM,), [pltpu.VMEM(x.shape, x.dtype) for x in fields] + [dma((5,)), dma((columns, tracers))],
-        10**5, 10**6, stay(state), stay(flag), *fields, col2)
+    packed, flag = call(
+        head_kernel, (f32(rows, LANES), jax.ShapeDtypeStruct(flag.shape, flag.dtype)), (HBM,) * 5 + (VMEM,),
+        [pltpu.VMEM(x.shape, x.dtype) for x in fields] + [dma((5,))], 10**5, 10**6, stay(flag), *fields, col2)
     across = swapped(packed, "trc", 2)
     others = [swapped(packed, "trc", 1), across, swapped(across, "trc", 1)]
-    turn = call(turn_kernel, f32(2, tracers, columns, levels, 8, LANES), (VMEM,), (), 10**6, 10**6, switch)
+    message, col1, turn = call(
+        turn_kernel, (f32(length, 8, LANES), column, f32(2, tracers, columns, levels, 8, LANES)), (HBM, VMEM),
+        [dma((2, tracers))], 10**6, 10**6, stay(state), switch)
     rates, factors, message = call(
         pre_kernel,
         (f32(4, columns, levels, 8, LANES), f32(3, columns, levels, 8, LANES), f32(length * 8, LANES)),

time: 35.5 us -> 35.4 us (level)
  starting transfers between devices: 9.18 us -> 8.59 us
  Pallas kernels: 8.78 us -> 9.16 us
    ppermute x4, waiting for transfers between devices: 13.3 us -> 14.1 us  [shifted(): lax.ppermute(value, axis, [(i, (i + by) % count) for i in range(count)])]
    ppermute x3, waiting for transfers between devices: 4.02 us -> 3.36 us  [swapped(): return lax.ppermute(value, axis, [(i, i ^ mask) for i in range(count)])]
    ppermute x4, starting transfers between devices: 7.62 us -> 7.03 us  [shifted(): lax.ppermute(value, axis, [(i, (i + by) % count) for i in range(count)])]
    pallas_call x11, Pallas kernels: 8.78 us -> 9.16 us  [call(): pl.pallas_call(kernel, out_shape=out, in_specs=in_specs, out_specs=jax.tr...]
  transfers between devices with their start and end apart: 7 -> 7, of which waited for: 6 -> 6; matrix products, arithmetic and copies ran while one was open for 0% -> 0% of each run, Pallas kernels for 19% -> 20%
where the time goes in v9:
time: 35.4 us; the launch traced here: 35.3 us
  waiting for transfers between devices  17.4 us (49%)
  Pallas kernels  9.16 us (26%)
  starting transfers between devices  8.59 us (24%)
    ppermute x4, waiting for transfers between devices, shifted(): lax.ppermute(value, axis, [(i, (i + by) % count) for i in range(count)])  14.1 us
    pallas_call x11, Pallas kernels, call(): pl.pallas_call(kernel, out_shape=out, in_specs=in_specs, out_specs=jax.tr...  9.16 us
    ppermute x4, starting transfers between devices, shifted(): lax.ppermute(value, axis, [(i, (i + by) % count) for i in range(count)])  7.03 us
    ppermute x3, waiting for transfers between devices, swapped(): return lax.ppermute(value, axis, [(i, i ^ mask) for i in range(count)])  3.36 us
    ppermute x3, starting transfers between devices, swapped(): return lax.ppermute(value, axis, [(i, i ^ mask) for i in range(count)])  1.56 us
  transfers between devices with their start and end apart: 7, of which 6 were waited for; matrix products, arithmetic and copies ran while one was open for 0% of the time, Pallas kernels for 20%

profile of v9, /device:TPU:0, one launch (start us, length us, event | category | flops | bytes accessed | tf_op | source)
XLA Modules:
  0.0 35.3 jit_solution(10317399179571978526)
XLA Ops:
  0.0 0.0 copy-start
  0.0 1.0 %shard_map.73.before.col2 = f32[2,34,8,128]{3,2,1,0:T(8,128)S(1)} custom-call(f32[2,3,34,8,128]{4,3,2,1,0:T(8,128)} %bitcast.24), custom_call_target="tpu_custom_call" | custom-call | flops 1 | bytes 1 | tf_op jit(solution)/shard_map/pallas_call | solution.py:48
  1.1 3.0 %collective-permute-start.3 = (f32[2,34,8,128]{3,2,1,0:T(8,128)S(1)}, f32[2,34,8,128]{3,2,1,0:T(8,128)S(1)}, u32[]{:S(2)}, u32[]{:S(2)}) collective-permute-start(f32[2,34,8,128]{3,2,1,0:T(8,128)S(1)} %shard_map.73.before.col2), channel_id=1, source_target_pairs={{0,4},{4,8},{8,12},{12,16},{16,20},{20,24},{24,28},{28,0},{1,5},{5... | collective-permute-start | bytes 835592 | tf_op jit(solution)/shard_map/ppermute | solution.py:39
  4.1 1.1 %shard_map.74 = (f32[208,128]{1,0:T(8,128)S(1)}, s32[3,136,128]{2,1,0:T(8,128)S(1)}) custom-call(s32[3,136,128]{2,1,0:T(8,128)} %bitcast.26, f32[3,34,64]{2,1,0:T(8,128)} %mass.1, f32[3,34,64]{2,1,0:T(8,128)} %xf.1, f32[3,34,64]{2,1,0:T(8,128)} %yf.1, f32[3,33,64]{2,1,0:T(8,128)} %km.1, f32[2,34,8,128]{3,2,1,0:T(8,128)S(1)} %shard_map.73.before.col2), custom_call_target="tpu_custom_call" | custom-call | flops 100000 | bytes 1000000 | tf_op jit(solution)/shard_map/pallas_call | solution.py:48
  5.2 1.6 %collective-permute-start.1 = (f32[208,128]{1,0:T(8,128)S(1)}, f32[208,128]{1,0:T(8,128)S(1)}, u32[]{:S(2)}, u32[]{:S(2)}) collective-permute-start(f32[208,128]{1,0:T(8,128)S(1)} %get-tuple-element.15.own), channel_id=1, source_target_pairs={{0,2},{1,3},{2,0},{3,1},{4,6},{5,7},{6,4},{7,5},{8,10},{9,11},{10,... | collective-permute-start | bytes 319496 | tf_op jit(solution)/shard_map/ppermute | solution.py:44
  6.7 0.0 collective-permute-start
  6.7 3.2 %collective-permute-done.1.second = f32[208,128]{1,0:T(8,128)S(1)} collective-permute-done((f32[208,128]{1,0:T(8,128)S(1)}, f32[208,128]{1,0:T(8,128)S(1)}, u32[]{:S(2)}, u32[]{:S(2)}) %collective-permute-start.1) | collective-permute-done | bytes 106528 | tf_op jit(solution)/shard_map/ppermute | solution.py:44
  9.9 0.0 collective-permute-start.2
  9.9 0.0 copy-done
  9.9 1.1 %shard_map.75 = (f32[77,8,128]{2,1,0:T(8,128)S(1)}, f32[2,34,8,128]{3,2,1,0:T(8,128)S(1)}, f32[2,2,3,34,8,128]{5,4,3,2,1,0:T(8,128)S(1)}) custom-call(f32[2,3,34,8,128]{4,3,2,1,0:T(8,128)} %bitcast.25, s32[2,3,136,128]{3,2,1,0:T(8,128)S(1)} %bitcast.23), custom_call_target="tpu_custom_call" | custom-call | flops 1000000 | bytes 1000000 | tf_op jit(solution)/shard_map/pallas_call | solution.py:48
  11.1 0.0 collective-permute-done.first
  11.1 0.1 collective-permute-done.2.third
  11.3 0.7 %shard_map.76 = (f32[4,3,34,8,128]{4,3,2,1,0:T(8,128)S(1)}, f32[3,3,34,8,128]{4,3,2,1,0:T(8,128)S(1)}, f32[616,128]{1,0:T(8,128)S(1)}) custom-call(f32[208,128]{1,0:T(8,128)S(1)} %get-tuple-element.15.own, f32[208,128]{1,0:T(8,128)S(1)} %collective-permute-done.first, f32[208,128]{1,0:T(8,128)S(1)} %collective-permute-done.1.second, ...), custom_call_target="tpu_custom_call", output_to_operand_aliasing={{2}: (6, {})} | custom-call | flops 1 | bytes 1 | tf_op jit(solution)/shard_map/pallas_call | solution.py:48
  12.0 1.8 %collective-permute-done.3.before.west_halo = f32[2,34,8,128]{3,2,1,0:T(8,128)S(1)} collective-permute-done((f32[2,34,8,128]{3,2,1,0:T(8,128)S(1)}, f32[2,34,8,128]{3,2,1,0:T(8,128)S(1)}, u32[]{:S(2)}, u32[]{:S(2)}) %collective-permute-start.3) | collective-permute-done | bytes 278560 | tf_op jit(solution)/shard_map/ppermute | solution.py:39
  13.8 1.7 %collective-permute-start.4 = (f32[616,128]{1,0:T(8,128)S(1)}, f32[616,128]{1,0:T(8,128)S(1)}, u32[]{:S(2)}, u32[]{:S(2)}) collective-permute-start(f32[616,128]{1,0:T(8,128)S(1)} %shard_map.77.message), channel_id=1, source_target_pairs={{0,28},{4,0},{8,4},{12,8},{16,12},{20,16},{24,20},{28,24},{1,29},{... | collective-permute-start | bytes 946184 | tf_op jit(solution)/shard_map/ppermute | solution.py:39
  15.5 0.8 %shard_map.78.before.mid0 = f32[2,34,8,128]{3,2,1,0:T(8,128)S(1)} custom-call(f32[616,128]{1,0:T(8,128)S(1)} %shard_map.77.message, f32[2,34,8,128]{3,2,1,0:T(8,128)S(1)} %get-tuple-element.20.col1, f32[2,34,8,128]{3,2,1,0:T(8,128)S(1)} %collective-permute-done.3.before.west_halo, f32[4,3,34,8,128]{4,3,2,1,0:T(8,128)S(1)} %get-tuple-element.21.rates, ...), custom_call_target="tpu_custom_call" | custom-call | flops 1000000 | bytes 1000000 | tf_op jit(solution)/shard_map/pallas_call | solution.py:48
  16.3 1.6 %collective-permute-start.5 = (f32[2,34,8,128]{3,2,1,0:T(8,128)S(1)}, f32[2,34,8,128]{3,2,1,0:T(8,128)S(1)}, u32[]{:S(2)}, u32[]{:S(2)}) collective-permute-start(f32[2,34,8,128]{3,2,1,0:T(8,128)S(1)} %shard_map.78.before.mid0), channel_id=1, source_target_pairs={{0,28},{4,0},{8,4},{12,8},{16,12},{20,16},{24,20},{28,24},{1,29},{... | collective-permute-start | bytes 835592 | tf_op jit(solution)/shard_map/ppermute | solution.py:39
  18.0 6.2 %collective-permute-done.4.halo = f32[616,128]{1,0:T(8,128)S(1)} collective-permute-done((f32[616,128]{1,0:T(8,128)S(1)}, f32[616,128]{1,0:T(8,128)S(1)}, u32[]{:S(2)}, u32[]{:S(2)}) %collective-permute-start.4) | collective-permute-done | bytes 315424 | tf_op jit(solution)/shard_map/ppermute | solution.py:39
  24.2 0.8 %shard_map.80 = (f32[2,34,8,128]{3,2,1,0:T(8,128)S(1)}, f32[34,8,128]{2,1,0:T(8,128)S(1)}) custom-call(f32[2,34,8,128]{3,2,1,0:T(8,128)S(1)} %get-tuple-element.20.col1, f32[2,34,8,128]{3,2,1,0:T(8,128)S(1)} %shard_map.73.before.col2, f32[616,128]{1,0:T(8,128)S(1)} %collective-permute-done.4.halo, f32[4,3,34,8,128]{4,3,2,1,0:T(8,128)S(1)} %get-tuple-element.21.rates, ...), custom_call_target="tpu_custom_call" | custom-call | flops 1000000 | bytes 1000000 | tf_op jit(solution)/shard_map/pallas_call | solution.py:48
  25.0 0.6 %collective-permute-start.6 = (f32[2,34,8,128]{3,2,1,0:T(8,128)S(1)}, f32[2,34,8,128]{3,2,1,0:T(8,128)S(1)}, u32[]{:S(2)}, u32[]{:S(2)}) collective-permute-start(f32[2,34,8,128]{3,2,1,0:T(8,128)S(1)} %get-tuple-element.23.mid2), channel_id=1, source_target_pairs={{0,4},{4,8},{8,12},{12,16},{16,20},{20,24},{24,28},{28,0},{1,5},{5... | collective-permute-start | bytes 835592 | tf_op jit(solution)/shard_map/ppermute | solution.py:39
  25.6 0.8 %shard_map.79.mid1 = f32[2,34,8,128]{3,2,1,0:T(8,128)S(1)} custom-call(f32[616,128]{1,0:T(8,128)S(1)} %shard_map.77.message, f32[2,34,8,128]{3,2,1,0:T(8,128)S(1)} %get-tuple-element.20.col1, f32[2,34,8,128]{3,2,1,0:T(8,128)S(1)} %shard_map.73.before.col2, f32[4,3,34,8,128]{4,3,2,1,0:T(8,128)S(1)} %get-tuple-element.21.rates, ...), custom_call_target="tpu_custom_call" | custom-call | flops 1000000 | bytes 1000000 | tf_op jit(solution)/shard_map/pallas_call | solution.py:48
  26.4 0.9 %shard_map.81.begun = f32[2,3,34,8,128]{4,3,2,1,0:T(8,128)} custom-call(f32[2,34,8,128]{3,2,1,0:T(8,128)S(1)} %shard_map.78.before.mid0, f32[2,34,8,128]{3,2,1,0:T(8,128)S(1)} %shard_map.79.mid1, f32[2,34,8,128]{3,2,1,0:T(8,128)S(1)} %get-tuple-element.23.mid2, f32[4,3,34,8,128]{4,3,2,1,0:T(8,128)S(1)} %get-tuple-element.21.rates, ...), custom_call_target="tpu_custom_call" | custom-call | flops 1000000 | bytes 1000000 | tf_op jit(solution)/shard_map/pallas_call | solution.py:48
  27.3 1.0 %collective-permute-done.5.halo = f32[2,34,8,128]{3,2,1,0:T(8,128)S(1)} collective-permute-done((f32[2,34,8,128]{3,2,1,0:T(8,128)S(1)}, f32[2,34,8,128]{3,2,1,0:T(8,128)S(1)}, u32[]{:S(2)}, u32[]{:S(2)}) %collective-permute-start.5) | collective-permute-done | bytes 278560 | tf_op jit(solution)/shard_map/ppermute | solution.py:39
  28.4 0.9 %shard_map.82.begun = f32[2,3,34,8,128]{4,3,2,1,0:T(8,128)} custom-call(f32[2,3,34,8,128]{4,3,2,1,0:T(8,128)} %shard_map.81.begun, f32[2,34,8,128]{3,2,1,0:T(8,128)S(1)} %shard_map.79.mid1, f32[2,34,8,128]{3,2,1,0:T(8,128)S(1)} %get-tuple-element.23.mid2, f32[2,34,8,128]{3,2,1,0:T(8,128)S(1)} %collective-permute-done.5.halo, ...), custom_call_target="tpu_custom_call", output_to_operand_aliasing={{}: (0, {})} | custom-call | flops 1000000 | bytes 1000000 | tf_op jit(solution)/shard_map/pallas_call | solution.py:48
  29.3 5.0 %collective-permute-done.6.halo = f32[2,34,8,128]{3,2,1,0:T(8,128)S(1)} collective-permute-done((f32[2,34,8,128]{3,2,1,0:T(8,128)S(1)}, f32[2,34,8,128]{3,2,1,0:T(8,128)S(1)}, u32[]{:S(2)}, u32[]{:S(2)}) %collective-permute-start.6) | collective-permute-done | bytes 278560 | tf_op jit(solution)/shard_map/ppermute | solution.py:39
  34.3 0.9 %shard_map.83 = f32[2,3,34,8,128]{4,3,2,1,0:T(8,128)} custom-call(f32[2,3,34,8,128]{4,3,2,1,0:T(8,128)} %shard_map.82.begun, f32[2,34,8,128]{3,2,1,0:T(8,128)S(1)} %shard_map.78.before.mid0, f32[2,34,8,128]{3,2,1,0:T(8,128)S(1)} %shard_map.79.mid1, f32[2,34,8,128]{3,2,1,0:T(8,128)S(1)} %collective-permute-done.6.halo, ...), custom_call_target="tpu_custom_call", output_to_operand_aliasing={{}: (0, {})} | custom-call | flops 1000000 | bytes 1000000 | tf_op jit(solution)/shard_map/pallas_call | solution.py:48
  (1 shorter events, 0.0 us)
Async XLA Ops:
  0.0 9.9 %copy-start = (s32[2,2,3,34,256]{4,1,3,2,0:T(2,128)S(1)}, s32[2,2,3,34,256]{4,1,3,2,0:T(2,128)}, u32[]{:S(2)}) copy-start(s32[2,2,3,34,256]{4,1,3,2,0:T(2,128)} %param.8) | copy-start | bytes 1253380
  1.1 12.7 %collective-permute-start.3 = (f32[2,34,8,128]{3,2,1,0:T(8,128)S(1)}, f32[2,34,8,128]{3,2,1,0:T(8,128)S(1)}, u32[]{:S(2)}, u32[]{:S(2)}) collective-permute-start(f32[2,34,8,128]{3,2,1,0:T(8,128)S(1)} %shard_map.73.before.col2), channel_id=1, source_target_pairs={{0,4},{4,8},{8,12},{12,16},{16,20},{20,24},{24,28},{28,0},{1,5},{5... | collective-permute-start | bytes 835592 | tf_op jit(solution)/shard_map/ppermute | solution.py:39
  5.2 4.8 %collective-permute-start.1 = (f32[208,128]{1,0:T(8,128)S(1)}, f32[208,128]{1,0:T(8,128)S(1)}, u32[]{:S(2)}, u32[]{:S(2)}) collective-permute-start(f32[208,128]{1,0:T(8,128)S(1)} %get-tuple-element.15.own), channel_id=1, source_target_pairs={{0,2},{1,3},{2,0},{3,1},{4,6},{5,7},{6,4},{7,5},{8,10},{9,11},{10,... | collective-permute-start | bytes 319496 | tf_op jit(solution)/shard_map/ppermute | solution.py:44
  6.7 4.4 %collective-permute-start = (f32[208,128]{1,0:T(8,128)S(1)}, f32[208,128]{1,0:T(8,128)S(1)}, u32[]{:S(2)}, u32[]{:S(2)}) collective-permute-start(f32[208,128]{1,0:T(8,128)S(1)} %get-tuple-element.15.own), channel_id=1, source_target_pairs={{0,1},{1,0},{2,3},{3,2},{4,5},{5,4},{6,7},{7,6},{8,9},{9,8},{10,11... | collective-permute-start | bytes 319496 | tf_op jit(solution)/shard_map/ppermute | solution.py:44
  9.9 1.3 %collective-permute-start.2 = (f32[208,128]{1,0:T(8,128)S(1)}, f32[208,128]{1,0:T(8,128)S(1)}, u32[]{:S(2)}, u32[]{:S(2)}) collective-permute-start(f32[208,128]{1,0:T(8,128)S(1)} %collective-permute-done.1.second), channel_id=1, source_target_pairs={{0,1},{1,0},{2,3},{3,2},{4,5},{5,4},{6,7},{7,6},{8,9},{9,8},{10,11... | collective-permute-start | bytes 319496 | tf_op jit(solution)/shard_map/ppermute | solution.py:44
  13.8 10.4 %collective-permute-start.4 = (f32[616,128]{1,0:T(8,128)S(1)}, f32[616,128]{1,0:T(8,128)S(1)}, u32[]{:S(2)}, u32[]{:S(2)}) collective-permute-start(f32[616,128]{1,0:T(8,128)S(1)} %shard_map.77.message), channel_id=1, source_target_pairs={{0,28},{4,0},{8,4},{12,8},{16,12},{20,16},{24,20},{28,24},{1,29},{... | collective-permute-start | bytes 946184 | tf_op jit(solution)/shard_map/ppermute | solution.py:39
  16.3 12.1 %collective-permute-start.5 = (f32[2,34,8,128]{3,2,1,0:T(8,128)S(1)}, f32[2,34,8,128]{3,2,1,0:T(8,128)S(1)}, u32[]{:S(2)}, u32[]{:S(2)}) collective-permute-start(f32[2,34,8,128]{3,2,1,0:T(8,128)S(1)} %shard_map.78.before.mid0), channel_id=1, source_target_pairs={{0,28},{4,0},{8,4},{12,8},{16,12},{20,16},{24,20},{28,24},{1,29},{... | collective-permute-start | bytes 835592 | tf_op jit(solution)/shard_map/ppermute | solution.py:39
  25.0 9.4 %collective-permute-start.6 = (f32[2,34,8,128]{3,2,1,0:T(8,128)S(1)}, f32[2,34,8,128]{3,2,1,0:T(8,128)S(1)}, u32[]{:S(2)}, u32[]{:S(2)}) collective-permute-start(f32[2,34,8,128]{3,2,1,0:T(8,128)S(1)} %get-tuple-element.23.mid2), channel_id=1, source_target_pairs={{0,4},{4,8},{8,12},{12,16},{16,20},{20,24},{24,28},{28,0},{1,5},{5... | collective-permute-start | bytes 835592 | tf_op jit(solution)/shard_map/ppermute | solution.py:39

commit v10 on v9

--- a/solution.py
+++ b/solution.py
@@ -1,3 +1,5 @@
+import functools
+
 import jax
 import jax.numpy as jnp
 from jax import lax
@@ -298,36 +300,75 @@
     middle(2, tiles(col2, levels), tiles(halo, levels), tiles(col1, levels), east_rate, rates, factors, turn, out)
 
 
-def finish(c, own, east_side, west_side, east_rate, rates, turn, out, buf, sems):
+def local_part(own, near, near_rate, far_rate, sign, masks):
+    is_slope = masks[1]
+    stay_rate = 1.0 - (near_rate + far_rate)
+    near_part = near_rate * jnp.where(is_slope, near_rate, 1.0)
+    near_cross = sign * near_rate * (1.0 - near_rate)
+    far_cross = -sign * far_rate * (1.0 - far_rate)
+    return [stay_rate * s + near_part * n
+            + jnp.where(is_slope, pltpu.roll(near_cross * (n - s) - far_cross * s, 1, 0), 0.0) for s, n in zip(own, near)]
+
+
+def far_part(local, far, far_rate, sign, turns, masks):
+    is_mass, is_slope = masks
+    part = far_rate * jnp.where(is_slope, far_rate, 1.0)
+    cross = -sign * far_rate * (1.0 - far_rate)
+    out = []
+    for p, f, z in zip(local, far, turns):
+        total = p + part * f + jnp.where(is_slope, pltpu.roll(cross * f, 1, 0), 0.0)
+        slope_up = pltpu.roll(total, 7, 0)
+        out.append(z * jnp.where(is_mass, slope_up, total) + jnp.where(is_mass, total, 0.0))
+    return out
+
+
+def finish(c, values, out, buf, sems):
     tracers, levels = buf.shape[0], buf.shape[1]
-    masks = tile_masks(1)
-    every = range(tracers)
     copies = []
     for part in range(PARTS):
         low, high = part * levels // PARTS, (part + 1) * levels // PARTS
         for l in range(low, high):
-            values = advect(*([side[t, l] for t in every] for side in (own, east_side, west_side)),
-                            east_rate(l), rates[1, c, l], [turn[0, t, c, l] for t in every], 1, masks)
-            for t in every:
-                buf[t, l] = values[t]
-        for t in every:
+            for t, value in enumerate(values(l)):
+                buf[t, l] = value
+        for t in range(tracers):
             span = pl.ds(low, high - low)
             copies.append(pltpu.make_async_copy(buf.at[t, span], out.at[t, c, span], sems.at[part, t]))
             copies[-1].start()
+    return copies
+
+
+def last_inner_kernel(mid0, mid1, mid2, rates, east, turn, out, local0, local2, buf, sems):
+    tracers, levels = buf.shape[0], buf.shape[1]
+    every = range(tracers)
+    masks = tile_masks(1)
+
+    def values(l):
+        return advect(*([side[t, l] for t in every] for side in (mid1, mid2, mid0)), rates[0, 1, l], rates[1, 1, l],
+                      [turn[0, t, 1, l] for t in every], 1, masks)
+
+    copies = finish(1, values, out, buf, sems)
+    for l in range(levels):
+        inner = [mid1[t, l] for t in every]
+        first = local_part([mid0[t, l] for t in every], inner, rates[0, 0, l], rates[1, 0, l], 1.0, masks)
+        final = local_part([mid2[t, l] for t in every], inner, rates[1, 2, l], east[l], -1.0, masks)
+        for t in every:
+            local0[t, l] = first[t]
+            local2[t, l] = final[t]
     for copy in copies:
         copy.wait()
 
 
-def last_inner_kernel(mid0, mid1, mid2, rates, turn, out, buf, sems):
-    finish(1, mid1, mid2, mid0, lambda l: rates[0, 1, l], rates, turn, out, buf, sems)
-
-
-def last_east_kernel(begun, mid1, mid2, halo, east, rates, turn, out, buf, sems):
-    finish(2, mid2, halo, mid1, lambda l: east[l], rates, turn, out, buf, sems)
-
-
-def last_west_kernel(begun, mid0, mid1, halo, rates, turn, out, buf, sems):
-    finish(0, mid0, mid1, halo, lambda l: rates[0, 0, l], rates, turn, out, buf, sems)
+def last_outer_kernel(c, begun, local, halo, far_rate, turn, out, buf, sems):
+    every = range(buf.shape[0])
+    masks = tile_masks(1)
+
+    def values(l):
+        rate = far_rate[l] if c else far_rate[1, c, l]
+        return far_part([local[t, l] for t in every], [halo[t, l] for t in every], rate, -1.0 if c else 1.0,
+                        [turn[0, t, c, l] for t in every], masks)
+
+    for copy in finish(c, values, out, buf, sems):
+        copy.wait()
 
 
 def body(state_adjoint, switches, flags, air_mass, x_flux, y_flux, vertical_mixing):
@@ -366,15 +407,12 @@
                       col1, col2, east_message, rates, factors, turn, mid0)
     west_halo = shifted(mid2, "lon", 1)
 
-    def last(kernel, aliases, *args):
-        first = (HBM,) * len(aliases)
-        return call(kernel, f32(*state.shape), first + (VMEM,) * (len(args) - len(first)),
-                    [pltpu.VMEM(column.shape, jnp.float32), dma((PARTS, tracers))], 10**6, 10**6,
-                    *args, out_specs=HBM, aliases=aliases)
-
-    out = last(last_inner_kernel, {}, mid0, mid1, mid2, rates, turn)
-    out = last(last_east_kernel, {0: 0}, out, mid1, mid2, east_halo, east, rates, turn)
-    out = last(last_west_kernel, {0: 0}, out, mid0, mid1, west_halo, rates, turn)
+    scratch = [pltpu.VMEM(column.shape, jnp.float32), dma((PARTS, tracers))]
+    out, local0, local2 = call(last_inner_kernel, (f32(*state.shape), column, column), (VMEM,) * 6, scratch,
+                               10**6, 10**6, mid0, mid1, mid2, rates, east, turn, out_specs=(HBM, VMEM, VMEM))
+    for c, local, halo, rate in ((2, local2, east_halo, east), (0, local0, west_halo, rates)):
+        out = call(functools.partial(last_outer_kernel, c), f32(*state.shape), (HBM,) + (VMEM,) * 4, scratch,
+                   10**6, 10**6, out, local, halo, rate, turn, out_specs=HBM, aliases={0: 0})
     return state_back(out)
 
 

time: 35.4 us -> 35.3 us (level)
  no operation moved by 1% of the time
where the time goes in v10:
time: 35.3 us; the launch traced here: 35.2 us
  waiting for transfers between devices  17.5 us (50%)
  Pallas kernels  8.98 us (25%)
  starting transfers between devices  8.59 us (24%)
    ppermute x4, waiting for transfers between devices, shifted(): lax.ppermute(value, axis, [(i, (i + by) % count) for i in range(count)])  14.2 us
    pallas_call x11, Pallas kernels, call(): pl.pallas_call(kernel, out_shape=out, in_specs=in_specs, out_specs=jax.tr...  8.98 us
    ppermute x4, starting transfers between devices, shifted(): lax.ppermute(value, axis, [(i, (i + by) % count) for i in range(count)])  7.03 us
    ppermute x3, waiting for transfers between devices, swapped(): return lax.ppermute(value, axis, [(i, i ^ mask) for i in range(count)])  3.36 us
    ppermute x3, starting transfers between devices, swapped(): return lax.ppermute(value, axis, [(i, i ^ mask) for i in range(count)])  1.56 us
  transfers between devices with their start and end apart: 7, of which 6 were waited for; matrix products, arithmetic and copies ran while one was open for 0% of the time, Pallas kernels for 20%

profile of v10, /device:TPU:0, one launch (start us, length us, event | category | flops | bytes accessed | tf_op | source)
XLA Modules:
  0.0 35.2 jit_solution(1642183611503843808)
XLA Ops:
  0.0 0.0 copy-start
  0.0 1.0 %shard_map.73.before.col2 = f32[2,34,8,128]{3,2,1,0:T(8,128)S(1)} custom-call(f32[2,3,34,8,128]{4,3,2,1,0:T(8,128)} %bitcast.24), custom_call_target="tpu_custom_call" | custom-call | flops 1 | bytes 1 | tf_op jit(solution)/shard_map/pallas_call | solution.py:50
  1.1 3.0 %collective-permute-start.3 = (f32[2,34,8,128]{3,2,1,0:T(8,128)S(1)}, f32[2,34,8,128]{3,2,1,0:T(8,128)S(1)}, u32[]{:S(2)}, u32[]{:S(2)}) collective-permute-start(f32[2,34,8,128]{3,2,1,0:T(8,128)S(1)} %shard_map.73.before.col2), channel_id=1, source_target_pairs={{0,4},{4,8},{8,12},{12,16},{16,20},{20,24},{24,28},{28,0},{1,5},{5... | collective-permute-start | bytes 835592 | tf_op jit(solution)/shard_map/ppermute | solution.py:41
  4.1 1.1 %shard_map.74 = (f32[208,128]{1,0:T(8,128)S(1)}, s32[3,136,128]{2,1,0:T(8,128)S(1)}) custom-call(s32[3,136,128]{2,1,0:T(8,128)} %bitcast.26, f32[3,34,64]{2,1,0:T(8,128)} %mass.1, f32[3,34,64]{2,1,0:T(8,128)} %xf.1, f32[3,34,64]{2,1,0:T(8,128)} %yf.1, f32[3,33,64]{2,1,0:T(8,128)} %km.1, f32[2,34,8,128]{3,2,1,0:T(8,128)S(1)} %shard_map.73.before.col2), custom_call_target="tpu_custom_call" | custom-call | flops 100000 | bytes 1000000 | tf_op jit(solution)/shard_map/pallas_call | solution.py:50
  5.2 1.6 %collective-permute-start.1 = (f32[208,128]{1,0:T(8,128)S(1)}, f32[208,128]{1,0:T(8,128)S(1)}, u32[]{:S(2)}, u32[]{:S(2)}) collective-permute-start(f32[208,128]{1,0:T(8,128)S(1)} %get-tuple-element.18.own), channel_id=1, source_target_pairs={{0,2},{1,3},{2,0},{3,1},{4,6},{5,7},{6,4},{7,5},{8,10},{9,11},{10,... | collective-permute-start | bytes 319496 | tf_op jit(solution)/shard_map/ppermute | solution.py:46
  6.7 0.0 collective-permute-start
  6.7 3.2 %collective-permute-done.1.second = f32[208,128]{1,0:T(8,128)S(1)} collective-permute-done((f32[208,128]{1,0:T(8,128)S(1)}, f32[208,128]{1,0:T(8,128)S(1)}, u32[]{:S(2)}, u32[]{:S(2)}) %collective-permute-start.1) | collective-permute-done | bytes 106528 | tf_op jit(solution)/shard_map/ppermute | solution.py:46
  9.9 0.0 collective-permute-start.2
  9.9 0.0 copy-done
  9.9 1.1 %shard_map.75 = (f32[77,8,128]{2,1,0:T(8,128)S(1)}, f32[2,34,8,128]{3,2,1,0:T(8,128)S(1)}, f32[2,2,3,34,8,128]{5,4,3,2,1,0:T(8,128)S(1)}) custom-call(f32[2,3,34,8,128]{4,3,2,1,0:T(8,128)} %bitcast.25, s32[2,3,136,128]{3,2,1,0:T(8,128)S(1)} %bitcast.23), custom_call_target="tpu_custom_call" | custom-call | flops 1000000 | bytes 1000000 | tf_op jit(solution)/shard_map/pallas_call | solution.py:50
  11.1 0.0 collective-permute-done.first
  11.1 0.1 collective-permute-done.2.third
  11.3 0.7 %shard_map.76 = (f32[4,3,34,8,128]{4,3,2,1,0:T(8,128)S(1)}, f32[3,3,34,8,128]{4,3,2,1,0:T(8,128)S(1)}, f32[616,128]{1,0:T(8,128)S(1)}) custom-call(f32[208,128]{1,0:T(8,128)S(1)} %get-tuple-element.18.own, f32[208,128]{1,0:T(8,128)S(1)} %collective-permute-done.first, f32[208,128]{1,0:T(8,128)S(1)} %collective-permute-done.1.second, ...), custom_call_target="tpu_custom_call", output_to_operand_aliasing={{2}: (6, {})} | custom-call | flops 1 | bytes 1 | tf_op jit(solution)/shard_map/pallas_call | solution.py:50
  12.0 1.8 %collective-permute-done.3.before.west_halo = f32[2,34,8,128]{3,2,1,0:T(8,128)S(1)} collective-permute-done((f32[2,34,8,128]{3,2,1,0:T(8,128)S(1)}, f32[2,34,8,128]{3,2,1,0:T(8,128)S(1)}, u32[]{:S(2)}, u32[]{:S(2)}) %collective-permute-start.3) | collective-permute-done | bytes 278560 | tf_op jit(solution)/shard_map/ppermute | solution.py:41
  13.8 1.7 %collective-permute-start.4 = (f32[616,128]{1,0:T(8,128)S(1)}, f32[616,128]{1,0:T(8,128)S(1)}, u32[]{:S(2)}, u32[]{:S(2)}) collective-permute-start(f32[616,128]{1,0:T(8,128)S(1)} %shard_map.77.message), channel_id=1, source_target_pairs={{0,28},{4,0},{8,4},{12,8},{16,12},{20,16},{24,20},{28,24},{1,29},{... | collective-permute-start | bytes 946184 | tf_op jit(solution)/shard_map/ppermute | solution.py:41
  15.5 0.8 %shard_map.78.before.mid0 = f32[2,34,8,128]{3,2,1,0:T(8,128)S(1)} custom-call(f32[616,128]{1,0:T(8,128)S(1)} %shard_map.77.message, f32[2,34,8,128]{3,2,1,0:T(8,128)S(1)} %get-tuple-element.23.col1, f32[2,34,8,128]{3,2,1,0:T(8,128)S(1)} %collective-permute-done.3.before.west_halo, f32[4,3,34,8,128]{4,3,2,1,0:T(8,128)S(1)} %get-tuple-element.24.rates.far_rate, ...), custom_call_target="tpu_custom_call" | custom-call | flops 1000000 | bytes 1000000 | tf_op jit(solution)/shard_map/pallas_call | solution.py:50
  16.3 1.6 %collective-permute-start.5 = (f32[2,34,8,128]{3,2,1,0:T(8,128)S(1)}, f32[2,34,8,128]{3,2,1,0:T(8,128)S(1)}, u32[]{:S(2)}, u32[]{:S(2)}) collective-permute-start(f32[2,34,8,128]{3,2,1,0:T(8,128)S(1)} %shard_map.78.before.mid0), channel_id=1, source_target_pairs={{0,28},{4,0},{8,4},{12,8},{16,12},{20,16},{24,20},{28,24},{1,29},{... | collective-permute-start | bytes 835592 | tf_op jit(solution)/shard_map/ppermute | solution.py:41
  18.0 6.2 %collective-permute-done.4.halo = f32[616,128]{1,0:T(8,128)S(1)} collective-permute-done((f32[616,128]{1,0:T(8,128)S(1)}, f32[616,128]{1,0:T(8,128)S(1)}, u32[]{:S(2)}, u32[]{:S(2)}) %collective-permute-start.4) | collective-permute-done | bytes 315424 | tf_op jit(solution)/shard_map/ppermute | solution.py:41
  24.2 0.8 %shard_map.80 = (f32[2,34,8,128]{3,2,1,0:T(8,128)S(1)}, f32[34,8,128]{2,1,0:T(8,128)S(1)}) custom-call(f32[2,34,8,128]{3,2,1,0:T(8,128)S(1)} %get-tuple-element.23.col1, f32[2,34,8,128]{3,2,1,0:T(8,128)S(1)} %shard_map.73.before.col2, f32[616,128]{1,0:T(8,128)S(1)} %collective-permute-done.4.halo, ...), custom_call_target="tpu_custom_call" | custom-call | flops 1000000 | bytes 1000000 | tf_op jit(solution)/shard_map/pallas_call | solution.py:50
  25.0 0.6 %collective-permute-start.6 = (f32[2,34,8,128]{3,2,1,0:T(8,128)S(1)}, f32[2,34,8,128]{3,2,1,0:T(8,128)S(1)}, u32[]{:S(2)}, u32[]{:S(2)}) collective-permute-start(f32[2,34,8,128]{3,2,1,0:T(8,128)S(1)} %get-tuple-element.26.mid2), channel_id=1, source_target_pairs={{0,4},{4,8},{8,12},{12,16},{16,20},{20,24},{24,28},{28,0},{1,5},{5... | collective-permute-start | bytes 835592 | tf_op jit(solution)/shard_map/ppermute | solution.py:41
  25.6 0.8 %shard_map.79.mid1 = f32[2,34,8,128]{3,2,1,0:T(8,128)S(1)} custom-call(f32[616,128]{1,0:T(8,128)S(1)} %shard_map.77.message, f32[2,34,8,128]{3,2,1,0:T(8,128)S(1)} %get-tuple-element.23.col1, f32[2,34,8,128]{3,2,1,0:T(8,128)S(1)} %shard_map.73.before.col2, f32[4,3,34,8,128]{4,3,2,1,0:T(8,128)S(1)} %get-tuple-element.24.rates.far_rate, ...), custom_call_target="tpu_custom_call" | custom-call | flops 1000000 | bytes 1000000 | tf_op jit(solution)/shard_map/pallas_call | solution.py:50
  26.4 0.9 %shard_map.81 = (f32[2,3,34,8,128]{4,3,2,1,0:T(8,128)}, f32[2,34,8,128]{3,2,1,0:T(8,128)S(1)}, f32[2,34,8,128]{3,2,1,0:T(8,128)S(1)}) custom-call(f32[2,34,8,128]{3,2,1,0:T(8,128)S(1)} %shard_map.78.before.mid0, f32[2,34,8,128]{3,2,1,0:T(8,128)S(1)} %shard_map.79.mid1, f32[2,34,8,128]{3,2,1,0:T(8,128)S(1)} %get-tuple-element.26.mid2, ...), custom_call_target="tpu_custom_call" | custom-call | flops 1000000 | bytes 1000000 | tf_op jit(solution)/shard_map/pallas_call | solution.py:50
  27.3 1.0 %collective-permute-done.5.halo = f32[2,34,8,128]{3,2,1,0:T(8,128)S(1)} collective-permute-done((f32[2,34,8,128]{3,2,1,0:T(8,128)S(1)}, f32[2,34,8,128]{3,2,1,0:T(8,128)S(1)}, u32[]{:S(2)}, u32[]{:S(2)}) %collective-permute-start.5) | collective-permute-done | bytes 278560 | tf_op jit(solution)/shard_map/ppermute | solution.py:41
  28.4 0.8 %shard_map.82.begun = f32[2,3,34,8,128]{4,3,2,1,0:T(8,128)} custom-call(f32[2,3,34,8,128]{4,3,2,1,0:T(8,128)} %get-tuple-element.28.begun, f32[2,34,8,128]{3,2,1,0:T(8,128)S(1)} %get-tuple-element.29.local, f32[2,34,8,128]{3,2,1,0:T(8,128)S(1)} %collective-permute-done.5.halo, ...), custom_call_target="tpu_custom_call", output_to_operand_aliasing={{}: (0, {})} | custom-call | flops 1000000 | bytes 1000000 | tf_op jit(solution)/shard_map/pallas_call | solution.py:50
  29.2 5.1 %collective-permute-done.6.halo = f32[2,34,8,128]{3,2,1,0:T(8,128)S(1)} collective-permute-done((f32[2,34,8,128]{3,2,1,0:T(8,128)S(1)}, f32[2,34,8,128]{3,2,1,0:T(8,128)S(1)}, u32[]{:S(2)}, u32[]{:S(2)}) %collective-permute-start.6) | collective-permute-done | bytes 278560 | tf_op jit(solution)/shard_map/ppermute | solution.py:41
  34.3 0.8 %shard_map.83 = f32[2,3,34,8,128]{4,3,2,1,0:T(8,128)} custom-call(f32[2,3,34,8,128]{4,3,2,1,0:T(8,128)} %shard_map.82.begun, f32[2,34,8,128]{3,2,1,0:T(8,128)S(1)} %get-tuple-element.30.local, f32[2,34,8,128]{3,2,1,0:T(8,128)S(1)} %collective-permute-done.6.halo, ...), custom_call_target="tpu_custom_call", output_to_operand_aliasing={{}: (0, {})} | custom-call | flops 1000000 | bytes 1000000 | tf_op jit(solution)/shard_map/pallas_call | solution.py:50
  (1 shorter events, 0.0 us)
Async XLA Ops:
  0.0 9.9 %copy-start = (s32[2,2,3,34,256]{4,1,3,2,0:T(2,128)S(1)}, s32[2,2,3,34,256]{4,1,3,2,0:T(2,128)}, u32[]{:S(2)}) copy-start(s32[2,2,3,34,256]{4,1,3,2,0:T(2,128)} %param.8) | copy-start | bytes 1253380
  1.1 12.7 %collective-permute-start.3 = (f32[2,34,8,128]{3,2,1,0:T(8,128)S(1)}, f32[2,34,8,128]{3,2,1,0:T(8,128)S(1)}, u32[]{:S(2)}, u32[]{:S(2)}) collective-permute-start(f32[2,34,8,128]{3,2,1,0:T(8,128)S(1)} %shard_map.73.before.col2), channel_id=1, source_target_pairs={{0,4},{4,8},{8,12},{12,16},{16,20},{20,24},{24,28},{28,0},{1,5},{5... | collective-permute-start | bytes 835592 | tf_op jit(solution)/shard_map/ppermute | solution.py:41
  5.2 4.8 %collective-permute-start.1 = (f32[208,128]{1,0:T(8,128)S(1)}, f32[208,128]{1,0:T(8,128)S(1)}, u32[]{:S(2)}, u32[]{:S(2)}) collective-permute-start(f32[208,128]{1,0:T(8,128)S(1)} %get-tuple-element.18.own), channel_id=1, source_target_pairs={{0,2},{1,3},{2,0},{3,1},{4,6},{5,7},{6,4},{7,5},{8,10},{9,11},{10,... | collective-permute-start | bytes 319496 | tf_op jit(solution)/shard_map/ppermute | solution.py:46
  6.7 4.4 %collective-permute-start = (f32[208,128]{1,0:T(8,128)S(1)}, f32[208,128]{1,0:T(8,128)S(1)}, u32[]{:S(2)}, u32[]{:S(2)}) collective-permute-start(f32[208,128]{1,0:T(8,128)S(1)} %get-tuple-element.18.own), channel_id=1, source_target_pairs={{0,1},{1,0},{2,3},{3,2},{4,5},{5,4},{6,7},{7,6},{8,9},{9,8},{10,11... | collective-permute-start | bytes 319496 | tf_op jit(solution)/shard_map/ppermute | solution.py:46
  9.9 1.3 %collective-permute-start.2 = (f32[208,128]{1,0:T(8,128)S(1)}, f32[208,128]{1,0:T(8,128)S(1)}, u32[]{:S(2)}, u32[]{:S(2)}) collective-permute-start(f32[208,128]{1,0:T(8,128)S(1)} %collective-permute-done.1.second), channel_id=1, source_target_pairs={{0,1},{1,0},{2,3},{3,2},{4,5},{5,4},{6,7},{7,6},{8,9},{9,8},{10,11... | collective-permute-start | bytes 319496 | tf_op jit(solution)/shard_map/ppermute | solution.py:46
  13.8 10.4 %collective-permute-start.4 = (f32[616,128]{1,0:T(8,128)S(1)}, f32[616,128]{1,0:T(8,128)S(1)}, u32[]{:S(2)}, u32[]{:S(2)}) collective-permute-start(f32[616,128]{1,0:T(8,128)S(1)} %shard_map.77.message), channel_id=1, source_target_pairs={{0,28},{4,0},{8,4},{12,8},{16,12},{20,16},{24,20},{28,24},{1,29},{... | collective-permute-start | bytes 946184 | tf_op jit(solution)/shard_map/ppermute | solution.py:41
  16.3 12.1 %collective-permute-start.5 = (f32[2,34,8,128]{3,2,1,0:T(8,128)S(1)}, f32[2,34,8,128]{3,2,1,0:T(8,128)S(1)}, u32[]{:S(2)}, u32[]{:S(2)}) collective-permute-start(f32[2,34,8,128]{3,2,1,0:T(8,128)S(1)} %shard_map.78.before.mid0), channel_id=1, source_target_pairs={{0,28},{4,0},{8,4},{12,8},{16,12},{20,16},{24,20},{28,24},{1,29},{... | collective-permute-start | bytes 835592 | tf_op jit(solution)/shard_map/ppermute | solution.py:41
  25.0 9.4 %collective-permute-start.6 = (f32[2,34,8,128]{3,2,1,0:T(8,128)S(1)}, f32[2,34,8,128]{3,2,1,0:T(8,128)S(1)}, u32[]{:S(2)}, u32[]{:S(2)}) collective-permute-start(f32[2,34,8,128]{3,2,1,0:T(8,128)S(1)} %get-tuple-element.26.mid2), channel_id=1, source_target_pairs={{0,4},{4,8},{8,12},{12,16},{16,20},{20,24},{24,28},{28,0},{1,5},{5... | collective-permute-start | bytes 835592 | tf_op jit(solution)/shard_map/ppermute | solution.py:41

commit v11 on v10

--- a/solution.py
+++ b/solution.py
@@ -401,6 +401,7 @@
     message = call(gate_kernel, f32(length * 8, LANES), (VMEM,) * 2, (), 1, 1, message, west_halo, aliases={0: 0})
     east_message = shifted(message, "lon", -1)
     mid0 = call(west_kernel, column, (VMEM,) * 6, (), 10**6, 10**6, message, col1, west_halo, rates, factors, turn)
+    mid0 = call(gate_kernel, column, (VMEM,) * 2, (), 1, 1, mid0, east_message, aliases={0: 0})
     east_halo = shifted(mid0, "lon", -1)
     mid1 = call(inner_kernel, column, (VMEM,) * 6, (), 10**6, 10**6, message, col1, col2, rates, factors, turn)
     mid2, east = call(east_kernel, (column, f32(levels, 8, LANES)), (VMEM,) * 7, (), 10**6, 10**6,

time: 35.3 us -> 39.5 us (1.12)
  starting transfers between devices: 8.59 us -> 11.5 us
  waiting for transfers between devices: 17.5 us -> 18.7 us
    ppermute x4, starting transfers between devices: 7.03 us -> 9.93 us  [shifted(): lax.ppermute(value, axis, [(i, (i + by) % count) for i in range(count)])]
    ppermute x4, waiting for transfers between devices: 14.2 us -> 15.4 us  [shifted(): lax.ppermute(value, axis, [(i, (i + by) % count) for i in range(count)])]
    pallas_call x11 -> x12, Pallas kernels: 8.98 us -> 8.99 us  [call(): pl.pallas_call(kernel, out_shape=out, in_specs=in_specs, out_specs=jax.tr...]
  transfers between devices with their start and end apart: 7 -> 7, of which waited for: 6 -> 6; matrix products, arithmetic and copies ran while one was open for 0% -> 0% of each run, Pallas kernels for 20% -> 18%
where the time goes in v11:
time: 39.5 us; the launch traced here: 39.3 us
  waiting for transfers between devices  18.7 us (47%)
  starting transfers between devices  11.5 us (29%)
  Pallas kernels  8.99 us (23%)
    ppermute x4, waiting for transfers between devices, shifted(): lax.ppermute(value, axis, [(i, (i + by) % count) for i in range(count)])  15.4 us
    ppermute x4, starting transfers between devices, shifted(): lax.ppermute(value, axis, [(i, (i + by) % count) for i in range(count)])  9.93 us
    pallas_call x12, Pallas kernels, call(): pl.pallas_call(kernel, out_shape=out, in_specs=in_specs, out_specs=jax.tr...  8.99 us
    ppermute x3, waiting for transfers between devices, swapped(): return lax.ppermute(value, axis, [(i, i ^ mask) for i in range(count)])  3.36 us
    ppermute x3, starting transfers between devices, swapped(): return lax.ppermute(value, axis, [(i, i ^ mask) for i in range(count)])  1.56 us
  transfers between devices with their start and end apart: 7, of which 6 were waited for; matrix products, arithmetic and copies ran while one was open for 0% of the time, Pallas kernels for 18%

profile of v11, /device:TPU:0, one launch (start us, length us, event | category | flops | bytes accessed | tf_op | source)
XLA Modules:
  0.0 39.3 jit_solution(4595248167786867123)
XLA Ops:
  0.0 0.0 copy-start
  0.0 1.0 %shard_map.73.before.col2 = f32[2,34,8,128]{3,2,1,0:T(8,128)S(1)} custom-call(f32[2,3,34,8,128]{4,3,2,1,0:T(8,128)} %bitcast.24), custom_call_target="tpu_custom_call" | custom-call | flops 1 | bytes 1 | tf_op jit(solution)/shard_map/pallas_call | solution.py:50
  1.1 3.0 %collective-permute-start.3 = (f32[2,34,8,128]{3,2,1,0:T(8,128)S(1)}, f32[2,34,8,128]{3,2,1,0:T(8,128)S(1)}, u32[]{:S(2)}, u32[]{:S(2)}) collective-permute-start(f32[2,34,8,128]{3,2,1,0:T(8,128)S(1)} %shard_map.73.before.col2), channel_id=1, source_target_pairs={{0,4},{4,8},{8,12},{12,16},{16,20},{20,24},{24,28},{28,0},{1,5},{5... | collective-permute-start | bytes 835592 | tf_op jit(solution)/shard_map/ppermute | solution.py:41
  4.1 1.1 %shard_map.74 = (f32[208,128]{1,0:T(8,128)S(1)}, s32[3,136,128]{2,1,0:T(8,128)S(1)}) custom-call(s32[3,136,128]{2,1,0:T(8,128)} %bitcast.26, f32[3,34,64]{2,1,0:T(8,128)} %mass.1, f32[3,34,64]{2,1,0:T(8,128)} %xf.1, f32[3,34,64]{2,1,0:T(8,128)} %yf.1, f32[3,33,64]{2,1,0:T(8,128)} %km.1, f32[2,34,8,128]{3,2,1,0:T(8,128)S(1)} %shard_map.73.before.col2), custom_call_target="tpu_custom_call" | custom-call | flops 100000 | bytes 1000000 | tf_op jit(solution)/shard_map/pallas_call | solution.py:50
  5.2 1.6 %collective-permute-start.1 = (f32[208,128]{1,0:T(8,128)S(1)}, f32[208,128]{1,0:T(8,128)S(1)}, u32[]{:S(2)}, u32[]{:S(2)}) collective-permute-start(f32[208,128]{1,0:T(8,128)S(1)} %get-tuple-element.18.own), channel_id=1, source_target_pairs={{0,2},{1,3},{2,0},{3,1},{4,6},{5,7},{6,4},{7,5},{8,10},{9,11},{10,... | collective-permute-start | bytes 319496 | tf_op jit(solution)/shard_map/ppermute | solution.py:46
  6.7 0.0 collective-permute-start
  6.7 3.2 %collective-permute-done.1.second = f32[208,128]{1,0:T(8,128)S(1)} collective-permute-done((f32[208,128]{1,0:T(8,128)S(1)}, f32[208,128]{1,0:T(8,128)S(1)}, u32[]{:S(2)}, u32[]{:S(2)}) %collective-permute-start.1) | collective-permute-done | bytes 106528 | tf_op jit(solution)/shard_map/ppermute | solution.py:46
  9.9 0.0 collective-permute-start.2
  9.9 0.0 copy-done
  9.9 1.1 %shard_map.75 = (f32[77,8,128]{2,1,0:T(8,128)S(1)}, f32[2,34,8,128]{3,2,1,0:T(8,128)S(1)}, f32[2,2,3,34,8,128]{5,4,3,2,1,0:T(8,128)S(1)}) custom-call(f32[2,3,34,8,128]{4,3,2,1,0:T(8,128)} %bitcast.25, s32[2,3,136,128]{3,2,1,0:T(8,128)S(1)} %bitcast.23), custom_call_target="tpu_custom_call" | custom-call | flops 1000000 | bytes 1000000 | tf_op jit(solution)/shard_map/pallas_call | solution.py:50
  11.1 0.0 collective-permute-done.first
  11.1 0.1 collective-permute-done.2.third
  11.3 0.7 %shard_map.76 = (f32[4,3,34,8,128]{4,3,2,1,0:T(8,128)S(1)}, f32[3,3,34,8,128]{4,3,2,1,0:T(8,128)S(1)}, f32[616,128]{1,0:T(8,128)S(1)}) custom-call(f32[208,128]{1,0:T(8,128)S(1)} %get-tuple-element.18.own, f32[208,128]{1,0:T(8,128)S(1)} %collective-permute-done.first, f32[208,128]{1,0:T(8,128)S(1)} %collective-permute-done.1.second, ...), custom_call_target="tpu_custom_call", output_to_operand_aliasing={{2}: (6, {})} | custom-call | flops 1 | bytes 1 | tf_op jit(solution)/shard_map/pallas_call | solution.py:50
  12.0 1.8 %collective-permute-done.3.before.west_halo = f32[2,34,8,128]{3,2,1,0:T(8,128)S(1)} collective-permute-done((f32[2,34,8,128]{3,2,1,0:T(8,128)S(1)}, f32[2,34,8,128]{3,2,1,0:T(8,128)S(1)}, u32[]{:S(2)}, u32[]{:S(2)}) %collective-permute-start.3) | collective-permute-done | bytes 278560 | tf_op jit(solution)/shard_map/ppermute | solution.py:41
  13.8 1.7 %collective-permute-start.4 = (f32[616,128]{1,0:T(8,128)S(1)}, f32[616,128]{1,0:T(8,128)S(1)}, u32[]{:S(2)}, u32[]{:S(2)}) collective-permute-start(f32[616,128]{1,0:T(8,128)S(1)} %shard_map.77.message), channel_id=1, source_target_pairs={{0,28},{4,0},{8,4},{12,8},{16,12},{20,16},{24,20},{28,24},{1,29},{... | collective-permute-start | bytes 946184 | tf_op jit(solution)/shard_map/ppermute | solution.py:41
  15.5 0.8 %shard_map.78.message = f32[2,34,8,128]{3,2,1,0:T(8,128)S(1)} custom-call(f32[616,128]{1,0:T(8,128)S(1)} %shard_map.77.message, f32[2,34,8,128]{3,2,1,0:T(8,128)S(1)} %get-tuple-element.23.col1, f32[2,34,8,128]{3,2,1,0:T(8,128)S(1)} %collective-permute-done.3.before.west_halo, f32[4,3,34,8,128]{4,3,2,1,0:T(8,128)S(1)} %get-tuple-element.24.rates.far_rate, ...), custom_call_target="tpu_custom_call" | custom-call | flops 1000000 | bytes 1000000 | tf_op jit(solution)/shard_map/pallas_call | solution.py:50
  16.3 6.1 %collective-permute-done.4.before.halo = f32[616,128]{1,0:T(8,128)S(1)} collective-permute-done((f32[616,128]{1,0:T(8,128)S(1)}, f32[616,128]{1,0:T(8,128)S(1)}, u32[]{:S(2)}, u32[]{:S(2)}) %collective-permute-start.4) | collective-permute-done | bytes 315424 | tf_op jit(solution)/shard_map/ppermute | solution.py:41
  22.4 5.1 %collective-permute-start.5 = (f32[2,34,8,128]{3,2,1,0:T(8,128)S(1)}, f32[2,34,8,128]{3,2,1,0:T(8,128)S(1)}, u32[]{:S(2)}, u32[]{:S(2)}) collective-permute-start(f32[2,34,8,128]{3,2,1,0:T(8,128)S(1)} %shard_map.79.before.mid0), channel_id=1, source_target_pairs={{0,28},{4,0},{8,4},{12,8},{16,12},{20,16},{24,20},{28,24},{1,29},{... | collective-permute-start | bytes 835592 | tf_op jit(solution)/shard_map/ppermute | solution.py:41
  27.5 0.8 %shard_map.81 = (f32[2,34,8,128]{3,2,1,0:T(8,128)S(1)}, f32[34,8,128]{2,1,0:T(8,128)S(1)}) custom-call(f32[2,34,8,128]{3,2,1,0:T(8,128)S(1)} %get-tuple-element.23.col1, f32[2,34,8,128]{3,2,1,0:T(8,128)S(1)} %shard_map.73.before.col2, f32[616,128]{1,0:T(8,128)S(1)} %collective-permute-done.4.before.halo, ...), custom_call_target="tpu_custom_call" | custom-call | flops 1000000 | bytes 1000000 | tf_op jit(solution)/shard_map/pallas_call | solution.py:50
  28.3 0.1 collective-permute-start.6
  28.4 0.8 %shard_map.80.mid1 = f32[2,34,8,128]{3,2,1,0:T(8,128)S(1)} custom-call(f32[616,128]{1,0:T(8,128)S(1)} %shard_map.77.message, f32[2,34,8,128]{3,2,1,0:T(8,128)S(1)} %get-tuple-element.23.col1, f32[2,34,8,128]{3,2,1,0:T(8,128)S(1)} %shard_map.73.before.col2, f32[4,3,34,8,128]{4,3,2,1,0:T(8,128)S(1)} %get-tuple-element.24.rates.far_rate, ...), custom_call_target="tpu_custom_call" | custom-call | flops 1000000 | bytes 1000000 | tf_op jit(solution)/shard_map/pallas_call | solution.py:50
  29.2 0.9 %shard_map.82 = (f32[2,3,34,8,128]{4,3,2,1,0:T(8,128)}, f32[2,34,8,128]{3,2,1,0:T(8,128)S(1)}, f32[2,34,8,128]{3,2,1,0:T(8,128)S(1)}) custom-call(f32[2,34,8,128]{3,2,1,0:T(8,128)S(1)} %shard_map.79.before.mid0, f32[2,34,8,128]{3,2,1,0:T(8,128)S(1)} %shard_map.80.mid1, f32[2,34,8,128]{3,2,1,0:T(8,128)S(1)} %get-tuple-element.26.mid2, ...), custom_call_target="tpu_custom_call" | custom-call | flops 1000000 | bytes 1000000 | tf_op jit(solution)/shard_map/pallas_call | solution.py:50
  30.2 2.5 %collective-permute-done.5.halo = f32[2,34,8,128]{3,2,1,0:T(8,128)S(1)} collective-permute-done((f32[2,34,8,128]{3,2,1,0:T(8,128)S(1)}, f32[2,34,8,128]{3,2,1,0:T(8,128)S(1)}, u32[]{:S(2)}, u32[]{:S(2)}) %collective-permute-start.5) | collective-permute-done | bytes 278560 | tf_op jit(solution)/shard_map/ppermute | solution.py:41
  32.7 0.8 %shard_map.83.begun = f32[2,3,34,8,128]{4,3,2,1,0:T(8,128)} custom-call(f32[2,3,34,8,128]{4,3,2,1,0:T(8,128)} %get-tuple-element.28.begun, f32[2,34,8,128]{3,2,1,0:T(8,128)S(1)} %get-tuple-element.29.local, f32[2,34,8,128]{3,2,1,0:T(8,128)S(1)} %collective-permute-done.5.halo, ...), custom_call_target="tpu_custom_call", output_to_operand_aliasing={{}: (0, {})} | custom-call | flops 1000000 | bytes 1000000 | tf_op jit(solution)/shard_map/pallas_call | solution.py:50
  33.5 4.9 %collective-permute-done.6.halo = f32[2,34,8,128]{3,2,1,0:T(8,128)S(1)} collective-permute-done((f32[2,34,8,128]{3,2,1,0:T(8,128)S(1)}, f32[2,34,8,128]{3,2,1,0:T(8,128)S(1)}, u32[]{:S(2)}, u32[]{:S(2)}) %collective-permute-start.6) | collective-permute-done | bytes 278560 | tf_op jit(solution)/shard_map/ppermute | solution.py:41
  38.5 0.8 %shard_map.84 = f32[2,3,34,8,128]{4,3,2,1,0:T(8,128)} custom-call(f32[2,3,34,8,128]{4,3,2,1,0:T(8,128)} %shard_map.83.begun, f32[2,34,8,128]{3,2,1,0:T(8,128)S(1)} %get-tuple-element.30.local, f32[2,34,8,128]{3,2,1,0:T(8,128)S(1)} %collective-permute-done.6.halo, ...), custom_call_target="tpu_custom_call", output_to_operand_aliasing={{}: (0, {})} | custom-call | flops 1000000 | bytes 1000000 | tf_op jit(solution)/shard_map/pallas_call | solution.py:50
  (2 shorter events, 0.0 us)
Async XLA Ops:
  0.0 9.9 %copy-start = (s32[2,2,3,34,256]{4,1,3,2,0:T(2,128)S(1)}, s32[2,2,3,34,256]{4,1,3,2,0:T(2,128)}, u32[]{:S(2)}) copy-start(s32[2,2,3,34,256]{4,1,3,2,0:T(2,128)} %param.8) | copy-start | bytes 1253380
  1.1 12.7 %collective-permute-start.3 = (f32[2,34,8,128]{3,2,1,0:T(8,128)S(1)}, f32[2,34,8,128]{3,2,1,0:T(8,128)S(1)}, u32[]{:S(2)}, u32[]{:S(2)}) collective-permute-start(f32[2,34,8,128]{3,2,1,0:T(8,128)S(1)} %shard_map.73.before.col2), channel_id=1, source_target_pairs={{0,4},{4,8},{8,12},{12,16},{16,20},{20,24},{24,28},{28,0},{1,5},{5... | collective-permute-start | bytes 835592 | tf_op jit(solution)/shard_map/ppermute | solution.py:41
  5.2 4.8 %collective-permute-start.1 = (f32[208,128]{1,0:T(8,128)S(1)}, f32[208,128]{1,0:T(8,128)S(1)}, u32[]{:S(2)}, u32[]{:S(2)}) collective-permute-start(f32[208,128]{1,0:T(8,128)S(1)} %get-tuple-element.18.own), channel_id=1, source_target_pairs={{0,2},{1,3},{2,0},{3,1},{4,6},{5,7},{6,4},{7,5},{8,10},{9,11},{10,... | collective-permute-start | bytes 319496 | tf_op jit(solution)/shard_map/ppermute | solution.py:46
  6.7 4.4 %collective-permute-start = (f32[208,128]{1,0:T(8,128)S(1)}, f32[208,128]{1,0:T(8,128)S(1)}, u32[]{:S(2)}, u32[]{:S(2)}) collective-permute-start(f32[208,128]{1,0:T(8,128)S(1)} %get-tuple-element.18.own), channel_id=1, source_target_pairs={{0,1},{1,0},{2,3},{3,2},{4,5},{5,4},{6,7},{7,6},{8,9},{9,8},{10,11... | collective-permute-start | bytes 319496 | tf_op jit(solution)/shard_map/ppermute | solution.py:46
  9.9 1.3 %collective-permute-start.2 = (f32[208,128]{1,0:T(8,128)S(1)}, f32[208,128]{1,0:T(8,128)S(1)}, u32[]{:S(2)}, u32[]{:S(2)}) collective-permute-start(f32[208,128]{1,0:T(8,128)S(1)} %collective-permute-done.1.second), channel_id=1, source_target_pairs={{0,1},{1,0},{2,3},{3,2},{4,5},{5,4},{6,7},{7,6},{8,9},{9,8},{10,11... | collective-permute-start | bytes 319496 | tf_op jit(solution)/shard_map/ppermute | solution.py:46
  13.8 8.6 %collective-permute-start.4 = (f32[616,128]{1,0:T(8,128)S(1)}, f32[616,128]{1,0:T(8,128)S(1)}, u32[]{:S(2)}, u32[]{:S(2)}) collective-permute-start(f32[616,128]{1,0:T(8,128)S(1)} %shard_map.77.message), channel_id=1, source_target_pairs={{0,28},{4,0},{8,4},{12,8},{16,12},{20,16},{24,20},{28,24},{1,29},{... | collective-permute-start | bytes 946184 | tf_op jit(solution)/shard_map/ppermute | solution.py:41
  22.4 10.3 %collective-permute-start.5 = (f32[2,34,8,128]{3,2,1,0:T(8,128)S(1)}, f32[2,34,8,128]{3,2,1,0:T(8,128)S(1)}, u32[]{:S(2)}, u32[]{:S(2)}) collective-permute-start(f32[2,34,8,128]{3,2,1,0:T(8,128)S(1)} %shard_map.79.before.mid0), channel_id=1, source_target_pairs={{0,28},{4,0},{8,4},{12,8},{16,12},{20,16},{24,20},{28,24},{1,29},{... | collective-permute-start | bytes 835592 | tf_op jit(solution)/shard_map/ppermute | solution.py:41
  28.3 10.1 %collective-permute-start.6 = (f32[2,34,8,128]{3,2,1,0:T(8,128)S(1)}, f32[2,34,8,128]{3,2,1,0:T(8,128)S(1)}, u32[]{:S(2)}, u32[]{:S(2)}) collective-permute-start(f32[2,34,8,128]{3,2,1,0:T(8,128)S(1)} %get-tuple-element.26.mid2), channel_id=1, source_target_pairs={{0,4},{4,8},{8,12},{12,16},{16,20},{20,24},{24,28},{28,0},{1,5},{5... | collective-permute-start | bytes 835592 | tf_op jit(solution)/shard_map/ppermute | solution.py:41

commit v12 on v9

--- a/solution.py
+++ b/solution.py
@@ -70,18 +70,11 @@
     return row == 0, row == slope
 
 
-def first_kernel(state, col2, sems):
-    copies = [pltpu.make_async_copy(state.at[t, 2], col2.at[t], sems.at[t]) for t in range(state.shape[0])]
-    for copy in copies:
-        copy.start()
-    for copy in copies:
-        copy.wait()
-
-
-def head_kernel(flags, mass, xf, yf, km, before, packed, flags_v, mass_v, xf_v, yf_v, km_v, sems):
+def head_kernel(state, mass, xf, yf, km, col2, packed, mass_v, xf_v, yf_v, km_v, sems):
     columns, levels = mass.shape[0], mass.shape[1]
     half = LANES // 2
-    pairs = ((mass, mass_v), (xf, xf_v), (yf, yf_v), (km, km_v), (flags, flags_v))
+    pairs = [(state.at[t, 2], col2.at[t]) for t in range(state.shape[0])]
+    pairs = [(mass, mass_v), (xf, xf_v), (yf, yf_v), (km, km_v)] + pairs
     copies = [pltpu.make_async_copy(src, dst, sems.at[i]) for i, (src, dst) in enumerate(pairs)]
     for copy in copies:
         copy.start()
@@ -94,7 +87,8 @@
         packed[top : top + levels, :half] = yf_v[c]
         packed[top : top + levels - 1, half:] = km_v[c]
         packed[top + levels - 1 : top + levels, half:] = jnp.zeros((1, half), jnp.float32)
-    copies[4].wait()
+    for copy in copies[4:]:
+        copy.wait()
 
 
 def spread(upper_block, ref, *where):
@@ -106,14 +100,18 @@
     return rows - -(-2 * levels // 8) * 8 + b * levels
 
 
-def turn_kernel(state, switches, message, col1, turn, sems):
+def turn_kernel(state, flags, switches_hbm, message, col1, flags_v, turn, switches, sems, flag_sem, switch_sem):
     tracers, columns = switches.shape[:2]
     levels = switches.shape[2] // 4
-    copies = []
+    fetch = pltpu.make_async_copy(switches_hbm, switches, switch_sem)
+    fetch.start()
+    copies = [pltpu.make_async_copy(flags, flags_v, flag_sem)]
+    copies[0].start()
     for t in range(tracers):
         for c, place in ((0, message.at[pl.ds(t * levels, levels)]), (1, col1.at[t])):
             copies.append(pltpu.make_async_copy(state.at[t, c], place, sems.at[c, t]))
             copies[-1].start()
+    fetch.wait()
     row = lax.broadcasted_iota(jnp.int32, (8, LANES), 0)
     moment = row % MOMENTS
     for t in range(tracers):
@@ -342,16 +340,18 @@
     dma = pltpu.SemaphoreType.DMA
     fields = tuple(stay(x) for x in (air_mass, x_flux, y_flux, vertical_mixing))
 
-    col2 = call(first_kernel, column, (HBM,), [dma((tracers,))], 1, 1, stay(state))
+    col2, packed = call(
+        head_kernel, (column, f32(rows, LANES)), (HBM,) * 5,
+        [pltpu.VMEM(x.shape, x.dtype) for x in fields] + [dma((4 + tracers,))], 10**5, 10**6, stay(state), *fields)
     west_halo = shifted(col2, "lon", 1)
-    packed, flag = call(
-        head_kernel, (f32(rows, LANES), jax.ShapeDtypeStruct(flag.shape, flag.dtype)), (HBM,) * 5 + (VMEM,),
-        [pltpu.VMEM(x.shape, x.dtype) for x in fields] + [dma((5,))], 10**5, 10**6, stay(flag), *fields, col2)
     across = swapped(packed, "trc", 2)
     others = [swapped(packed, "trc", 1), across, swapped(across, "trc", 1)]
-    message, col1, turn = call(
-        turn_kernel, (f32(length, 8, LANES), column, f32(2, tracers, columns, levels, 8, LANES)), (HBM, VMEM),
-        [dma((2, tracers))], 10**6, 10**6, stay(state), switch)
+    message, col1, flag, turn = call(
+        turn_kernel,
+        (f32(length, 8, LANES), column, jax.ShapeDtypeStruct(flag.shape, flag.dtype),
+         f32(2, tracers, columns, levels, 8, LANES)),
+        (HBM,) * 3, [pltpu.VMEM(switch.shape, switch.dtype), dma((2, tracers)), dma, dma],
+        10**6, 10**6, stay(state), stay(flag), stay(switch))
     rates, factors, message = call(
         pre_kernel,
         (f32(4, columns, levels, 8, LANES), f32(3, columns, levels, 8, LANES), f32(length * 8, LANES)),

time: 35.4 us -> 35.5 us (level)
  waiting for transfers between devices: 17.4 us -> 18.7 us
  starting transfers between devices: 8.59 us -> 7.77 us
  Pallas kernels: 9.16 us -> 8.79 us
    ppermute x4, waiting for transfers between devices: 14.1 us -> 15.5 us  [shifted(): lax.ppermute(value, axis, [(i, (i + by) % count) for i in range(count)])]
    ppermute x4, starting transfers between devices: 7.03 us -> 6.28 us  [shifted(): lax.ppermute(value, axis, [(i, (i + by) % count) for i in range(count)])]
    pallas_call x11 -> x10, Pallas kernels: 9.16 us -> 8.79 us  [call(): pl.pallas_call(kernel, out_shape=out, in_specs=in_specs, out_specs=jax.tr...]
  transfers between devices with their start and end apart: 7 -> 7, of which waited for: 6 -> 5; matrix products, arithmetic and copies ran while one was open for 0% -> 0% of each run, Pallas kernels for 20% -> 19%
where the time goes in v12:
time: 35.5 us; the launch traced here: 35.4 us
  waiting for transfers between devices  18.7 us (53%)
  Pallas kernels  8.79 us (25%)
  starting transfers between devices  7.77 us (22%)
    ppermute x4, waiting for transfers between devices, shifted(): lax.ppermute(value, axis, [(i, (i + by) % count) for i in range(count)])  15.5 us
    pallas_call x10, Pallas kernels, call(): pl.pallas_call(kernel, out_shape=out, in_specs=in_specs, out_specs=jax.tr...  8.79 us
    ppermute x4, starting transfers between devices, shifted(): lax.ppermute(value, axis, [(i, (i + by) % count) for i in range(count)])  6.28 us
    ppermute x3, waiting for transfers between devices, swapped(): return lax.ppermute(value, axis, [(i, i ^ mask) for i in range(count)])  3.22 us
    ppermute x3, starting transfers between devices, swapped(): return lax.ppermute(value, axis, [(i, i ^ mask) for i in range(count)])  1.5 us
  transfers between devices with their start and end apart: 7, of which 5 were waited for; matrix products, arithmetic and copies ran while one was open for 0% of the time, Pallas kernels for 19%

profile of v12, /device:TPU:0, one launch (start us, length us, event | category | flops | bytes accessed | tf_op | source)
XLA Modules:
  0.0 35.4 jit_solution(14261546300165482649)
XLA Ops:
  0.0 1.1 %shard_map.73 = (f32[2,34,8,128]{3,2,1,0:T(8,128)S(1)}, f32[208,128]{1,0:T(8,128)S(1)}) custom-call(f32[2,3,34,8,128]{4,3,2,1,0:T(8,128)} %bitcast.23, f32[3,34,64]{2,1,0:T(8,128)} %mass.1, f32[3,34,64]{2,1,0:T(8,128)} %xf.1, f32[3,34,64]{2,1,0:T(8,128)} %yf.1, f32[3,33,64]{2,1,0:T(8,128)} %km.1), custom_call_target="tpu_custom_call" | custom-call | flops 100000 | bytes 1000000 | tf_op jit(solution)/shard_map/pallas_call | solution.py:48
  1.1 3.0 %collective-permute-start.3 = (f32[2,34,8,128]{3,2,1,0:T(8,128)S(1)}, f32[2,34,8,128]{3,2,1,0:T(8,128)S(1)}, u32[]{:S(2)}, u32[]{:S(2)}) collective-permute-start(f32[2,34,8,128]{3,2,1,0:T(8,128)S(1)} %get-tuple-element.21.col2), channel_id=1, source_target_pairs={{0,4},{4,8},{8,12},{12,16},{16,20},{20,24},{24,28},{28,0},{1,5},{5... | collective-permute-start | bytes 835592 | tf_op jit(solution)/shard_map/ppermute | solution.py:39
  4.2 1.5 %collective-permute-start.1 = (f32[208,128]{1,0:T(8,128)S(1)}, f32[208,128]{1,0:T(8,128)S(1)}, u32[]{:S(2)}, u32[]{:S(2)}) collective-permute-start(f32[208,128]{1,0:T(8,128)S(1)} %get-tuple-element.16.own), channel_id=1, source_target_pairs={{0,2},{1,3},{2,0},{3,1},{4,6},{5,7},{6,4},{7,5},{8,10},{9,11},{10,... | collective-permute-start | bytes 319496 | tf_op jit(solution)/shard_map/ppermute | solution.py:44
  5.7 0.0 collective-permute-start
  5.7 3.2 %collective-permute-done.1.second = f32[208,128]{1,0:T(8,128)S(1)} collective-permute-done((f32[208,128]{1,0:T(8,128)S(1)}, f32[208,128]{1,0:T(8,128)S(1)}, u32[]{:S(2)}, u32[]{:S(2)}) %collective-permute-start.1) | collective-permute-done | bytes 106528 | tf_op jit(solution)/shard_map/ppermute | solution.py:44
  8.9 0.0 collective-permute-start.2
  8.9 1.8 %shard_map.74 = (f32[77,8,128]{2,1,0:T(8,128)S(1)}, f32[2,34,8,128]{3,2,1,0:T(8,128)S(1)}, s32[3,136,128]{2,1,0:T(8,128)S(1)}, f32[2,2,3,34,8,128]{5,4,3,2,1,0:T(8,128)S(1)}) custom-call(f32[2,3,34,8,128]{4,3,2,1,0:T(8,128)} %bitcast.24, s32[3,136,128]{2,1,0:T(8,128)} %bitcast.26, s32[2,3,136,128]{3,2,1,0:T(8,128)} %bitcast.25), custom_call_target="tpu_custom_call" | custom-call | flops 1000000 | bytes 1000000 | tf_op jit(solution)/shard_map/pallas_call | solution.py:48
  10.6 0.0 collective-permute-done.first
  10.7 0.0 collective-permute-done.2.third
  10.7 0.7 %shard_map.75 = (f32[4,3,34,8,128]{4,3,2,1,0:T(8,128)S(1)}, f32[3,3,34,8,128]{4,3,2,1,0:T(8,128)S(1)}, f32[616,128]{1,0:T(8,128)S(1)}) custom-call(f32[208,128]{1,0:T(8,128)S(1)} %get-tuple-element.16.own, f32[208,128]{1,0:T(8,128)S(1)} %collective-permute-done.first, f32[208,128]{1,0:T(8,128)S(1)} %collective-permute-done.1.second, ...), custom_call_target="tpu_custom_call", output_to_operand_aliasing={{2}: (6, {})} | custom-call | flops 1 | bytes 1 | tf_op jit(solution)/shard_map/pallas_call | solution.py:48
  11.4 2.5 %collective-permute-done.3.before.west_halo = f32[2,34,8,128]{3,2,1,0:T(8,128)S(1)} collective-permute-done((f32[2,34,8,128]{3,2,1,0:T(8,128)S(1)}, f32[2,34,8,128]{3,2,1,0:T(8,128)S(1)}, u32[]{:S(2)}, u32[]{:S(2)}) %collective-permute-start.3) | collective-permute-done | bytes 278560 | tf_op jit(solution)/shard_map/ppermute | solution.py:39
  13.9 1.7 %collective-permute-start.4 = (f32[616,128]{1,0:T(8,128)S(1)}, f32[616,128]{1,0:T(8,128)S(1)}, u32[]{:S(2)}, u32[]{:S(2)}) collective-permute-start(f32[616,128]{1,0:T(8,128)S(1)} %shard_map.76.message), channel_id=1, source_target_pairs={{0,28},{4,0},{8,4},{12,8},{16,12},{20,16},{24,20},{28,24},{1,29},{... | collective-permute-start | bytes 946184 | tf_op jit(solution)/shard_map/ppermute | solution.py:39
  15.6 0.8 %shard_map.77.before.mid0 = f32[2,34,8,128]{3,2,1,0:T(8,128)S(1)} custom-call(f32[616,128]{1,0:T(8,128)S(1)} %shard_map.76.message, f32[2,34,8,128]{3,2,1,0:T(8,128)S(1)} %get-tuple-element.22.col1, f32[2,34,8,128]{3,2,1,0:T(8,128)S(1)} %collective-permute-done.3.before.west_halo, f32[4,3,34,8,128]{4,3,2,1,0:T(8,128)S(1)} %get-tuple-element.23.rates, ...), custom_call_target="tpu_custom_call" | custom-call | flops 1000000 | bytes 1000000 | tf_op jit(solution)/shard_map/pallas_call | solution.py:48
  16.4 1.5 %collective-permute-start.5 = (f32[2,34,8,128]{3,2,1,0:T(8,128)S(1)}, f32[2,34,8,128]{3,2,1,0:T(8,128)S(1)}, u32[]{:S(2)}, u32[]{:S(2)}) collective-permute-start(f32[2,34,8,128]{3,2,1,0:T(8,128)S(1)} %shard_map.77.before.mid0), channel_id=1, source_target_pairs={{0,28},{4,0},{8,4},{12,8},{16,12},{20,16},{24,20},{28,24},{1,29},{... | collective-permute-start | bytes 835592 | tf_op jit(solution)/shard_map/ppermute | solution.py:39
  17.9 6.4 %collective-permute-done.4.halo = f32[616,128]{1,0:T(8,128)S(1)} collective-permute-done((f32[616,128]{1,0:T(8,128)S(1)}, f32[616,128]{1,0:T(8,128)S(1)}, u32[]{:S(2)}, u32[]{:S(2)}) %collective-permute-start.4) | collective-permute-done | bytes 315424 | tf_op jit(solution)/shard_map/ppermute | solution.py:39
  24.2 0.8 %shard_map.79 = (f32[2,34,8,128]{3,2,1,0:T(8,128)S(1)}, f32[34,8,128]{2,1,0:T(8,128)S(1)}) custom-call(f32[2,34,8,128]{3,2,1,0:T(8,128)S(1)} %get-tuple-element.22.col1, f32[2,34,8,128]{3,2,1,0:T(8,128)S(1)} %get-tuple-element.21.col2, f32[616,128]{1,0:T(8,128)S(1)} %collective-permute-done.4.halo, f32[4,3,34,8,128]{4,3,2,1,0:T(8,128)S(1)} %get-tuple-element.23.rates, ...), custom_call_target="tpu_custom_call" | custom-call | flops 1000000 | bytes 1000000 | tf_op jit(solution)/shard_map/pallas_call | solution.py:48
  25.1 0.1 collective-permute-start.6
  25.1 0.8 %shard_map.78.mid1 = f32[2,34,8,128]{3,2,1,0:T(8,128)S(1)} custom-call(f32[616,128]{1,0:T(8,128)S(1)} %shard_map.76.message, f32[2,34,8,128]{3,2,1,0:T(8,128)S(1)} %get-tuple-element.22.col1, f32[2,34,8,128]{3,2,1,0:T(8,128)S(1)} %get-tuple-element.21.col2, f32[4,3,34,8,128]{4,3,2,1,0:T(8,128)S(1)} %get-tuple-element.23.rates, ...), custom_call_target="tpu_custom_call" | custom-call | flops 1000000 | bytes 1000000 | tf_op jit(solution)/shard_map/pallas_call | solution.py:48
  25.9 0.9 %shard_map.80.begun = f32[2,3,34,8,128]{4,3,2,1,0:T(8,128)} custom-call(f32[2,34,8,128]{3,2,1,0:T(8,128)S(1)} %shard_map.77.before.mid0, f32[2,34,8,128]{3,2,1,0:T(8,128)S(1)} %shard_map.78.mid1, f32[2,34,8,128]{3,2,1,0:T(8,128)S(1)} %get-tuple-element.25.mid2, f32[4,3,34,8,128]{4,3,2,1,0:T(8,128)S(1)} %get-tuple-element.23.rates, ...), custom_call_target="tpu_custom_call" | custom-call | flops 1000000 | bytes 1000000 | tf_op jit(solution)/shard_map/pallas_call | solution.py:48
  26.9 4.6 %collective-permute-done.5.halo = f32[2,34,8,128]{3,2,1,0:T(8,128)S(1)} collective-permute-done((f32[2,34,8,128]{3,2,1,0:T(8,128)S(1)}, f32[2,34,8,128]{3,2,1,0:T(8,128)S(1)}, u32[]{:S(2)}, u32[]{:S(2)}) %collective-permute-start.5) | collective-permute-done | bytes 278560 | tf_op jit(solution)/shard_map/ppermute | solution.py:39
  31.5 0.9 %shard_map.81.begun = f32[2,3,34,8,128]{4,3,2,1,0:T(8,128)} custom-call(f32[2,3,34,8,128]{4,3,2,1,0:T(8,128)} %shard_map.80.begun, f32[2,34,8,128]{3,2,1,0:T(8,128)S(1)} %shard_map.78.mid1, f32[2,34,8,128]{3,2,1,0:T(8,128)S(1)} %get-tuple-element.25.mid2, f32[2,34,8,128]{3,2,1,0:T(8,128)S(1)} %collective-permute-done.5.halo, ...), custom_call_target="tpu_custom_call", output_to_operand_aliasing={{}: (0, {})} | custom-call | flops 1000000 | bytes 1000000 | tf_op jit(solution)/shard_map/pallas_call | solution.py:48
  32.4 2.0 %collective-permute-done.6.halo = f32[2,34,8,128]{3,2,1,0:T(8,128)S(1)} collective-permute-done((f32[2,34,8,128]{3,2,1,0:T(8,128)S(1)}, f32[2,34,8,128]{3,2,1,0:T(8,128)S(1)}, u32[]{:S(2)}, u32[]{:S(2)}) %collective-permute-start.6) | collective-permute-done | bytes 278560 | tf_op jit(solution)/shard_map/ppermute | solution.py:39
  34.4 0.9 %shard_map.82 = f32[2,3,34,8,128]{4,3,2,1,0:T(8,128)} custom-call(f32[2,3,34,8,128]{4,3,2,1,0:T(8,128)} %shard_map.81.begun, f32[2,34,8,128]{3,2,1,0:T(8,128)S(1)} %shard_map.77.before.mid0, f32[2,34,8,128]{3,2,1,0:T(8,128)S(1)} %shard_map.78.mid1, f32[2,34,8,128]{3,2,1,0:T(8,128)S(1)} %collective-permute-done.6.halo, ...), custom_call_target="tpu_custom_call", output_to_operand_aliasing={{}: (0, {})} | custom-call | flops 1000000 | bytes 1000000 | tf_op jit(solution)/shard_map/pallas_call | solution.py:48
  (1 shorter events, 0.0 us)
Async XLA Ops:
  1.1 12.7 %collective-permute-start.3 = (f32[2,34,8,128]{3,2,1,0:T(8,128)S(1)}, f32[2,34,8,128]{3,2,1,0:T(8,128)S(1)}, u32[]{:S(2)}, u32[]{:S(2)}) collective-permute-start(f32[2,34,8,128]{3,2,1,0:T(8,128)S(1)} %get-tuple-element.21.col2), channel_id=1, source_target_pairs={{0,4},{4,8},{8,12},{12,16},{16,20},{20,24},{24,28},{28,0},{1,5},{5... | collective-permute-start | bytes 835592 | tf_op jit(solution)/shard_map/ppermute | solution.py:39
  4.2 4.7 %collective-permute-start.1 = (f32[208,128]{1,0:T(8,128)S(1)}, f32[208,128]{1,0:T(8,128)S(1)}, u32[]{:S(2)}, u32[]{:S(2)}) collective-permute-start(f32[208,128]{1,0:T(8,128)S(1)} %get-tuple-element.16.own), channel_id=1, source_target_pairs={{0,2},{1,3},{2,0},{3,1},{4,6},{5,7},{6,4},{7,5},{8,10},{9,11},{10,... | collective-permute-start | bytes 319496 | tf_op jit(solution)/shard_map/ppermute | solution.py:44
  5.7 5.0 %collective-permute-start = (f32[208,128]{1,0:T(8,128)S(1)}, f32[208,128]{1,0:T(8,128)S(1)}, u32[]{:S(2)}, u32[]{:S(2)}) collective-permute-start(f32[208,128]{1,0:T(8,128)S(1)} %get-tuple-element.16.own), channel_id=1, source_target_pairs={{0,1},{1,0},{2,3},{3,2},{4,5},{5,4},{6,7},{7,6},{8,9},{9,8},{10,11... | collective-permute-start | bytes 319496 | tf_op jit(solution)/shard_map/ppermute | solution.py:44
  8.9 1.8 %collective-permute-start.2 = (f32[208,128]{1,0:T(8,128)S(1)}, f32[208,128]{1,0:T(8,128)S(1)}, u32[]{:S(2)}, u32[]{:S(2)}) collective-permute-start(f32[208,128]{1,0:T(8,128)S(1)} %collective-permute-done.1.second), channel_id=1, source_target_pairs={{0,1},{1,0},{2,3},{3,2},{4,5},{5,4},{6,7},{7,6},{8,9},{9,8},{10,11... | collective-permute-start | bytes 319496 | tf_op jit(solution)/shard_map/ppermute | solution.py:44
  13.9 10.4 %collective-permute-start.4 = (f32[616,128]{1,0:T(8,128)S(1)}, f32[616,128]{1,0:T(8,128)S(1)}, u32[]{:S(2)}, u32[]{:S(2)}) collective-permute-start(f32[616,128]{1,0:T(8,128)S(1)} %shard_map.76.message), channel_id=1, source_target_pairs={{0,28},{4,0},{8,4},{12,8},{16,12},{20,16},{24,20},{28,24},{1,29},{... | collective-permute-start | bytes 946184 | tf_op jit(solution)/shard_map/ppermute | solution.py:39
  16.4 15.1 %collective-permute-start.5 = (f32[2,34,8,128]{3,2,1,0:T(8,128)S(1)}, f32[2,34,8,128]{3,2,1,0:T(8,128)S(1)}, u32[]{:S(2)}, u32[]{:S(2)}) collective-permute-start(f32[2,34,8,128]{3,2,1,0:T(8,128)S(1)} %shard_map.77.before.mid0), channel_id=1, source_target_pairs={{0,28},{4,0},{8,4},{12,8},{16,12},{20,16},{24,20},{28,24},{1,29},{... | collective-permute-start | bytes 835592 | tf_op jit(solution)/shard_map/ppermute | solution.py:39
  25.1 9.4 %collective-permute-start.6 = (f32[2,34,8,128]{3,2,1,0:T(8,128)S(1)}, f32[2,34,8,128]{3,2,1,0:T(8,128)S(1)}, u32[]{:S(2)}, u32[]{:S(2)}) collective-permute-start(f32[2,34,8,128]{3,2,1,0:T(8,128)S(1)} %get-tuple-element.25.mid2), channel_id=1, source_target_pairs={{0,4},{4,8},{8,12},{12,16},{16,20},{20,24},{24,28},{28,0},{1,5},{5... | collective-permute-start | bytes 835592 | tf_op jit(solution)/shard_map/ppermute | solution.py:39
